TPU v7x, 32 devices: a whole 2x2x4 slice. The times are simulated.
32 devices in a mesh: dp: 8 (over z, core), tensor: 4 (over y, x).
Axes of the slice: x: 2, y: 2, z: 4, core: 2. Of those that a mesh axis runs over, the one named last changes fastest.
Arguments:
- tokens: bfloat16 [4096, 2048], P(('dp', 'tensor')), may hold values from -6 to 6
- cotangent: bfloat16 [4096, 2048], P(('dp', 'tensor')), may hold values from -6 to 6
- lengths: int32 [8, 6], P('dp'), may hold values from 0 to 512, as said below
- entry_weight: float32 [2048, 3, 2048], P('dp', None, 'tensor'), may hold values from -0.125 to 0.125
- entry_first: float32 [2048, 3, 2048], P('dp', None, 'tensor'), may hold values from -160 to 160
- entry_second: float32 [2048, 3, 2048], P('dp', None, 'tensor'), may hold values from 4096 to 13107.2
- exit_weight: float32 [2048, 2048], P('dp', 'tensor'), may hold values from -1 to 1
- exit_first: float32 [2048, 2048], P('dp', 'tensor'), may hold values from -20 to 20
- exit_second: float32 [2048, 2048], P('dp', 'tensor'), may hold values from 61.44 to 204.8
- gate_weight: float32 [2048, 2, 5632], P('dp', None, 'tensor'), may hold values from -0.125 to 0.125
- gate_first: float32 [2048, 2, 5632], P('dp', None, 'tensor'), may hold values from -24 to 24
- gate_second: float32 [2048, 2, 5632], P('dp', None, 'tensor'), may hold values from 81.92 to 286.72
- down_weight: float32 [2048, 5632], P('dp', 'tensor'), may hold values from -0.078125 to 0.078125
- down_first: float32 [2048, 5632], P('dp', 'tensor'), may hold values from -24 to 24
- down_second: float32 [2048, 5632], P('dp', 'tensor'), may hold values from 81.92 to 286.72
- bias_rows: float32 [5, 2048], replicated, may hold values from -3 to 3
- bias_first: float32 [5, 2048], replicated, may hold values from -160 to 160
- bias_second: float32 [5, 2048], replicated, may hold values from 4096 to 13107.2
- norm_gains: float32 [2, 2048], replicated, may hold values from 0.5 to 1.5
- gains_first: float32 [2, 2048], replicated, may hold values from -112 to 112
- gains_second: float32 [2, 2048], replicated, may hold values from 2252.8 to 7372.8
Outputs:
- output_rows: bfloat16 [4096, 2048], P(('dp', 'tensor'))
- input_gradient: float32 [4096, 2048], P(('dp', 'tensor'))
- entry_gradient: float32 [2048, 3, 2048], P('dp', None, 'tensor')
- entry_updated: float32 [2048, 3, 2048], P('dp', None, 'tensor')
- entry_first_new: float32 [2048, 3, 2048], P('dp', None, 'tensor')
- entry_second_new: float32 [2048, 3, 2048], P('dp', None, 'tensor')
- exit_gradient: float32 [2048, 2048], P('dp', 'tensor')
- exit_updated: float32 [2048, 2048], P('dp', 'tensor')
- exit_first_new: float32 [2048, 2048], P('dp', 'tensor')
- exit_second_new: float32 [2048, 2048], P('dp', 'tensor')
- gate_gradient: float32 [2048, 2, 5632], P('dp', None, 'tensor')
- gate_updated: float32 [2048, 2, 5632], P('dp', None, 'tensor')
- gate_first_new: float32 [2048, 2, 5632], P('dp', None, 'tensor')
- gate_second_new: float32 [2048, 2, 5632], P('dp', None, 'tensor')
- down_gradient: float32 [2048, 5632], P('dp', 'tensor')
- down_updated: float32 [2048, 5632], P('dp', 'tensor')
- down_first_new: float32 [2048, 5632], P('dp', 'tensor')
- down_second_new: float32 [2048, 5632], P('dp', 'tensor')
- bias_gradient: float32 [5, 2048], replicated
- bias_updated: float32 [5, 2048], replicated
- bias_first_new: float32 [5, 2048], replicated
- bias_second_new: float32 [5, 2048], replicated
- gains_gradient: float32 [2, 2048], replicated
- gains_updated: float32 [2, 2048], replicated
- gains_first_new: float32 [2, 2048], replicated
- gains_second_new: float32 [2, 2048], replicated
Inputs may be any that keep to these rules, and one draw needn't show every extreme that they name: In each row the nonzero lengths come first and sum to at most 512; some row holds a length equal to 512; every row sums to 256 or more.
All inputs are finite; a program needn't handle non-finite values.
Results may differ from a plain program's by a relative error of at most 0.025.
Values may be sent and summed in bfloat16 or wider, within the bound.
No kernel may reach another device: no remote copies, remote signals or barrier semaphores. Data moves between devices by JAX's collectives and lax.ppermute only.
A program may use at most 192 MiB of HBM per device.

v0:
```python
import jax
import jax.numpy as jnp
from jax import lax
from jax.sharding import PartitionSpec as P

HD = 64
ROT = 16
STEP = 3


norm_eps = 1e-05
rope_base = 10000.0
masked_score = -1e30
beta_one = 0.9
beta_two = 0.95
adam_eps = 1e-08
matrix_rate = 0.08
vector_rate = 0.4
weight_decay = 0.1


def norm_forward(rows, gain, shift):
    centre = jnp.mean(rows, axis=-1, keepdims=True)
    centred = rows - centre
    spread = jnp.mean(centred * centred, axis=-1, keepdims=True)
    factor = lax.rsqrt(spread + norm_eps)
    unit = centred * factor
    return (unit * gain + shift, unit, factor)


def norm_backward(incoming, unit, factor, gain):
    scaled = incoming * gain
    mean_plain = jnp.mean(scaled, axis=-1, keepdims=True)
    mean_along = jnp.mean(scaled * unit, axis=-1, keepdims=True)
    return factor * (scaled - mean_plain - unit * mean_along)


def segments(lengths_row, count):
    ends = jnp.cumsum(lengths_row)
    index = jnp.arange(count, dtype=jnp.int32)
    after = index[:, None] >= ends[None, :]
    segment = jnp.sum(after.astype(jnp.int32), axis=1)
    begin = jnp.max(jnp.where(after, ends[None, :], jnp.zeros_like(ends)[None, :]), axis=1)
    return (segment, index - begin)


def rotary_tables(positions):
    half = ROT // 2
    freqs = rope_base ** (-2.0 * jnp.arange(half, dtype=jnp.float32) / ROT)
    angles = positions[:, None] * freqs[None, :]
    return (jnp.cos(angles), jnp.sin(angles))


def rotate(heads, cosine, sine, direction):
    half = ROT // 2
    first = heads[..., :half]
    second = heads[..., half:ROT]
    cosine = cosine[:, None, :]
    sine = direction * sine[:, None, :]
    return jnp.concatenate(
        [first * cosine - second * sine, second * cosine + first * sine, heads[..., ROT:]], axis=-1
    )


def adamw(weight, first, second, gradient, rate, decay):
    first_new = beta_one * first + (1.0 - beta_one) * gradient
    second_new = beta_two * second + (1.0 - beta_two) * gradient * gradient
    first_hat = first_new / (1.0 - beta_one**STEP)
    second_hat = second_new / (1.0 - beta_two**STEP)
    updated = weight - rate * (first_hat / (jnp.sqrt(second_hat) + adam_eps) + decay * weight)
    return (updated, first_new, second_new)


def on_device(
    tokens,
    cotangent,
    lengths,
    entry_weight,
    entry_first,
    entry_second,
    exit_weight,
    exit_first,
    exit_second,
    gate_weight,
    gate_first,
    gate_second,
    down_weight,
    down_first,
    down_second,
    bias_rows,
    bias_first,
    bias_second,
    norm_gains,
    gains_first,
    gains_second,
):
    parts = lax.axis_size("tensor")
    part_index = lax.axis_index("tensor")
    local_rows = tokens.shape[0]
    group = local_rows * parts
    width = tokens.shape[1]
    head_cols = entry_weight.shape[2]
    local_heads = head_cols // HD
    score_scale = HD ** (-0.5)
    rows_in = tokens.astype(jnp.float32)
    entry_full, exit_full = (
        lax.all_gather(entry_weight.astype(jnp.bfloat16), "dp", axis=0, tiled=True),
        lax.all_gather(exit_weight.astype(jnp.bfloat16), "dp", axis=0, tiled=True),
    )
    gate_full, down_full = (
        lax.all_gather(gate_weight.astype(jnp.bfloat16), "dp", axis=0, tiled=True),
        lax.all_gather(down_weight.astype(jnp.bfloat16), "dp", axis=0, tiled=True),
    )
    segment, positions = segments(lengths[0], group)
    cosine, sine = rotary_tables(positions.astype(jnp.float32))
    column_start = part_index * head_cols
    rotmask = (jnp.arange(head_cols, dtype=jnp.int32) % HD < ROT).astype(jnp.float32)
    query_bias = lax.dynamic_slice_in_dim(bias_rows[0], column_start, head_cols, 0)
    key_bias = lax.dynamic_slice_in_dim(bias_rows[1], column_start, head_cols, 0) * rotmask
    value_bias = lax.dynamic_slice_in_dim(bias_rows[2], column_start, head_cols, 0)
    normed, unit_one, factor_one = norm_forward(rows_in, norm_gains[0], bias_rows[3])
    normed_all = lax.all_gather(normed.astype(jnp.bfloat16), "tensor", axis=0, tiled=True)
    mixed = jnp.einsum("nd,dkc->nkc", normed_all, entry_full, preferred_element_type=jnp.float32)
    offsets = jnp.stack([query_bias, key_bias, value_bias])
    mixed = mixed + offsets[None]
    queries = rotate(mixed[:, 0].reshape(group, local_heads, HD), cosine, sine, 1.0).astype(
        jnp.bfloat16
    )
    keys = rotate(mixed[:, 1].reshape(group, local_heads, HD), cosine, sine, 1.0).astype(
        jnp.bfloat16
    )
    values = mixed[:, 2].reshape(group, local_heads, HD).astype(jnp.bfloat16)
    block = min(512, group)
    starts = jnp.arange(group // block, dtype=jnp.int32) * block
    key_index = jnp.arange(group, dtype=jnp.int32)

    def block_scores(start):
        query_block = lax.dynamic_slice_in_dim(queries, start, block, 0)
        segment_block = lax.dynamic_slice_in_dim(segment, start, block, 0)
        index = start + jnp.arange(block, dtype=jnp.int32)
        visible = (segment_block[:, None] == segment[None, :]) & (
            index[:, None] >= key_index[None, :]
        )
        scores = score_scale * jnp.einsum(
            "qhd,khd->hqk", query_block, keys, preferred_element_type=jnp.float32
        )
        return (jnp.where(visible[None], scores, masked_score), query_block)

    def attend(start):
        scores, query_block = block_scores(start)
        summit = jnp.max(scores, axis=-1, keepdims=True)
        weights = jnp.exp(scores - summit)
        totals = jnp.sum(weights, axis=-1, keepdims=True)
        probs = (weights / totals).astype(jnp.bfloat16)
        attended = jnp.einsum("hqk,khd->qhd", probs, values, preferred_element_type=jnp.float32)
        return (attended, (summit + jnp.log(totals))[..., 0])

    attended, log_totals = lax.map(attend, starts)
    context = attended.reshape(group, head_cols).astype(jnp.bfloat16)
    picked = context
    branch = lax.psum_scatter(
        jnp.einsum("nc,dc->nd", picked, exit_full, preferred_element_type=jnp.float32),
        "tensor",
        scatter_dimension=0,
        tiled=True,
    )
    middle = rows_in + branch
    second, unit_two, factor_two = norm_forward(middle, norm_gains[1], bias_rows[4])
    second_all = lax.all_gather(second.astype(jnp.bfloat16), "tensor", axis=0, tiled=True)
    gate_up = jnp.einsum("nd,dkf->nkf", second_all, gate_full, preferred_element_type=jnp.float32)
    gate = gate_up[:, 0]
    upper = gate_up[:, 1]
    sigmoid = jax.nn.sigmoid(gate)
    activated = gate * sigmoid
    hidden = (activated * upper).astype(jnp.bfloat16)
    picked = hidden
    branch_two = lax.psum_scatter(
        jnp.einsum("nf,df->nd", picked, down_full, preferred_element_type=jnp.float32).astype(
            jnp.bfloat16
        ),
        "tensor",
        scatter_dimension=0,
        tiled=True,
    ).astype(jnp.float32)
    output_rows = (middle + branch_two).astype(jnp.bfloat16)
    cotangent_all = lax.all_gather(cotangent, "tensor", axis=0, tiled=True)
    down_grad_full = jnp.einsum(
        "nd,nf->df", cotangent_all, hidden, preferred_element_type=jnp.float32
    )
    hidden_grad = jnp.einsum(
        "nd,df->nf", cotangent_all, down_full, preferred_element_type=jnp.float32
    )
    gate_grad = hidden_grad * upper * sigmoid * (1.0 + gate * (1.0 - sigmoid))
    upper_grad = hidden_grad * activated
    gate_up_grad = jnp.stack([gate_grad, upper_grad], axis=1).astype(jnp.bfloat16)
    gate_grad_full = jnp.einsum(
        "nd,nkf->dkf", second_all, gate_up_grad, preferred_element_type=jnp.float32
    )
    gate_gradient, down_gradient = (
        lax.psum_scatter(
            gate_grad_full.astype(jnp.bfloat16), "dp", scatter_dimension=0, tiled=True
        ).astype(jnp.float32),
        lax.psum_scatter(
            down_grad_full.astype(jnp.bfloat16), "dp", scatter_dimension=0, tiled=True
        ).astype(jnp.float32),
    )
    picked = gate_up_grad
    second_grad = lax.psum_scatter(
        jnp.einsum("nkf,dkf->nd", picked, gate_full, preferred_element_type=jnp.float32).astype(
            jnp.bfloat16
        ),
        "tensor",
        scatter_dimension=0,
        tiled=True,
    ).astype(jnp.float32)
    middle_grad = cotangent.astype(jnp.float32) + norm_backward(
        second_grad, unit_two, factor_two, norm_gains[1]
    )
    gain_two_grad = jnp.sum(second_grad * unit_two, axis=0)
    shift_two_grad = jnp.sum(second_grad, axis=0)
    middle_all = lax.all_gather(middle_grad.astype(jnp.bfloat16), "tensor", axis=0, tiled=True)
    exit_grad_full = jnp.einsum(
        "nd,nc->dc", middle_all, context, preferred_element_type=jnp.float32
    )
    context_grad = jnp.einsum(
        "nd,dc->nc", middle_all, exit_full, preferred_element_type=jnp.float32
    )
    context_grad = context_grad.astype(jnp.bfloat16).reshape(group, local_heads, HD)

    def attend_back(carry, inputs):
        key_grad, value_grad = carry
        start, log_block = inputs
        scores, query_block = block_scores(start)
        probs = jnp.exp(scores - log_block[:, :, None])
        context_block = lax.dynamic_slice_in_dim(context_grad, start, block, 0)
        prob_grad = jnp.einsum(
            "qhd,khd->hqk", context_block, values, preferred_element_type=jnp.float32
        )
        inner = jnp.sum(probs * prob_grad, axis=-1, keepdims=True)
        score_grad = (probs * (prob_grad - inner)).astype(jnp.bfloat16)
        query_grad = score_scale * jnp.einsum(
            "hqk,khd->qhd", score_grad, keys, preferred_element_type=jnp.float32
        )
        key_grad = key_grad + score_scale * jnp.einsum(
            "hqk,qhd->khd", score_grad, query_block, preferred_element_type=jnp.float32
        )
        value_grad = value_grad + jnp.einsum(
            "hqk,qhd->khd",
            probs.astype(jnp.bfloat16),
            context_block,
            preferred_element_type=jnp.float32,
        )
        return ((key_grad, value_grad), query_grad)

    zero_heads = jnp.zeros((group, local_heads, HD), jnp.float32)
    (key_grad, value_grad), query_grad = lax.scan(
        attend_back, (zero_heads, zero_heads), (starts, log_totals)
    )
    query_grad = rotate(query_grad.reshape(group, local_heads, HD), cosine, sine, -1.0)
    key_grad = rotate(key_grad, cosine, sine, -1.0)
    mixed_grad = jnp.stack(
        [
            query_grad.reshape(group, head_cols),
            key_grad.reshape(group, head_cols),
            value_grad.reshape(group, head_cols),
        ],
        axis=1,
    ).astype(jnp.bfloat16)
    entry_grad_full = jnp.einsum(
        "nd,nkc->dkc", normed_all, mixed_grad, preferred_element_type=jnp.float32
    )
    column_sums = jnp.sum(mixed_grad.astype(jnp.float32), axis=0)
    blank = jnp.zeros((width,), jnp.float32)
    query_bias_grad = lax.dynamic_update_slice_in_dim(blank, column_sums[0], column_start, 0)
    key_bias_grad = lax.dynamic_update_slice_in_dim(
        blank, column_sums[1] * rotmask, column_start, 0
    )
    value_bias_grad = lax.dynamic_update_slice_in_dim(blank, column_sums[2], column_start, 0)
    entry_gradient, exit_gradient = (
        lax.psum_scatter(
            entry_grad_full.astype(jnp.bfloat16), "dp", scatter_dimension=0, tiled=True
        ).astype(jnp.float32),
        lax.psum_scatter(
            exit_grad_full.astype(jnp.bfloat16), "dp", scatter_dimension=0, tiled=True
        ).astype(jnp.float32),
    )
    picked = mixed_grad
    normed_grad = lax.psum_scatter(
        jnp.einsum("nkc,dkc->nd", picked, entry_full, preferred_element_type=jnp.float32).astype(
            jnp.bfloat16
        ),
        "tensor",
        scatter_dimension=0,
        tiled=True,
    ).astype(jnp.float32)
    input_gradient = middle_grad + norm_backward(normed_grad, unit_one, factor_one, norm_gains[0])
    gain_one_grad = jnp.sum(normed_grad * unit_one, axis=0)
    shift_one_grad = jnp.sum(normed_grad, axis=0)
    gains_local = jnp.stack([gain_one_grad, gain_two_grad])
    bias_local = jnp.stack(
        [query_bias_grad, key_bias_grad, value_bias_grad, shift_one_grad, shift_two_grad]
    )
    gains_gradient, bias_gradient = lax.psum((gains_local, bias_local), ("dp", "tensor"))
    entry_updated, entry_first_new, entry_second_new = adamw(
        entry_weight, entry_first, entry_second, entry_gradient, matrix_rate, weight_decay
    )
    exit_updated, exit_first_new, exit_second_new = adamw(
        exit_weight, exit_first, exit_second, exit_gradient, matrix_rate, weight_decay
    )
    gate_updated, gate_first_new, gate_second_new = adamw(
        gate_weight, gate_first, gate_second, gate_gradient, matrix_rate, weight_decay
    )
    down_updated, down_first_new, down_second_new = adamw(
        down_weight, down_first, down_second, down_gradient, matrix_rate, weight_decay
    )
    bias_updated, bias_first_new, bias_second_new = adamw(
        bias_rows, bias_first, bias_second, bias_gradient, vector_rate, 0.0
    )
    gains_updated, gains_first_new, gains_second_new = adamw(
        norm_gains, gains_first, gains_second, gains_gradient, vector_rate, 0.0
    )
    return (
        output_rows,
        input_gradient,
        entry_gradient,
        entry_updated,
        entry_first_new,
        entry_second_new,
        exit_gradient,
        exit_updated,
        exit_first_new,
        exit_second_new,
        gate_gradient,
        gate_updated,
        gate_first_new,
        gate_second_new,
        down_gradient,
        down_updated,
        down_first_new,
        down_second_new,
        bias_gradient,
        bias_updated,
        bias_first_new,
        bias_second_new,
        gains_gradient,
        gains_updated,
        gains_first_new,
        gains_second_new,
    )


def solution(mesh):
    return jax.shard_map(
        on_device,
        mesh=mesh,
        in_specs=(
            P(("dp", "tensor"), None),
            P(("dp", "tensor"), None),
            P("dp", None),
            P("dp", None, "tensor"),
            P("dp", None, "tensor"),
            P("dp", None, "tensor"),
            P("dp", "tensor"),
            P("dp", "tensor"),
            P("dp", "tensor"),
            P("dp", None, "tensor"),
            P("dp", None, "tensor"),
            P("dp", None, "tensor"),
            P("dp", "tensor"),
            P("dp", "tensor"),
            P("dp", "tensor"),
            P(),
            P(),
            P(),
            P(),
            P(),
            P(),
        ),
        out_specs=(
            P(("dp", "tensor"), None),
            P(("dp", "tensor"), None),
            P("dp", None, "tensor"),
            P("dp", None, "tensor"),
            P("dp", None, "tensor"),
            P("dp", None, "tensor"),
            P("dp", "tensor"),
            P("dp", "tensor"),
            P("dp", "tensor"),
            P("dp", "tensor"),
            P("dp", None, "tensor"),
            P("dp", None, "tensor"),
            P("dp", None, "tensor"),
            P("dp", None, "tensor"),
            P("dp", "tensor"),
            P("dp", "tensor"),
            P("dp", "tensor"),
            P("dp", "tensor"),
            P(),
            P(),
            P(),
            P(),
            P(),
            P(),
            P(),
            P(),
        ),
        check_vma=False,
    )
```

profile of v0, /device:TPU:0, one launch (start us, length us, event | category | flops | bytes accessed | tf_op | source)
XLA Modules:
  0.0 946.5 jit_solution(2112155590872001332)
XLA Ops:
  18.2 34.7 %all-gather.9.cloned.1.call-done = bf16[512,2048]{1,0:T(8,128)(2,1)} async-done(((bf16[128,2048]{1,0:T(8,128)(2,1)}), bf16[512,2048]{1,0:T(8,128)(2,1)}) %all-gather.9.cloned.1.call-update) | async-done | bytes 2097168 | tf_op jit(solution)/shard_map/all_gather | solution.py:122
  52.9 67.4 %all-gather.11.cloned.1.call-done = bf16[2048,3,512]{0,2,1:T(8,128)(2,1)} async-done(((bf16[256,3,512]{0,2,1:T(8,128)(2,1)}), bf16[2048,3,512]{0,2,1:T(8,128)(2,1)}) %all-gather.11.cloned.1.call-update) | async-done | bytes 6291472 | tf_op jit(solution)/shard_map/all_gather | solution.py:107
  120.2 6.2 fusion.16
  133.6 16.2 %all-gather.13.cloned.1.call-done = bf16[2048,512]{1,0:T(8,128)(2,1)} async-done(((bf16[256,512]{1,0:T(8,128)(2,1)}), bf16[2048,512]{1,0:T(8,128)(2,1)}) %all-gather.13.cloned.1.call-update) | async-done | bytes 2097168 | tf_op jit(solution)/shard_map/all_gather | solution.py:108
  149.7 5.0 fusion.76
  157.9 49.2 %reduce-scatter.9.cloned.1.call-done = f32[128,2048]{1,0:T(8,128)} async-done(((f32[512,2048]{1,0:T(8,128)}), f32[128,2048]{1,0:T(8,128)}) %reduce-scatter.9.cloned.1.call-update) | async-done | bytes 1048592 | tf_op jit(solution)/shard_map/reduce_scatter | solution.py:161
  212.1 105.2 %all-gather.17.cloned.1.call-done = bf16[2048,2,1408]{2,0,1:T(8,128)(2,1)} async-done(((bf16[256,2,1408]{2,0,1:T(8,128)(2,1)}), bf16[2048,2,1408]{2,0,1:T(8,128)(2,1)}) %all-gather.17.cloned.1.call-update) | async-done | bytes 11534352 | tf_op jit(solution)/shard_map/all_gather | solution.py:111
  317.3 36.1 %all-gather.15.cloned.1.call-done = bf16[512,2048]{1,0:T(8,128)(2,1)} async-done(((bf16[128,2048]{1,0:T(8,128)(2,1)}), bf16[512,2048]{1,0:T(8,128)(2,1)}) %all-gather.15.cloned.1.call-update) | async-done | bytes 2097168 | tf_op jit(solution)/shard_map/all_gather | solution.py:169
  353.3 12.6 %fusion.11 = f32[512,2,1408]{2,0,1:T(8,128)} fusion(bf16[2048,2,1408]{2,0,1:T(8,128)(2,1)} %all-gather.17.cloned.1.call-done, bf16[512,2048]{1,0:T(8,128)(2,1)} %all-gather.15.cloned.1.call-done), kind=kOutput, calls=%fused_computation.38 | convolution fusion | flops 5905580032 | bytes 19398656 | tf_op jit(solution)/shard_map/nd,dkf->nkf/dot_general | solution.py:170
  365.9 24.8 %all-gather.21.cloned.1.call-done = bf16[512,2048]{1,0:T(8,128)(2,1)} async-done(((bf16[128,2048]{1,0:T(8,128)(2,1)}), bf16[512,2048]{1,0:T(8,128)(2,1)}) %all-gather.21.cloned.1.call-update) | async-done | bytes 2097168 | tf_op jit(solution)/shard_map/all_gather | solution.py:186
  390.7 62.8 %all-gather.19.cloned.1.call-done = bf16[2048,1408]{1,0:T(8,128)(2,1)} async-done(((bf16[256,1408]{1,0:T(8,128)(2,1)}), bf16[2048,1408]{1,0:T(8,128)(2,1)}) %all-gather.19.cloned.1.call-update) | async-done | bytes 5767184 | tf_op jit(solution)/shard_map/all_gather | solution.py:112
  453.4 10.3 %fusion.28 = (bf16[512,1,1408]{2,0,1:T(8,128)(2,1)S(1)}, bf16[512,1,1408]{2,0,1:T(8,128)(2,1)S(1)}, bf16[512,1408]{1,0:T(8,128)(2,1)}) fusion(f32[512,2,1408]{2,0,1:T(8,128)} %fusion.11, bf16[512,2048]{1,0:T(8,128)(2,1)} %all-gather.21.cloned.1.call-done, bf16[2048,1408]{1,0:T(8,128)(2,1)} %all-gather.19.cloned.1.call-done), kind=kOutput, calls=%fused_computation.67 | convolution fusion | flops 2963603456 | bytes 17956864 | tf_op jit(solution)/shard_map/nd,df->nf/dot_general | solution.py:190
  465.3 10.0 %bitcast_convert_fusion.1 = bf16[512,2048]{1,0:T(8,128)(2,1)} fusion(bf16[2048,2,1408]{2,0,1:T(8,128)(2,1)} %all-gather.17.cloned.1.call-done, bf16[512,1,1408]{2,0,1:T(8,128)(2,1)S(1)} %get-tuple-element.172, bf16[512,1,1408]{2,0,1:T(8,128)(2,1)S(1)} %get-tuple-element.171), kind=kOutput, calls=%fused_computation.15 | convolution fusion | flops 5908070400 | bytes 16515072 | tf_op jit(solution)/shard_map/nkf,dkf->nd/dot_general | solution.py:209
  475.4 7.9 convolution_convert_fusion.4
  483.3 26.1 %reduce-scatter.13.cloned.1.call-done = bf16[128,2048]{1,0:T(8,128)(2,1)} async-done(((bf16[512,2048]{1,0:T(8,128)(2,1)}), bf16[128,2048]{1,0:T(8,128)(2,1)}) %reduce-scatter.13.cloned.1.call-update) | async-done | bytes 524304 | tf_op jit(solution)/shard_map/reduce_scatter | solution.py:208
  511.5 36.5 %reduce-scatter.11.cloned.1.call-done = bf16[128,2048]{1,0:T(8,128)(2,1)} async-done(((bf16[512,2048]{1,0:T(8,128)(2,1)}), bf16[128,2048]{1,0:T(8,128)(2,1)}) %reduce-scatter.11.cloned.1.call-update) | async-done | bytes 524304 | tf_op jit(solution)/shard_map/reduce_scatter | solution.py:177
  551.6 7.7 fusion.1
  560.1 26.7 %all-gather.23.cloned.1.call-done = bf16[512,2048]{1,0:T(8,128)(2,1)} async-done(((bf16[128,2048]{1,0:T(8,128)(2,1)}), bf16[512,2048]{1,0:T(8,128)(2,1)}) %all-gather.23.cloned.1.call-update) | async-done | bytes 2097168 | tf_op jit(solution)/shard_map/all_gather | solution.py:221
  590.4 5.4 multiply_reduce_fusion
  606.9 5.7 fusion.32
  613.9 7.9 bitcast_convert_fusion
  621.9 4.4 convolution_convert_fusion.3
  626.8 7.8 convolution_convert_fusion.2
  636.0 10.6 %convolution_convert_fusion = bf16[2048,2,1408]{2,0,1:T(8,128)(2,1)} fusion(bf16[512,2048]{1,0:T(8,128)(2,1)} %all-gather.15.cloned.1.call-done, bf16[512,1,1408]{2,0,1:T(8,128)(2,1)} %copy-done.54, bf16[512,1,1408]{2,0,1:T(8,128)(2,1)S(1)} %copy-done.53), kind=kOutput, calls=%fused_computation | convolution fusion | flops 5917114368 | bytes 16515072 | tf_op jit(solution)/shard_map/nd,nkf->dkf/dot_general | solution.py:196
  653.9 4.3 multiply_subtract_fusion.2
  664.4 26.9 %reduce-scatter.15.cloned.1.call-done = bf16[128,2048]{1,0:T(8,128)(2,1)} async-done(((bf16[512,2048]{1,0:T(8,128)(2,1)}), bf16[128,2048]{1,0:T(8,128)(2,1)}) %reduce-scatter.15.cloned.1.call-update) | async-done | bytes 524304 | tf_op jit(solution)/shard_map/reduce_scatter | solution.py:288
  695.0 40.5 %all-reduce = (f32[5,2048]{1,0:T(8,128)S(1)}, f32[2,2048]{1,0:T(2,128)S(1)}) all-reduce(f32[5,2048]{1,0:T(8,128)S(1)} %stack.50, f32[2,2048]{1,0:T(2,128)S(1)} %pad_maximum_fusion.12), channel_id=1, replica_groups=mesh['dp'=8,'tensor'=4] {'dp','tensor'}, use_global_device_ids=true, to_apply=%region_25.26 | all-reduce | flops 14336 | bytes 114688 | tf_op jit(solution)/shard_map/psum | solution.py:303
  742.6 58.3 %reduce-scatter.17.cloned.1.call-done = bf16[256,3,512]{2,0,1:T(8,128)(2,1)} async-done(((bf16[2048,3,512]{2,0,1:T(8,128)(2,1)}), bf16[256,3,512]{2,0,1:T(8,128)(2,1)}) %reduce-scatter.17.cloned.1.call-update) | async-done | bytes 786448 | tf_op jit(solution)/shard_map/reduce_scatter | solution.py:280
  800.9 5.8 multiply_subtract_fusion.1
  806.8 114.0 %reduce-scatter.21.cloned.1.call-done = bf16[256,2,1408]{2,0,1:T(8,128)(2,1)} async-done(((bf16[2048,2,1408]{2,0,1:T(8,128)(2,1)}), bf16[256,2,1408]{2,0,1:T(8,128)(2,1)}) %reduce-scatter.21.cloned.1.call-update) | async-done | bytes 1441808 | tf_op jit(solution)/shard_map/reduce_scatter | solution.py:200
  920.8 4.5 multiply_subtract_fusion
  925.3 3.8 copy.96
  (225 shorter events, 86.3 us)
Async XLA Ops:
  7.2 45.7 %all-gather.9.cloned.1.call-start = ((), (), s32[]{:S(2)}) async-start(), calls=%async_computation.8 | async-start | bytes 2621440 | tf_op jit(solution)/shard_map/all_gather | solution.py:122
  14.7 105.5 %all-gather.11.cloned.1.call-start = ((), (), s32[]{:S(2)}) async-start(), calls=%async_computation.9 | async-start | bytes 7077888 | tf_op jit(solution)/shard_map/all_gather | solution.py:107
  15.9 133.8 %all-gather.13.cloned.1.call-start = ((), (), s32[]{:S(2)}) async-start(), calls=%async_computation.10 | async-start | bytes 2359296 | tf_op jit(solution)/shard_map/all_gather | solution.py:108
  16.8 190.3 %reduce-scatter.9.cloned.1.call-start = ((), (), s32[]{:S(2)}) async-start(), calls=%async_computation.11 | async-start | bytes 5242880 | tf_op jit(solution)/shard_map/reduce_scatter | solution.py:161
  18.1 108.7 %copy-start.29 = (f32[512,8]{0,1:T(8,128)}, f32[512,8]{0,1:T(8,128)S(1)}, u32[]{:S(2)}) copy-start(f32[512,8]{0,1:T(8,128)S(1)} %get-tuple-element.198) | copy-start | bytes 49156
  154.7 52.4 %copy-start.1 = (bf16[128,2048]{1,0:T(8,128)(2,1)S(1)}, bf16[128,2048]{1,0:T(8,128)(2,1)}, u32[]{:S(2)}) copy-start(bf16[128,2048]{1,0:T(8,128)(2,1)} %param.21) | copy-start | bytes 1572868
  154.7 162.6 %all-gather.17.cloned.1.call-start = ((), (), s32[]{:S(2)}) async-start(), calls=%async_computation.13 | async-start | bytes 12976128 | tf_op jit(solution)/shard_map/all_gather | solution.py:111
  157.8 52.9 %copy-start.7 = (f32[256,1408]{1,0:T(8,128)S(1)}, f32[256,1408]{1,0:T(8,128)}, u32[]{:S(2)}) copy-start(f32[256,1408]{1,0:T(8,128)} %param.33) | copy-start | bytes 4325380
  157.8 195.5 %all-gather.15.cloned.1.call-start = ((), (), s32[]{:S(2)}) async-start(), calls=%async_computation.12 | async-start | bytes 2621440 | tf_op jit(solution)/shard_map/all_gather | solution.py:169
  209.8 180.8 %all-gather.21.cloned.1.call-start = ((), (), s32[]{:S(2)}) async-start(), calls=%async_computation.16 | async-start | bytes 2621440 | tf_op jit(solution)/shard_map/all_gather | solution.py:186
  210.6 242.9 %all-gather.19.cloned.1.call-start = ((), (), s32[]{:S(2)}) async-start(), calls=%async_computation.14 | async-start | bytes 6488064 | tf_op jit(solution)/shard_map/all_gather | solution.py:112
  211.6 297.8 %reduce-scatter.13.cloned.1.call-start = ((), (), s32[]{:S(2)}) async-start(), calls=%async_computation.17 | async-start | bytes 2621440 | tf_op jit(solution)/shard_map/reduce_scatter | solution.py:208
  475.3 72.7 %reduce-scatter.11.cloned.1.call-start = ((), (), s32[]{:S(2)}) async-start(), calls=%async_computation.15 | async-start | bytes 2621440 | tf_op jit(solution)/shard_map/reduce_scatter | solution.py:177
  483.3 103.5 %all-gather.23.cloned.1.call-start = ((), (), s32[]{:S(2)}) async-start(), calls=%async_computation.18 | async-start | bytes 2621440 | tf_op jit(solution)/shard_map/all_gather | solution.py:221
  551.3 102.6 %reduce-scatter.23.cloned.1.call-start = ((), (), s32[]{:S(2)}) async-start(), calls=%async_computation.23 | async-start | bytes 6488064 | tf_op jit(solution)/shard_map/reduce_scatter | solution.py:203
  559.3 132.0 %reduce-scatter.15.cloned.1.call-start = ((), (), s32[]{:S(2)}) async-start(), calls=%async_computation.19 | async-start | bytes 2621440 | tf_op jit(solution)/shard_map/reduce_scatter | solution.py:288
  621.9 115.0 %reduce-scatter.19.cloned.1.call-start = ((), (), s32[]{:S(2)}) async-start(), calls=%async_computation.21 | async-start | bytes 2359296 | tf_op jit(solution)/shard_map/reduce_scatter | solution.py:283
  626.3 174.6 %reduce-scatter.17.cloned.1.call-start = ((), (), s32[]{:S(2)}) async-start(), calls=%async_computation.20 | async-start | bytes 7077888 | tf_op jit(solution)/shard_map/reduce_scatter | solution.py:280
  634.6 286.2 %reduce-scatter.21.cloned.1.call-start = ((), (), s32[]{:S(2)}) async-start(), calls=%async_computation.22 | async-start | bytes 12976128 | tf_op jit(solution)/shard_map/reduce_scatter | solution.py:200
  661.3 32.1 %copy-start.43 = (f32[2048]{0:T(1024)S(1)}, f32[2048]{0:T(1024)}, u32[]{:S(2)}) copy-start(f32[2048]{0:T(1024)} %get-tuple-element.142) | copy-start | bytes 24580
  662.9 30.6 %copy-start.10 = (bf16[256,1408]{0,1:T(8,128)(2,1)S(1)}, bf16[256,1408]{0,1:T(8,128)(2,1)}, u32[]{:S(2)}) copy-start(bf16[256,1408]{0,1:T(8,128)(2,1)} %reduce-scatter.23.cloned.1.call-done) | copy-start | bytes 2162692
  662.9 32.0 %copy-start.42 = (f32[2048]{0:T(1024)S(1)}, f32[2048]{0:T(1024)}, u32[]{:S(2)}) copy-start(f32[2048]{0:T(1024)} %get-tuple-element.135) | copy-start | bytes 24580
  662.9 74.0 %copy-start.12 = (f32[256,512]{1,0:T(8,128)S(1)}, f32[256,512]{1,0:T(8,128)}, u32[]{:S(2)}) copy-start(f32[256,512]{1,0:T(8,128)} %param.27) | copy-start | bytes 1572868
  693.5 47.0 %copy-start.28 = (f32[5,2048]{1,0:T(8,128)S(1)}, f32[5,2048]{1,0:T(8,128)}, u32[]{:S(2)}) copy-start(f32[5,2048]{1,0:T(8,128)} %param.36) | copy-start | bytes 122884
  693.5 47.0 %copy-start.37 = (f32[5,2048]{1,0:T(8,128)S(1)}, f32[5,2048]{1,0:T(8,128)}, u32[]{:S(2)}) copy-start(f32[5,2048]{1,0:T(8,128)} %param.37) | copy-start | bytes 122884
  693.5 46.9 %copy-start.38 = (f32[5,2048]{1,0:T(8,128)S(1)}, f32[5,2048]{1,0:T(8,128)}, u32[]{:S(2)}) copy-start(f32[5,2048]{1,0:T(8,128)} %param.38) | copy-start | bytes 122884
  693.5 47.6 %copy-start.9 = (f32[128,2048]{1,0:T(8,128)S(1)}, f32[128,2048]{1,0:T(8,128)}, u32[]{:S(2)}) copy-start(f32[128,2048]{1,0:T(8,128)} %get-tuple-element.168) | copy-start | bytes 3145732
  694.9 44.9 %copy-start.41 = (f32[2,2048]{1,0:T(2,128)S(1)}, f32[2,2048]{1,0:T(2,128)}, u32[]{:S(2)}) copy-start(f32[2,2048]{1,0:T(2,128)} %param.39) | copy-start | bytes 49156
  694.9 44.9 %copy-start.44 = (f32[2,2048]{1,0:T(2,128)S(1)}, f32[2,2048]{1,0:T(2,128)}, u32[]{:S(2)}) copy-start(f32[2,2048]{1,0:T(2,128)} %param.40) | copy-start | bytes 49156
  694.9 44.9 %copy-start.45 = (f32[2,2048]{1,0:T(2,128)S(1)}, f32[2,2048]{1,0:T(2,128)}, u32[]{:S(2)}) copy-start(f32[2,2048]{1,0:T(2,128)} %param.41) | copy-start | bytes 49156
  694.9 46.2 %copy-start.18 = (bf16[128,2048]{1,0:T(8,128)(2,1)S(1)}, bf16[128,2048]{1,0:T(8,128)(2,1)}, u32[]{:S(2)}) copy-start(bf16[128,2048]{1,0:T(8,128)(2,1)} %reduce-scatter.15.cloned.1.call-done) | copy-start | bytes 1572868
  742.6 178.2 %copy-start.3 = (f32[256,2,1408]{2,1,0:T(2,128)S(1)}, f32[256,2,1408]{2,1,0:T(2,128)}, u32[]{:S(2)}) copy-start(f32[256,2,1408]{2,1,0:T(2,128)} %param.30) | copy-start | bytes 8650756
  (41 other events, 280.8 us)
Sparse Core Ops, SparseCore 0:
  14.8 38.0 all-gather.8
  55.0 65.1 all-gather.10
  122.4 27.2 all-gather.12
  154.8 52.1 reduce-scatter.8
  209.2 108.0 all-gather.16
  319.7 33.6 all-gather.14
  355.3 35.2 all-gather.20
  393.0 60.4 all-gather.18
  475.5 33.8 reduce-scatter.12
  512.8 35.1 reduce-scatter.10
  551.5 35.3 all-gather.22
  589.1 64.8 reduce-scatter.22
  657.8 33.5 reduce-scatter.14
  694.1 36.0 reduce-scatter.18
  732.3 68.5 reduce-scatter.16
  803.1 117.6 reduce-scatter.20
where the time goes:
time: 955 us; the launch traced here: 947 us
  waiting for transfers between devices  686 us (72%)
  matrix products  110 us (12%)
  other arithmetic  46.9 us (5%)
  local copies, waits for them, and re-layouts  45.9 us (5%)
  blocking collectives  40.5 us (4%)
  between operations  14.9 us (2%)
    reduce_scatter x1, waiting for transfers between devices, on_device(): lax.psum_scatter(gate_grad_full.astype(jnp.bfloat16), 'dp', scatter_dimen...  114 us
    all_gather x1, waiting for transfers between devices, on_device(): lax.all_gather(gate_weight.astype(jnp.bfloat16), 'dp', axis=0, tiled=True)  105 us
    all_gather x1, waiting for transfers between devices, on_device(): lax.all_gather(entry_weight.astype(jnp.bfloat16), 'dp', axis=0, tiled=True)  67.4 us
    all_gather x1, waiting for transfers between devices, on_device(): lax.all_gather(down_weight.astype(jnp.bfloat16), 'dp', axis=0, tiled=True)  62.8 us
    reduce_scatter x1, waiting for transfers between devices, on_device(): lax.psum_scatter(entry_grad_full.astype(jnp.bfloat16), 'dp', scatter_dime...  58.3 us
    reduce_scatter x1, waiting for transfers between devices, on_device(): lax.psum_scatter(jnp.einsum('nc,dc->nd', picked, exit_full, preferred_ele...  49.2 us
    psum x1, blocking collectives, on_device(): lax.psum((gains_local, bias_local), ('dp', 'tensor'))  40.5 us
    unnamed x127, local copies, waits for them, and re-layouts  38.8 us
  transfers between devices with their start and end apart: 16, of which 15 were waited for; matrix products, arithmetic and copies ran while one was open for 15% of the time, Pallas kernels for 0%

commit v1 on v0

v1 whole, which is shorter than its diff:
```python
import jax
import jax.numpy as jnp
from jax import lax
from jax.sharding import PartitionSpec as P

HD = 64
ROT = 16
STEP = 3


norm_eps = 1e-05
rope_base = 10000.0
masked_score = -1e30
beta_one = 0.9
beta_two = 0.95
adam_eps = 1e-08
matrix_rate = 0.08
vector_rate = 0.4
weight_decay = 0.1


def norm_forward(rows, gain, shift):
    centre = jnp.mean(rows, axis=-1, keepdims=True)
    centred = rows - centre
    spread = jnp.mean(centred * centred, axis=-1, keepdims=True)
    factor = lax.rsqrt(spread + norm_eps)
    unit = centred * factor
    return (unit * gain + shift, unit, factor)


def norm_backward(incoming, unit, factor, gain):
    scaled = incoming * gain
    mean_plain = jnp.mean(scaled, axis=-1, keepdims=True)
    mean_along = jnp.mean(scaled * unit, axis=-1, keepdims=True)
    return factor * (scaled - mean_plain - unit * mean_along)


def segments(lengths_row, count):
    ends = jnp.cumsum(lengths_row)
    index = jnp.arange(count, dtype=jnp.int32)
    after = index[:, None] >= ends[None, :]
    segment = jnp.sum(after.astype(jnp.int32), axis=1)
    begin = jnp.max(jnp.where(after, ends[None, :], jnp.zeros_like(ends)[None, :]), axis=1)
    return (segment, index - begin)


def rotary_tables(positions):
    half = ROT // 2
    freqs = rope_base ** (-2.0 * jnp.arange(half, dtype=jnp.float32) / ROT)
    angles = positions[:, None] * freqs[None, :]
    return (jnp.cos(angles), jnp.sin(angles))


def rotate(heads, cosine, sine, direction):
    half = ROT // 2
    first = heads[..., :half]
    second = heads[..., half:ROT]
    cosine = cosine[:, None, :]
    sine = direction * sine[:, None, :]
    return jnp.concatenate(
        [first * cosine - second * sine, second * cosine + first * sine, heads[..., ROT:]], axis=-1
    )


def adamw(weight, first, second, gradient, rate, decay):
    first_new = beta_one * first + (1.0 - beta_one) * gradient
    second_new = beta_two * second + (1.0 - beta_two) * gradient * gradient
    first_hat = first_new / (1.0 - beta_one**STEP)
    second_hat = second_new / (1.0 - beta_two**STEP)
    updated = weight - rate * (first_hat / (jnp.sqrt(second_hat) + adam_eps) + decay * weight)
    return (updated, first_new, second_new)


MLP_CHUNKS = 4


def pairs_up(lines, low, high, step):
    return [(z * 2 + c, (z + step) * 2 + c) for z in range(low, high) for c in range(2)]


def other_core(array):
    count = lax.axis_size("dp")
    return lax.ppermute(array, "dp", [(d, d ^ 1) for d in range(count)])


def line_gather(own, place, lines):
    ups, downs = [own], [own]
    for s in range(1, lines):
        ups.append(lax.ppermute(ups[-1], "dp", pairs_up(lines, s - 1, lines - 1, 1)))
        downs.append(lax.ppermute(downs[-1], "dp", pairs_up(lines, 1, lines - s + 1, -1)))
    return [own] + [jnp.where(place >= s, ups[s], downs[lines - s]) for s in range(1, lines)]


def full_gather(own, place, lines):
    half = jnp.concatenate(line_gather(own, place, lines), axis=0)
    return jnp.concatenate([half, other_core(half)], axis=0)


def line_scatter(blocks, lines):
    up = None
    down = None
    for j in range(lines - 1, 0, -1):
        up_send = blocks[lines - j] if up is None else blocks[lines - j] + up
        up = lax.ppermute(up_send, "dp", pairs_up(lines, 0, lines - j, 1))
        down_send = blocks[j] if down is None else blocks[j] + down
        down = lax.ppermute(down_send, "dp", pairs_up(lines, j, lines, -1))
    total = blocks[0].astype(jnp.float32)
    if up is not None:
        total = total + up.astype(jnp.float32) + down.astype(jnp.float32)
    return total


def swap_rows(array, offset):
    count = lax.axis_size("tensor")
    return lax.ppermute(array, "tensor", [(t, t ^ offset) for t in range(count)])


def gather_rows(own, parts):
    return jnp.concatenate([own] + [swap_rows(own, r) for r in range(1, parts)], axis=0)


def scatter_rows(partial, parts):
    rows = partial.shape[0] // parts
    total = partial[:rows].astype(jnp.float32)
    for r in range(1, parts):
        total = total + swap_rows(partial[r * rows : (r + 1) * rows], r).astype(jnp.float32)
    return total


def sum_all(array):
    for axis in ("dp", "tensor"):
        count = lax.axis_size(axis)
        bit = 1
        while bit < count:
            array = array + lax.ppermute(array, axis, [(i, i ^ bit) for i in range(count)])
            bit *= 2
    return array


def pick_blocks(array, indices, size):
    return jnp.concatenate(
        [lax.dynamic_slice_in_dim(array, i * size, size, array.ndim - 1) for i in indices], axis=-1
    )


def cuts(columns, count):
    tiles = -(-columns // 128)
    bounds = [min(columns, 128 * ((tiles * i + count - 1) // count)) for i in range(count + 1)]
    return [(a, b) for a, b in zip(bounds[:-1], bounds[1:]) if b > a]


def dot(a, b, contract):
    return lax.dot_general(a, b, (contract, ((), ())), preferred_element_type=jnp.float32)


def on_device(
    tokens,
    cotangent,
    lengths,
    entry_weight,
    entry_first,
    entry_second,
    exit_weight,
    exit_first,
    exit_second,
    gate_weight,
    gate_first,
    gate_second,
    down_weight,
    down_first,
    down_second,
    bias_rows,
    bias_first,
    bias_second,
    norm_gains,
    gains_first,
    gains_second,
):
    parts = lax.axis_size("tensor")
    part_index = lax.axis_index("tensor")
    dp_index = lax.axis_index("dp")
    dp_count = lax.axis_size("dp")
    lines = dp_count // 2
    place = dp_index // 2
    core = dp_index % 2
    local_rows = tokens.shape[0]
    group = local_rows * parts
    width = tokens.shape[1]
    halfwidth = width // 2
    size = width // dp_count
    head_cols = entry_weight.shape[2]
    hidden_cols = down_weight.shape[1]
    local_heads = head_cols // HD
    score_scale = HD ** (-0.5)
    bf16 = jnp.bfloat16

    to_mine = [
        ((place - s + lines) % lines) * 2 + (core ^ cc) for cc in range(2) for s in range(lines)
    ]
    to_whole = [
        (core ^ c) * lines + (place - z + lines) % lines for z in range(lines) for c in range(2)
    ]
    rows_bf = pick_blocks(tokens, to_mine, size)
    cot_bf = pick_blocks(cotangent, to_mine, size)
    gains_mine = pick_blocks(norm_gains, to_mine, size)
    shifts_mine = pick_blocks(bias_rows[3:5], to_mine, size)
    rows_in = rows_bf.astype(jnp.float32)

    entry_full = full_gather(
        entry_weight.astype(bf16).reshape(size, 3 * head_cols), place, lines
    )
    exit_full = full_gather(exit_weight.astype(bf16), place, lines)
    chunks = cuts(hidden_cols, MLP_CHUNKS)
    mlp_full = [
        full_gather(
            jnp.concatenate(
                [
                    gate_weight[:, 0, a:b].astype(bf16),
                    gate_weight[:, 1, a:b].astype(bf16),
                    down_weight[:, a:b].astype(bf16),
                ],
                axis=1,
            ),
            place,
            lines,
        )
        for a, b in chunks
    ]

    segment, positions = segments(lengths[0], group)
    row_blocks = jnp.arange(parts, dtype=jnp.int32) ^ part_index
    row_index = (
        row_blocks[:, None] * local_rows + jnp.arange(local_rows, dtype=jnp.int32)[None, :]
    ).reshape(group)
    segment = jnp.concatenate(
        [
            lax.dynamic_slice_in_dim(segment, (part_index ^ r) * local_rows, local_rows, 0)
            for r in range(parts)
        ]
    )
    positions = jnp.concatenate(
        [
            lax.dynamic_slice_in_dim(positions, (part_index ^ r) * local_rows, local_rows, 0)
            for r in range(parts)
        ]
    )
    cosine, sine = rotary_tables(positions.astype(jnp.float32))
    column_start = part_index * head_cols
    rotmask = (jnp.arange(head_cols, dtype=jnp.int32) % HD < ROT).astype(jnp.float32)
    query_bias = lax.dynamic_slice_in_dim(bias_rows[0], column_start, head_cols, 0)
    key_bias = lax.dynamic_slice_in_dim(bias_rows[1], column_start, head_cols, 0) * rotmask
    value_bias = lax.dynamic_slice_in_dim(bias_rows[2], column_start, head_cols, 0)
    offsets = jnp.concatenate([query_bias, key_bias, value_bias])

    normed, unit_one, factor_one = norm_forward(rows_in, gains_mine[0], shifts_mine[0])
    normed_all = gather_rows(normed.astype(bf16), parts)
    normed_other = other_core(normed_all[:, halfwidth:])
    mixed = dot(normed_all, entry_full, ((1,), (0,))) + offsets[None]
    queries = rotate(
        mixed[:, :head_cols].reshape(group, local_heads, HD), cosine, sine, 1.0
    ).astype(bf16)
    keys = rotate(
        mixed[:, head_cols : 2 * head_cols].reshape(group, local_heads, HD), cosine, sine, 1.0
    ).astype(bf16)
    values = mixed[:, 2 * head_cols :].reshape(group, local_heads, HD).astype(bf16)
    visible = (segment[:, None] == segment[None, :]) & (row_index[:, None] >= row_index[None, :])

    def all_scores():
        scores = score_scale * jnp.einsum(
            "qhd,khd->hqk", queries, keys, preferred_element_type=jnp.float32
        )
        return jnp.where(visible[None], scores, masked_score)

    scores = all_scores()
    summit = jnp.max(scores, axis=-1, keepdims=True)
    weights = jnp.exp(scores - summit)
    totals = jnp.sum(weights, axis=-1, keepdims=True)
    probs = (weights / totals).astype(bf16)
    attended = jnp.einsum("hqk,khd->qhd", probs, values, preferred_element_type=jnp.float32)
    log_totals = summit + jnp.log(totals)
    context = attended.reshape(group, head_cols).astype(bf16)
    context_other = other_core(context)
    branch = scatter_rows(dot(context, exit_full, ((1,), (1,))).astype(bf16), parts)
    middle = rows_in + branch
    second, unit_two, factor_two = norm_forward(middle, gains_mine[1], shifts_mine[1])
    second_all = gather_rows(second.astype(bf16), parts)
    second_other = other_core(second_all[:, halfwidth:])
    cot_all = gather_rows(cot_bf, parts)
    cot_other = other_core(cot_all[:, halfwidth:])

    branch_two = jnp.zeros((group, width), jnp.float32)
    second_grad = jnp.zeros((group, width), jnp.float32)
    gate_pieces, down_pieces = [], []
    for (a, b), full in zip(chunks, mlp_full):
        n = b - a
        gate_up = dot(second_all, full[:, : 2 * n], ((1,), (0,)))
        gate = gate_up[:, :n]
        upper = gate_up[:, n:]
        sigmoid = jax.nn.sigmoid(gate)
        activated = gate * sigmoid
        hidden = (activated * upper).astype(bf16)
        hidden_grad = dot(cot_all, full[:, 2 * n :], ((1,), (0,)))
        gate_grad = hidden_grad * upper * sigmoid * (1.0 + gate * (1.0 - sigmoid))
        upper_grad = hidden_grad * activated
        gate_up_grad = jnp.concatenate([gate_grad, upper_grad], axis=1).astype(bf16)
        branch_two = branch_two + dot(hidden, full[:, 2 * n :], ((1,), (1,)))
        second_grad = second_grad + dot(gate_up_grad, full[:, : 2 * n], ((1,), (1,)))
        hidden_other = other_core(hidden)
        gate_up_other = other_core(gate_up_grad)
        gate_term = dot(second_all[:, :halfwidth], gate_up_grad, ((0,), (0,))) + dot(
            second_other, gate_up_other, ((0,), (0,))
        )
        down_term = dot(cot_all[:, :halfwidth], hidden, ((0,), (0,))) + dot(
            cot_other, hidden_other, ((0,), (0,))
        )
        terms = jnp.concatenate([gate_term, down_term], axis=1).astype(bf16)
        total = line_scatter([terms[s * size : (s + 1) * size] for s in range(lines)], lines)
        gate_pieces.append(total[:, : 2 * n].reshape(size, 2, n))
        down_pieces.append(total[:, 2 * n :])
    gate_gradient = jnp.concatenate(gate_pieces, axis=2)
    down_gradient = jnp.concatenate(down_pieces, axis=1)

    second_grad = scatter_rows(second_grad.astype(bf16), parts)
    middle_grad = cot_bf.astype(jnp.float32) + norm_backward(
        second_grad, unit_two, factor_two, gains_mine[1]
    )
    gain_two_grad = jnp.sum(second_grad * unit_two, axis=0)
    shift_two_grad = jnp.sum(second_grad, axis=0)
    middle_all = gather_rows(middle_grad.astype(bf16), parts)
    middle_other = other_core(middle_all[:, halfwidth:])
    branch_two = scatter_rows(branch_two.astype(bf16), parts)
    output_rows = pick_blocks((middle + branch_two).astype(bf16), to_whole, size)

    exit_terms = (
        dot(middle_all[:, :halfwidth], context, ((0,), (0,)))
        + dot(middle_other, context_other, ((0,), (0,)))
    ).astype(bf16)
    exit_gradient = line_scatter([exit_terms[s * size : (s + 1) * size] for s in range(lines)], lines)
    context_grad = dot(middle_all, exit_full, ((1,), (0,)))
    context_grad = context_grad.astype(bf16).reshape(group, local_heads, HD)

    scores = all_scores()
    probs = jnp.exp(scores - log_totals)
    prob_grad = jnp.einsum("qhd,khd->hqk", context_grad, values, preferred_element_type=jnp.float32)
    inner = jnp.sum(probs * prob_grad, axis=-1, keepdims=True)
    score_grad = (probs * (prob_grad - inner)).astype(bf16)
    query_grad = score_scale * jnp.einsum(
        "hqk,khd->qhd", score_grad, keys, preferred_element_type=jnp.float32
    )
    key_grad = score_scale * jnp.einsum(
        "hqk,qhd->khd", score_grad, queries, preferred_element_type=jnp.float32
    )
    value_grad = jnp.einsum(
        "hqk,qhd->khd", probs.astype(bf16), context_grad, preferred_element_type=jnp.float32
    )
    query_grad = rotate(query_grad, cosine, sine, -1.0)
    key_grad = rotate(key_grad, cosine, sine, -1.0)
    mixed_grad = jnp.concatenate(
        [
            query_grad.reshape(group, head_cols),
            key_grad.reshape(group, head_cols),
            value_grad.reshape(group, head_cols),
        ],
        axis=1,
    ).astype(bf16)
    mixed_other = other_core(mixed_grad)
    entry_terms = (
        dot(normed_all[:, :halfwidth], mixed_grad, ((0,), (0,)))
        + dot(normed_other, mixed_other, ((0,), (0,)))
    ).astype(bf16)
    entry_gradient = line_scatter(
        [entry_terms[s * size : (s + 1) * size] for s in range(lines)], lines
    ).reshape(size, 3, head_cols)
    normed_grad = scatter_rows(dot(mixed_grad, entry_full, ((1,), (1,))).astype(bf16), parts)
    input_gradient = middle_grad + norm_backward(normed_grad, unit_one, factor_one, gains_mine[0])
    input_gradient = pick_blocks(input_gradient, to_whole, size)
    gain_one_grad = jnp.sum(normed_grad * unit_one, axis=0)
    shift_one_grad = jnp.sum(normed_grad, axis=0)

    column_sums = jnp.sum(mixed_grad.astype(jnp.float32), axis=0).reshape(3, head_cols)
    column_sums = column_sums * jnp.stack([jnp.ones_like(rotmask), rotmask, jnp.ones_like(rotmask)])
    placed = lax.dynamic_update_slice_in_dim(
        jnp.zeros((3, width), jnp.float32), column_sums, column_start, 1
    )
    norms_local = pick_blocks(
        jnp.stack([shift_one_grad, shift_two_grad, gain_one_grad, gain_two_grad]), to_whole, size
    )
    vectors = sum_all(jnp.concatenate([placed, norms_local], axis=0))
    bias_gradient = vectors[:5]
    gains_gradient = vectors[5:]
    entry_updated, entry_first_new, entry_second_new = adamw(
        entry_weight, entry_first, entry_second, entry_gradient, matrix_rate, weight_decay
    )
    exit_updated, exit_first_new, exit_second_new = adamw(
        exit_weight, exit_first, exit_second, exit_gradient, matrix_rate, weight_decay
    )
    gate_updated, gate_first_new, gate_second_new = adamw(
        gate_weight, gate_first, gate_second, gate_gradient, matrix_rate, weight_decay
    )
    down_updated, down_first_new, down_second_new = adamw(
        down_weight, down_first, down_second, down_gradient, matrix_rate, weight_decay
    )
    bias_updated, bias_first_new, bias_second_new = adamw(
        bias_rows, bias_first, bias_second, bias_gradient, vector_rate, 0.0
    )
    gains_updated, gains_first_new, gains_second_new = adamw(
        norm_gains, gains_first, gains_second, gains_gradient, vector_rate, 0.0
    )
    return (
        output_rows,
        input_gradient,
        entry_gradient,
        entry_updated,
        entry_first_new,
        entry_second_new,
        exit_gradient,
        exit_updated,
        exit_first_new,
        exit_second_new,
        gate_gradient,
        gate_updated,
        gate_first_new,
        gate_second_new,
        down_gradient,
        down_updated,
        down_first_new,
        down_second_new,
        bias_gradient,
        bias_updated,
        bias_first_new,
        bias_second_new,
        gains_gradient,
        gains_updated,
        gains_first_new,
        gains_second_new,
    )


def solution(mesh):
    return jax.shard_map(
        on_device,
        mesh=mesh,
        in_specs=(
            P(("dp", "tensor"), None),
            P(("dp", "tensor"), None),
            P("dp", None),
            P("dp", None, "tensor"),
            P("dp", None, "tensor"),
            P("dp", None, "tensor"),
            P("dp", "tensor"),
            P("dp", "tensor"),
            P("dp", "tensor"),
            P("dp", None, "tensor"),
            P("dp", None, "tensor"),
            P("dp", None, "tensor"),
            P("dp", "tensor"),
            P("dp", "tensor"),
            P("dp", "tensor"),
            P(),
            P(),
            P(),
            P(),
            P(),
            P(),
        ),
        out_specs=(
            P(("dp", "tensor"), None),
            P(("dp", "tensor"), None),
            P("dp", None, "tensor"),
            P("dp", None, "tensor"),
            P("dp", None, "tensor"),
            P("dp", None, "tensor"),
            P("dp", "tensor"),
            P("dp", "tensor"),
            P("dp", "tensor"),
            P("dp", "tensor"),
            P("dp", None, "tensor"),
            P("dp", None, "tensor"),
            P("dp", None, "tensor"),
            P("dp", None, "tensor"),
            P("dp", "tensor"),
            P("dp", "tensor"),
            P("dp", "tensor"),
            P("dp", "tensor"),
            P(),
            P(),
            P(),
            P(),
            P(),
            P(),
            P(),
            P(),
        ),
        check_vma=False,
    )
```

time: 955 us -> 893 us (0.935)
  waiting for transfers between devices: 686 us -> 280 us
  starting transfers between devices: 1.71 us -> 271 us
  other arithmetic: 46.9 us -> 129 us
  local copies, waits for them, and re-layouts: 45.9 us -> 104 us
  blocking collectives: 40.5 us -> 0 us
  matrix products: 110 us -> 90.1 us
  between operations: 14.9 us -> 4.77 us
    all_gather x8 -> x0, waiting for transfers between devices: 374 us -> none  [the longest x1 105 us: on_device(): lax.all_gather(gate_weight.astype(jnp.bfloat16), 'dp', axis=0, tiled=True)]
    reduce_scatter x8 -> x0, waiting for transfers between devices: 312 us -> none  [the longest x1 114 us: on_device(): lax.psum_scatter(gate_grad_full.astype(jnp.bfloat16), 'dp', scatter_dimen...]
    ppermute x0 -> x121, waiting for transfers between devices: none -> 280 us  [the longest x18 119 us: line_gather(): lax.ppermute(downs[-1], 'dp', pairs_up(lines, 1, lines - s + 1, -1))]
    ppermute x0 -> x121, starting transfers between devices: none -> 271 us  [the longest x18 147 us: line_scatter(): up = lax.ppermute(up_send, 'dp', pairs_up(lines, 0, lines - j, 1))]
    psum x1 -> x0, blocking collectives: 40.5 us -> none  [on_device(): lax.psum((gains_local, bias_local), ('dp', 'tensor'))]
    concatenate x0 -> x25, other arithmetic: none -> 38.3 us  [the longest x6 23 us: full_gather(): half = jnp.concatenate(line_gather(own, place, lines), axis=0)]
    add x2 -> x33, other arithmetic: 1.44 us -> 26.7 us  [the longest x12 10.9 us: line_scatter(): up_send = blocks[lines - j] if up is None else blocks[lines - j] + up]
    dot_general x18 -> x46, matrix products: 110 us -> 90.1 us  [the longest x40 77.5 us: dot(): lax.dot_general(a, b, (contract, ((), ())), preferred_element_type=jnp.fl...]
  transfers between devices with their start and end apart: 16 -> 121, of which waited for: 15 -> 34; matrix products, arithmetic and copies ran while one was open for 15% -> 33% of each run, Pallas kernels for 0% -> 0%
where the time goes in v1:
time: 893 us; the launch traced here: 879 us
  waiting for transfers between devices  280 us (31%)
  starting transfers between devices  271 us (30%)
  other arithmetic  129 us (14%)
  local copies, waits for them, and re-layouts  104 us (12%)
  matrix products  90.1 us (10%)
    ppermute x18, starting transfers between devices, line_scatter(): up = lax.ppermute(up_send, 'dp', pairs_up(lines, 0, lines - j, 1))  147 us
    ppermute x18, waiting for transfers between devices, line_gather(): lax.ppermute(downs[-1], 'dp', pairs_up(lines, 1, lines - s + 1, -1))  119 us
    ppermute x24, waiting for transfers between devices, swap_rows(): lax.ppermute(array, 'tensor', [(t, t ^ offset) for t in range(count)])  95.7 us
    dot_general x40, matrix products, dot(): lax.dot_general(a, b, (contract, ((), ())), preferred_element_type=jnp.fl...  77.5 us
    unnamed x393, local copies, waits for them, and re-layouts  55.1 us
    ppermute x5, waiting for transfers between devices, sum_all(): lax.ppermute(array, axis, [(i, i ^ bit) for i in range(count)])  31.4 us
    ppermute x18, starting transfers between devices, line_gather(): lax.ppermute(ups[-1], 'dp', pairs_up(lines, s - 1, lines - 1, 1))  29.4 us
    ppermute x24, starting transfers between devices, swap_rows(): lax.ppermute(array, 'tensor', [(t, t ^ offset) for t in range(count)])  29.1 us
  transfers between devices with their start and end apart: 121, of which 34 were waited for; matrix products, arithmetic and copies ran while one was open for 33% of the time, Pallas kernels for 0%

profile of v1, /device:TPU:0, one launch (start us, length us, event | category | flops | bytes accessed | tf_op | source)
XLA Modules:
  0.0 878.9 jit_solution(5065573407867098631)
XLA Ops:
  93.3 11.7 %collective-permute-done.13 = bf16[256,512]{1,0:T(8,128)(2,1)S(1)} collective-permute-done((bf16[256,512]{1,0:T(8,128)(2,1)S(1)}, bf16[256,512]{1,0:T(8,128)(2,1)S(1)}, u32[]{:S(2)}, u32[]{:S(2)}) %collective-permute-start.13) | collective-permute-done | bytes 262176 | tf_op jit(solution)/shard_map/ppermute | solution.py:90
  120.5 9.8 %collective-permute-done.32 = bf16[256,1152]{1,0:T(8,128)(2,1)S(1)} collective-permute-done((bf16[256,1152]{1,0:T(8,128)(2,1)}, bf16[256,1152]{1,0:T(8,128)(2,1)S(1)}, u32[]{:S(2)}, u32[]{:S(2)}) %collective-permute-start.32) | collective-permute-done | bytes 589856 | tf_op jit(solution)/shard_map/ppermute | solution.py:90
  131.0 7.7 collective-permute-done.47
  152.1 11.9 %collective-permute-done.33 = bf16[256,1152]{1,0:T(8,128)(2,1)S(1)} collective-permute-done((bf16[256,1152]{1,0:T(8,128)(2,1)S(1)}, bf16[256,1152]{1,0:T(8,128)(2,1)S(1)}, u32[]{:S(2)}, u32[]{:S(2)}) %collective-permute-start.33) | collective-permute-done | bytes 589856 | tf_op jit(solution)/shard_map/ppermute | solution.py:90
  166.3 14.6 %collective-permute-done.4 = bf16[256,1536]{0,1:T(8,128)(2,1)S(1)} collective-permute-done((bf16[256,1536]{0,1:T(8,128)(2,1)S(1)}, bf16[256,1536]{0,1:T(8,128)(2,1)S(1)}, u32[]{:S(2)}, u32[]{:S(2)}) %collective-permute-start.4) | collective-permute-done | bytes 786464 | tf_op jit(solution)/shard_map/ppermute | solution.py:90
  184.7 8.9 %collective-permute-done.38 = bf16[256,1152]{1,0:T(8,128)(2,1)S(1)} collective-permute-done((bf16[256,1152]{1,0:T(8,128)(2,1)S(1)}, bf16[256,1152]{1,0:T(8,128)(2,1)S(1)}, u32[]{:S(2)}, u32[]{:S(2)}) %collective-permute-start.38) | collective-permute-done | bytes 589856 | tf_op jit(solution)/shard_map/ppermute | solution.py:90
  195.8 10.4 %collective-permute-done.26 = bf16[256,1152]{1,0:T(8,128)(2,1)S(1)} collective-permute-done((bf16[256,1152]{1,0:T(8,128)(2,1)S(1)}, bf16[256,1152]{1,0:T(8,128)(2,1)S(1)}, u32[]{:S(2)}, u32[]{:S(2)}) %collective-permute-start.26) | collective-permute-done | bytes 589856 | tf_op jit(solution)/shard_map/ppermute | solution.py:90
  208.6 9.8 %collective-permute-done.5 = bf16[256,1536]{0,1:T(8,128)(2,1)S(1)} collective-permute-done((bf16[256,1536]{0,1:T(8,128)(2,1)S(1)}, bf16[256,1536]{0,1:T(8,128)(2,1)S(1)}, u32[]{:S(2)}, u32[]{:S(2)}) %collective-permute-start.5) | collective-permute-done | bytes 786464 | tf_op jit(solution)/shard_map/ppermute | solution.py:90
  225.4 22.5 %collective-permute-done.39 = bf16[256,1152]{1,0:T(8,128)(2,1)S(1)} collective-permute-done((bf16[256,1152]{1,0:T(8,128)(2,1)S(1)}, bf16[256,1152]{1,0:T(8,128)(2,1)S(1)}, u32[]{:S(2)}, u32[]{:S(2)}) %collective-permute-start.39) | collective-permute-done | bytes 589856 | tf_op jit(solution)/shard_map/ppermute | solution.py:90
  252.6 7.0 pad_maximum_fusion.3
  259.6 7.0 pad_maximum_fusion.2
  270.1 7.4 pad_maximum_fusion.4
  328.2 11.5 %collective-permute-done.18 = bf16[128,2048]{1,0:T(8,128)(2,1)S(1)} collective-permute-done((bf16[128,2048]{1,0:T(8,128)(2,1)S(1)}, bf16[128,2048]{1,0:T(8,128)(2,1)S(1)}, u32[]{:S(2)}, u32[]{:S(2)}) %collective-permute-start.18) | collective-permute-done | bytes 524320 | tf_op jit(solution)/shard_map/ppermute | solution.py:115
  346.8 8.9 %collective-permute-done.20 = bf16[128,2048]{1,0:T(8,128)(2,1)S(1)} collective-permute-done((bf16[128,2048]{1,0:T(8,128)(2,1)S(1)}, bf16[128,2048]{1,0:T(8,128)(2,1)S(1)}, u32[]{:S(2)}, u32[]{:S(2)}) %collective-permute-start.20) | collective-permute-done | bytes 524320 | tf_op jit(solution)/shard_map/ppermute | solution.py:115
  355.7 9.5 %collective-permute-done.21 = bf16[128,2048]{1,0:T(8,128)(2,1)S(1)} collective-permute-done((bf16[128,2048]{1,0:T(8,128)(2,1)S(1)}, bf16[128,2048]{1,0:T(8,128)(2,1)S(1)}, u32[]{:S(2)}, u32[]{:S(2)}) %collective-permute-start.21) | collective-permute-done | bytes 524320 | tf_op jit(solution)/shard_map/ppermute | solution.py:115
  425.7 11.7 %collective-permute-done.57 = bf16[128,2048]{1,0:T(8,128)(2,1)S(1)} collective-permute-done((bf16[128,2048]{1,0:T(8,128)(2,1)S(1)}, bf16[128,2048]{1,0:T(8,128)(2,1)S(1)}, u32[]{:S(2)}, u32[]{:S(2)}) %collective-permute-start.57) | collective-permute-done | bytes 524320 | tf_op jit(solution)/shard_map/ppermute | solution.py:115
  439.9 9.8 %collective-permute-done.59 = bf16[128,2048]{1,0:T(8,128)(2,1)S(1)} collective-permute-done((bf16[128,2048]{1,0:T(8,128)(2,1)S(1)}, bf16[128,2048]{1,0:T(8,128)(2,1)S(1)}, u32[]{:S(2)}, u32[]{:S(2)}) %collective-permute-start.59) | collective-permute-done | bytes 524320 | tf_op jit(solution)/shard_map/ppermute | solution.py:115
  451.9 19.3 %collective-permute-done.52 = bf16[128,2048]{1,0:T(8,128)(2,1)S(1)} collective-permute-done((bf16[128,2048]{1,0:T(8,128)(2,1)S(1)}, bf16[128,2048]{1,0:T(8,128)(2,1)S(1)}, u32[]{:S(2)}, u32[]{:S(2)}) %collective-permute-start.52) | collective-permute-done | bytes 524320 | tf_op jit(solution)/shard_map/ppermute | solution.py:115
  494.4 7.1 collective-permute-done.61
  554.5 19.6 %collective-permute-done.117 = f32[7,2048]{1,0:T(8,128)S(1)} collective-permute-done((f32[7,2048]{1,0:T(8,128)S(1)}, f32[7,2048]{1,0:T(8,128)S(1)}, u32[]{:S(2)}, u32[]{:S(2)}) %collective-permute-start.117) | collective-permute-done | bytes 57376 | tf_op jit(solution)/shard_map/ppermute | solution.py:135
  574.1 15.5 %collective-permute-start.118 = (f32[7,2048]{1,0:T(8,128)S(1)}, f32[7,2048]{1,0:T(8,128)S(1)}, u32[]{:S(2)}, u32[]{:S(2)}) collective-permute-start(f32[7,2048]{1,0:T(8,128)S(1)} %add.820), channel_id=1, source_target_pairs={{0,16},{4,20},{8,24},{12,28},{16,0},{20,4},{24,8},{28,12},{1,17},{... | collective-permute-start | bytes 172040 | tf_op jit(solution)/shard_map/ppermute | solution.py:135
  589.9 6.3 collective-permute-done.118
  622.5 6.3 collective-permute-done.87
  630.5 10.9 %collective-permute-done.95 = bf16[256,1152]{0,1:T(8,128)(2,1)S(1)} collective-permute-done((bf16[256,1152]{0,1:T(8,128)(2,1)S(1)}, bf16[256,1152]{0,1:T(8,128)(2,1)S(1)}, u32[]{:S(2)}, u32[]{:S(2)}) %collective-permute-start.95) | collective-permute-done | bytes 589856 | tf_op jit(solution)/shard_map/ppermute | solution.py:104
  646.9 6.4 collective-permute-done.103
  675.0 13.3 %collective-permute-start.78 = (bf16[256,512]{1,0:T(8,128)(2,1)S(1)}, bf16[256,512]{1,0:T(8,128)(2,1)S(1)}, u32[]{:S(2)}, u32[]{:S(2)}) collective-permute-start(bf16[256,512]{1,0:T(8,128)(2,1)S(1)} %get-tuple-element.238), channel_id=1, source_target_pairs={{0,8},{4,12},{8,16},{12,20},{16,24},{20,28},{1,9},{5,13},{9,17},{1... | collective-permute-start | bytes 786440 | tf_op jit(solution)/shard_map/ppermute | solution.py:104
  692.2 24.5 %collective-permute-start.68 = (bf16[256,1536]{1,0:T(8,128)(2,1)}, bf16[256,1536]{1,0:T(8,128)(2,1)}, u32[]{:S(2)}, u32[]{:S(2)}) collective-permute-start(bf16[256,1536]{1,0:T(8,128)(2,1)} %get-tuple-element.194), channel_id=1, source_target_pairs={{0,8},{4,12},{1,9},{5,13},{2,10},{6,14},{3,11},{7,15}} | collective-permute-start | bytes 2359304 | tf_op jit(solution)/shard_map/ppermute | solution.py:104
  722.5 8.9 %collective-permute-start.88 = (bf16[256,1152]{0,1:T(8,128)(2,1)}, bf16[256,1152]{0,1:T(8,128)(2,1)}, u32[]{:S(2)}, u32[]{:S(2)}) collective-permute-start(bf16[256,1152]{0,1:T(8,128)(2,1)} %get-tuple-element.131), channel_id=1, source_target_pairs={{0,8},{4,12},{8,16},{12,20},{16,24},{20,28},{1,9},{5,13},{9,17},{1... | collective-permute-start | bytes 1769480 | tf_op jit(solution)/shard_map/ppermute | solution.py:104
  739.5 23.9 %collective-permute-start.96 = (bf16[256,1152]{0,1:T(8,128)(2,1)}, bf16[256,1152]{0,1:T(8,128)(2,1)}, u32[]{:S(2)}, u32[]{:S(2)}) collective-permute-start(bf16[256,1152]{0,1:T(8,128)(2,1)} %get-tuple-element.133), channel_id=1, source_target_pairs={{0,8},{4,12},{8,16},{12,20},{16,24},{20,28},{1,9},{5,13},{9,17},{1... | collective-permute-start | bytes 1769480 | tf_op jit(solution)/shard_map/ppermute | solution.py:104
  767.5 23.8 %collective-permute-start.104 = (bf16[256,1152]{0,1:T(8,128)(2,1)}, bf16[256,1152]{0,1:T(8,128)(2,1)}, u32[]{:S(2)}, u32[]{:S(2)}) collective-permute-start(bf16[256,1152]{0,1:T(8,128)(2,1)} %get-tuple-element.135), channel_id=1, source_target_pairs={{0,8},{4,12},{8,16},{12,20},{16,24},{20,28},{1,9},{5,13},{9,17},{1... | collective-permute-start | bytes 1769480 | tf_op jit(solution)/shard_map/ppermute | solution.py:104
  815.0 15.3 %multiply_subtract_fusion = (f32[256,2,1408]{2,1,0:T(2,128)}, f32[256,2,1408]{2,1,0:T(2,128)}, f32[256,2,1408]{2,1,0:T(2,128)}, f32[256,2,1408]{2,1,0:T(2,128)}) fusion(f32[256,2,1408]{2,1,0:T(2,128)} %param.30, f32[256,2,1408]{2,1,0:T(2,128)} %param.31, f32[256,2,1408]{2,1,0:T(2,128)} %param.32, f32[256,2,256]{2,1,0:T(2,128)} %copy.141, ...), kind=kLoop, calls=%fused_computation.35 | loop fusion | flops 12976128 | bytes 23068672 | tf_op jit(solution)/shard_map/sub | solution.py:70
  833.2 6.6 collective-permute-start.70
  (837 shorter events, 486.3 us)
Async XLA Ops:
  2.5 46.0 %collective-permute-start.11 = (bf16[256,512]{1,0:T(8,128)(2,1)}, bf16[256,512]{1,0:T(8,128)(2,1)}, u32[]{:S(2)}, u32[]{:S(2)}) collective-permute-start(bf16[256,512]{1,0:T(8,128)(2,1)} %get-tuple-element.183), channel_id=1, source_target_pairs={{8,0},{12,4},{16,8},{20,12},{24,16},{28,20},{9,1},{13,5},{17,9},{2... | collective-permute-start | bytes 786440 | tf_op jit(solution)/shard_map/ppermute | solution.py:90
  3.8 46.7 %collective-permute-start.10 = (bf16[256,512]{1,0:T(8,128)(2,1)}, bf16[256,512]{1,0:T(8,128)(2,1)}, u32[]{:S(2)}, u32[]{:S(2)}) collective-permute-start(bf16[256,512]{1,0:T(8,128)(2,1)} %get-tuple-element.183), channel_id=1, source_target_pairs={{0,8},{4,12},{8,16},{12,20},{16,24},{20,28},{1,9},{5,13},{9,17},{1... | collective-permute-start | bytes 786440 | tf_op jit(solution)/shard_map/ppermute | solution.py:89
  17.0 41.7 %collective-permute-start.54 = (bf16[128,2048]{1,0:T(8,128)(2,1)S(1)}, bf16[128,2048]{1,0:T(8,128)(2,1)}, u32[]{:S(2)}, u32[]{:S(2)}) collective-permute-start(bf16[128,2048]{1,0:T(8,128)(2,1)S(1)} %constant_dynamic-update-slice_fusion.62), channel_id=1, source_target_pairs={{0,1},{1,0},{2,3},{3,2},{4,5},{5,4},{6,7},{7,6},{8,9},{9,8},{10,11... | collective-permute-start | bytes 1572872 | tf_op jit(solution)/shard_map/ppermute | solution.py:115
  19.0 42.5 %collective-permute-start.55 = (bf16[128,2048]{1,0:T(8,128)(2,1)S(1)}, bf16[128,2048]{1,0:T(8,128)(2,1)}, u32[]{:S(2)}, u32[]{:S(2)}) collective-permute-start(bf16[128,2048]{1,0:T(8,128)(2,1)S(1)} %constant_dynamic-update-slice_fusion.62), channel_id=1, source_target_pairs={{0,2},{1,3},{2,0},{3,1},{4,6},{5,7},{6,4},{7,5},{8,10},{9,11},{10,... | collective-permute-start | bytes 1572872 | tf_op jit(solution)/shard_map/ppermute | solution.py:115
  143.1 39.3 %collective-permute-start.34 = (bf16[256,1152]{1,0:T(8,128)(2,1)S(1)}, bf16[256,1152]{1,0:T(8,128)(2,1)S(1)}, u32[]{:S(2)}, u32[]{:S(2)}) collective-permute-start(bf16[256,1152]{1,0:T(8,128)(2,1)S(1)} %collective-permute-done.30), channel_id=1, source_target_pairs={{8,16},{12,20},{16,24},{20,28},{9,17},{13,21},{17,25},{21,29},{10,... | collective-permute-start | bytes 1769480 | tf_op jit(solution)/shard_map/ppermute | solution.py:89
  145.9 47.7 %collective-permute-start.38 = (bf16[256,1152]{1,0:T(8,128)(2,1)S(1)}, bf16[256,1152]{1,0:T(8,128)(2,1)S(1)}, u32[]{:S(2)}, u32[]{:S(2)}) collective-permute-start(bf16[256,1152]{1,0:T(8,128)(2,1)S(1)} %copy-done.90), channel_id=1, source_target_pairs={{8,0},{12,4},{16,8},{20,12},{24,16},{28,20},{9,1},{13,5},{17,9},{2... | collective-permute-start | bytes 1769480 | tf_op jit(solution)/shard_map/ppermute | solution.py:90
  151.4 43.6 %collective-permute-start.27 = (bf16[256,1152]{1,0:T(8,128)(2,1)S(1)}, bf16[256,1152]{1,0:T(8,128)(2,1)S(1)}, u32[]{:S(2)}, u32[]{:S(2)}) collective-permute-start(bf16[256,1152]{1,0:T(8,128)(2,1)S(1)} %collective-permute-done.23), channel_id=1, source_target_pairs={{8,16},{12,20},{16,24},{20,28},{9,17},{13,21},{17,25},{21,29},{10,... | collective-permute-start | bytes 1769480 | tf_op jit(solution)/shard_map/ppermute | solution.py:89
  164.1 42.1 %collective-permute-start.26 = (bf16[256,1152]{1,0:T(8,128)(2,1)S(1)}, bf16[256,1152]{1,0:T(8,128)(2,1)S(1)}, u32[]{:S(2)}, u32[]{:S(2)}) collective-permute-start(bf16[256,1152]{1,0:T(8,128)(2,1)S(1)} %collective-permute-done.25), channel_id=1, source_target_pairs={{8,0},{12,4},{9,1},{13,5},{10,2},{14,6},{11,3},{15,7}} | collective-permute-start | bytes 1769480 | tf_op jit(solution)/shard_map/ppermute | solution.py:90
  207.9 41.3 %collective-permute-start.7 = (bf16[256,1536]{0,1:T(8,128)(2,1)S(1)}, bf16[256,1536]{0,1:T(8,128)(2,1)S(1)}, u32[]{:S(2)}, u32[]{:S(2)}) collective-permute-start(bf16[256,1536]{0,1:T(8,128)(2,1)S(1)} %collective-permute-done.3), channel_id=1, source_target_pairs={{8,16},{12,20},{16,24},{20,28},{9,17},{13,21},{17,25},{21,29},{10,... | collective-permute-start | bytes 2359304 | tf_op jit(solution)/shard_map/ppermute | solution.py:89
  223.0 54.5 %collective-permute-start.16 = (bf16[1024,512]{1,0:T(8,128)(2,1)S(1)}, bf16[1024,512]{1,0:T(8,128)(2,1)S(1)}, u32[]{:S(2)}, u32[]{:S(2)}) collective-permute-start(bf16[1024,512]{1,0:T(8,128)(2,1)S(1)} %pad_maximum_fusion.12), channel_id=1, source_target_pairs={{0,4},{4,0},{8,12},{12,8},{16,20},{20,16},{24,28},{28,24},{1,5},{5... | collective-permute-start | bytes 3145736 | tf_op jit(solution)/shard_map/ppermute | solution.py:83
  266.6 48.8 %collective-permute-start.36 = (bf16[1024,1152]{1,0:T(8,128)(2,1)}, bf16[1024,1152]{1,0:T(8,128)(2,1)}, u32[]{:S(2)}, u32[]{:S(2)}) collective-permute-start(bf16[1024,1152]{1,0:T(8,128)(2,1)} %pad_maximum_fusion.3), channel_id=1, source_target_pairs={{0,4},{4,0},{8,12},{12,8},{16,20},{20,16},{24,28},{28,24},{1,5},{5... | collective-permute-start | bytes 7077896 | tf_op jit(solution)/shard_map/ppermute | solution.py:83
  269.1 51.2 %collective-permute-start.29 = (bf16[1024,1152]{1,0:T(8,128)(2,1)}, bf16[1024,1152]{1,0:T(8,128)(2,1)}, u32[]{:S(2)}, u32[]{:S(2)}) collective-permute-start(bf16[1024,1152]{1,0:T(8,128)(2,1)} %pad_maximum_fusion.2), channel_id=1, source_target_pairs={{0,4},{4,0},{8,12},{12,8},{16,20},{20,16},{24,28},{28,24},{1,5},{5... | collective-permute-start | bytes 7077896 | tf_op jit(solution)/shard_map/ppermute | solution.py:83
  277.5 65.3 %collective-permute-start.43 = (bf16[1024,1152]{1,0:T(8,128)(2,1)}, bf16[1024,1152]{1,0:T(8,128)(2,1)}, u32[]{:S(2)}, u32[]{:S(2)}) collective-permute-start(bf16[1024,1152]{1,0:T(8,128)(2,1)} %pad_maximum_fusion.4), channel_id=1, source_target_pairs={{0,4},{4,0},{8,12},{12,8},{16,20},{20,16},{24,28},{28,24},{1,5},{5... | collective-permute-start | bytes 7077896 | tf_op jit(solution)/shard_map/ppermute | solution.py:83
  320.3 90.6 %collective-permute-start.84 = (bf16[512,1024]{1,0:T(8,128)(2,1)}, bf16[512,1024]{1,0:T(8,128)(2,1)S(1)}, u32[]{:S(2)}, u32[]{:S(2)}) collective-permute-start(bf16[512,1024]{1,0:T(8,128)(2,1)} %slice.547), channel_id=1, source_target_pairs={{0,4},{4,0},{8,12},{12,8},{16,20},{20,16},{24,28},{28,24},{1,5},{5... | collective-permute-start | bytes 3145736 | tf_op jit(solution)/shard_map/ppermute | solution.py:83
  328.2 332.9 %collective-permute-start.66 = (bf16[512,1024]{1,0:T(8,128)(2,1)}, bf16[512,1024]{1,0:T(8,128)(2,1)}, u32[]{:S(2)}, u32[]{:S(2)}) collective-permute-start(bf16[512,1024]{1,0:T(8,128)(2,1)} %slice.533), channel_id=1, source_target_pairs={{0,4},{4,0},{8,12},{12,8},{16,20},{20,16},{24,28},{28,24},{1,5},{5... | collective-permute-start | bytes 3145736 | tf_op jit(solution)/shard_map/ppermute | solution.py:83
  373.3 41.9 %collective-permute-start.85 = (bf16[512,384]{1,0:T(8,128)(2,1)}, bf16[512,384]{1,0:T(8,128)(2,1)}, u32[]{:S(2)}, u32[]{:S(2)}) collective-permute-start(bf16[512,384]{1,0:T(8,128)(2,1)} %get-tuple-element.219), channel_id=1, source_target_pairs={{0,4},{4,0},{8,12},{12,8},{16,20},{20,16},{24,28},{28,24},{1,5},{5... | collective-permute-start | bytes 1179656 | tf_op jit(solution)/shard_map/ppermute | solution.py:83
  379.5 40.1 %collective-permute-start.93 = (bf16[512,384]{1,0:T(8,128)(2,1)S(1)}, bf16[512,384]{1,0:T(8,128)(2,1)}, u32[]{:S(2)}, u32[]{:S(2)}) collective-permute-start(bf16[512,384]{1,0:T(8,128)(2,1)S(1)} %get-tuple-element.218), channel_id=1, source_target_pairs={{0,4},{4,0},{8,12},{12,8},{16,20},{20,16},{24,28},{28,24},{1,5},{5... | collective-permute-start | bytes 1179656 | tf_op jit(solution)/shard_map/ppermute | solution.py:83
  411.4 39.9 %collective-permute-start.51 = (bf16[128,2048]{1,0:T(8,128)(2,1)S(1)}, bf16[128,2048]{1,0:T(8,128)(2,1)S(1)}, u32[]{:S(2)}, u32[]{:S(2)}) collective-permute-start(bf16[128,2048]{1,0:T(8,128)(2,1)S(1)} %get-tuple-element.210), channel_id=1, source_target_pairs={{0,1},{1,0},{2,3},{3,2},{4,5},{5,4},{6,7},{7,6},{8,9},{9,8},{10,11... | collective-permute-start | bytes 1572872 | tf_op jit(solution)/shard_map/ppermute | solution.py:115
  486.0 39.9 %collective-permute-start.110 = (bf16[256,768]{0,1:T(8,128)(2,1)S(1)}, bf16[256,768]{0,1:T(8,128)(2,1)}, u32[]{:S(2)}, u32[]{:S(2)}) collective-permute-start(bf16[256,768]{0,1:T(8,128)(2,1)S(1)} %pad_maximum_fusion.27), channel_id=1, source_target_pairs={{0,8},{4,12},{1,9},{5,13},{2,10},{6,14},{3,11},{7,15}} | collective-permute-start | bytes 1179656 | tf_op jit(solution)/shard_map/ppermute | solution.py:104
  525.9 90.7 %collective-permute-start.75 = (bf16[512,512]{0,1:T(8,128)(2,1)}, bf16[512,512]{0,1:T(8,128)(2,1)S(1)}, u32[]{:S(2)}, u32[]{:S(2)}) collective-permute-start(bf16[512,512]{0,1:T(8,128)(2,1)} %bitcast.125), channel_id=1, source_target_pairs={{0,4},{4,0},{8,12},{12,8},{16,20},{20,16},{24,28},{28,24},{1,5},{5... | collective-permute-start | bytes 1572872 | tf_op jit(solution)/shard_map/ppermute | solution.py:83
  552.6 45.8 %collective-permute-start.102 = (bf16[256,1152]{0,1:T(8,128)(2,1)S(1)}, bf16[256,1152]{0,1:T(8,128)(2,1)S(1)}, u32[]{:S(2)}, u32[]{:S(2)}) collective-permute-start(bf16[256,1152]{0,1:T(8,128)(2,1)S(1)} %copy-done.43), channel_id=1, source_target_pairs={{0,8},{4,12},{1,9},{5,13},{2,10},{6,14},{3,11},{7,15}} | collective-permute-start | bytes 1769480 | tf_op jit(solution)/shard_map/ppermute | solution.py:104
  574.1 87.7 %collective-permute-start.67 = (bf16[512,1536]{0,1:T(8,128)(2,1)S(1)}, bf16[512,1536]{0,1:T(8,128)(2,1)S(1)}, u32[]{:S(2)}, u32[]{:S(2)}) collective-permute-start(bf16[512,1536]{0,1:T(8,128)(2,1)S(1)} %copy-done.26), channel_id=1, source_target_pairs={{0,4},{4,0},{8,12},{12,8},{16,20},{20,16},{24,28},{28,24},{1,5},{5... | collective-permute-start | bytes 4718600 | tf_op jit(solution)/shard_map/ppermute | solution.py:83
  655.0 67.4 %collective-permute-start.112 = (bf16[256,768]{0,1:T(8,128)(2,1)S(1)}, bf16[256,768]{0,1:T(8,128)(2,1)S(1)}, u32[]{:S(2)}, u32[]{:S(2)}) collective-permute-start(bf16[256,768]{0,1:T(8,128)(2,1)S(1)} %get-tuple-element.137), channel_id=1, source_target_pairs={{0,8},{4,12},{8,16},{12,20},{16,24},{20,28},{1,9},{5,13},{9,17},{1... | collective-permute-start | bytes 1179656 | tf_op jit(solution)/shard_map/ppermute | solution.py:104
  674.2 44.0 %collective-permute-start.90 = (bf16[256,1152]{0,1:T(8,128)(2,1)S(1)}, bf16[256,1152]{0,1:T(8,128)(2,1)S(1)}, u32[]{:S(2)}, u32[]{:S(2)}) collective-permute-start(bf16[256,1152]{0,1:T(8,128)(2,1)S(1)} %fusion.106), channel_id=1, source_target_pairs={{16,8},{20,12},{24,16},{28,20},{17,9},{21,13},{25,17},{29,21},{18,... | collective-permute-start | bytes 1769480 | tf_op jit(solution)/shard_map/ppermute | solution.py:106
  690.1 41.3 %collective-permute-start.115 = (bf16[256,768]{0,1:T(8,128)(2,1)S(1)}, bf16[256,768]{0,1:T(8,128)(2,1)S(1)}, u32[]{:S(2)}, u32[]{:S(2)}) collective-permute-start(bf16[256,768]{0,1:T(8,128)(2,1)S(1)} %add.806), channel_id=1, source_target_pairs={{8,0},{12,4},{16,8},{20,12},{24,16},{28,20},{9,1},{13,5},{17,9},{2... | collective-permute-start | bytes 1179656 | tf_op jit(solution)/shard_map/ppermute | solution.py:106
  692.2 47.3 %collective-permute-start.68 = (bf16[256,1536]{1,0:T(8,128)(2,1)}, bf16[256,1536]{1,0:T(8,128)(2,1)}, u32[]{:S(2)}, u32[]{:S(2)}) collective-permute-start(bf16[256,1536]{1,0:T(8,128)(2,1)} %get-tuple-element.194), channel_id=1, source_target_pairs={{0,8},{4,12},{1,9},{5,13},{2,10},{6,14},{3,11},{7,15}} | collective-permute-start | bytes 2359304 | tf_op jit(solution)/shard_map/ppermute | solution.py:104
  716.7 46.7 %collective-permute-start.71 = (bf16[256,1536]{1,0:T(8,128)(2,1)}, bf16[256,1536]{1,0:T(8,128)(2,1)}, u32[]{:S(2)}, u32[]{:S(2)}) collective-permute-start(bf16[256,1536]{1,0:T(8,128)(2,1)} %get-tuple-element.195), channel_id=1, source_target_pairs={{24,16},{28,20},{25,17},{29,21},{26,18},{30,22},{27,19},{31,23}} | collective-permute-start | bytes 2359304 | tf_op jit(solution)/shard_map/ppermute | solution.py:106
  722.5 70.9 %collective-permute-start.88 = (bf16[256,1152]{0,1:T(8,128)(2,1)}, bf16[256,1152]{0,1:T(8,128)(2,1)}, u32[]{:S(2)}, u32[]{:S(2)}) collective-permute-start(bf16[256,1152]{0,1:T(8,128)(2,1)} %get-tuple-element.131), channel_id=1, source_target_pairs={{0,8},{4,12},{8,16},{12,20},{16,24},{20,28},{1,9},{5,13},{9,17},{1... | collective-permute-start | bytes 1769480 | tf_op jit(solution)/shard_map/ppermute | solution.py:104
  732.9 61.8 %collective-permute-start.91 = (bf16[256,1152]{0,1:T(8,128)(2,1)}, bf16[256,1152]{0,1:T(8,128)(2,1)}, u32[]{:S(2)}, u32[]{:S(2)}) collective-permute-start(bf16[256,1152]{0,1:T(8,128)(2,1)} %add.782), channel_id=1, source_target_pairs={{8,0},{12,4},{16,8},{20,12},{24,16},{28,20},{9,1},{13,5},{17,9},{2... | collective-permute-start | bytes 1769480 | tf_op jit(solution)/shard_map/ppermute | solution.py:106
  739.5 66.2 %collective-permute-start.96 = (bf16[256,1152]{0,1:T(8,128)(2,1)}, bf16[256,1152]{0,1:T(8,128)(2,1)}, u32[]{:S(2)}, u32[]{:S(2)}) collective-permute-start(bf16[256,1152]{0,1:T(8,128)(2,1)} %get-tuple-element.133), channel_id=1, source_target_pairs={{0,8},{4,12},{8,16},{12,20},{16,24},{20,28},{1,9},{5,13},{9,17},{1... | collective-permute-start | bytes 1769480 | tf_op jit(solution)/shard_map/ppermute | solution.py:104
  763.3 44.1 %collective-permute-start.99 = (bf16[256,1152]{0,1:T(8,128)(2,1)}, bf16[256,1152]{0,1:T(8,128)(2,1)}, u32[]{:S(2)}, u32[]{:S(2)}) collective-permute-start(bf16[256,1152]{0,1:T(8,128)(2,1)} %add.790), channel_id=1, source_target_pairs={{8,0},{12,4},{16,8},{20,12},{24,16},{28,20},{9,1},{13,5},{17,9},{2... | collective-permute-start | bytes 1769480 | tf_op jit(solution)/shard_map/ppermute | solution.py:106
  767.5 43.7 %collective-permute-start.104 = (bf16[256,1152]{0,1:T(8,128)(2,1)}, bf16[256,1152]{0,1:T(8,128)(2,1)}, u32[]{:S(2)}, u32[]{:S(2)}) collective-permute-start(bf16[256,1152]{0,1:T(8,128)(2,1)} %get-tuple-element.135), channel_id=1, source_target_pairs={{0,8},{4,12},{8,16},{12,20},{16,24},{20,28},{1,9},{5,13},{9,17},{1... | collective-permute-start | bytes 1769480 | tf_op jit(solution)/shard_map/ppermute | solution.py:104
  (257 other events, 4706.9 us)

commit v2 on v1

v2 whole, which is shorter than its diff:
```python
import jax
import jax.numpy as jnp
from jax import lax
from jax.experimental import pallas as pl
from jax.experimental.pallas import tpu as pltpu
from jax.sharding import PartitionSpec as P

HD = 64
ROT = 16
STEP = 3
MLP_CHUNKS = 2


norm_eps = 1e-05
rope_base = 10000.0
masked_score = -1e30
beta_one = 0.9
beta_two = 0.95
adam_eps = 1e-08
matrix_rate = 0.08
vector_rate = 0.4
weight_decay = 0.1


def norm_forward(rows, gain, shift):
    centre = jnp.mean(rows, axis=-1, keepdims=True)
    centred = rows - centre
    spread = jnp.mean(centred * centred, axis=-1, keepdims=True)
    factor = lax.rsqrt(spread + norm_eps)
    unit = centred * factor
    return (unit * gain + shift, unit, factor)


def norm_backward(incoming, unit, factor, gain):
    scaled = incoming * gain
    mean_plain = jnp.mean(scaled, axis=-1, keepdims=True)
    mean_along = jnp.mean(scaled * unit, axis=-1, keepdims=True)
    return factor * (scaled - mean_plain - unit * mean_along)


def segments(lengths_row, count):
    ends = jnp.cumsum(lengths_row)
    index = jnp.arange(count, dtype=jnp.int32)
    after = index[:, None] >= ends[None, :]
    segment = jnp.sum(after.astype(jnp.int32), axis=1)
    begin = jnp.max(jnp.where(after, ends[None, :], jnp.zeros_like(ends)[None, :]), axis=1)
    return (segment, index - begin)


def rotary_tables(positions):
    half = ROT // 2
    freqs = rope_base ** (-2.0 * jnp.arange(half, dtype=jnp.float32) / ROT)
    angles = positions[:, None] * freqs[None, :]
    return (jnp.cos(angles), jnp.sin(angles))


def adamw(weight, first, second, gradient, rate, decay):
    first_new = beta_one * first + (1.0 - beta_one) * gradient
    second_new = beta_two * second + (1.0 - beta_two) * gradient * gradient
    first_hat = first_new / (1.0 - beta_one**STEP)
    second_hat = second_new / (1.0 - beta_two**STEP)
    updated = weight - rate * (first_hat / (jnp.sqrt(second_hat) + adam_eps) + decay * weight)
    return (updated, first_new, second_new)


def together(*groups):
    flat, tree = jax.tree.flatten(groups)
    return jax.tree.unflatten(tree, lax.optimization_barrier(flat))


def after(value, *earlier):
    return lax.optimization_barrier((value,) + tuple(earlier))[0]


def pairs_up(lines, low, high, step):
    return [(z * 2 + c, (z + step) * 2 + c) for z in range(low, high) for c in range(2)]


def other_core(array):
    count = lax.axis_size("dp")
    return lax.ppermute(array, "dp", [(d, d ^ 1) for d in range(count)])


def scatter_step(blocks, up, down, j, lines):
    up_send = blocks[lines - j] if up is None else blocks[lines - j] + up
    down_send = blocks[j] if down is None else blocks[j] + down
    up = lax.ppermute(up_send, "dp", pairs_up(lines, 0, lines - j, 1))
    down = lax.ppermute(down_send, "dp", pairs_up(lines, j, lines, -1))
    return up, down


def swap_rows(array, offset):
    count = lax.axis_size("tensor")
    return lax.ppermute(array, "tensor", [(t, t ^ offset) for t in range(count)])


def gather_rows(own, parts):
    return jnp.concatenate([own] + [swap_rows(own, r) for r in range(1, parts)], axis=0)


def scatter_rows(partial, parts):
    rows = partial.shape[0] // parts
    total = partial[:rows].astype(jnp.float32)
    for r in range(1, parts):
        total = total + swap_rows(partial[r * rows : (r + 1) * rows], r).astype(jnp.float32)
    return total


def together_streams(streams, others):
    ways, blocks, others = together(
        [way for _, way, _ in streams], [blocks for blocks, _, _ in streams], others
    )
    return [(b, w, left) for b, w, (_, _, left) in zip(blocks, ways, streams)], others


def add_terms(terms):
    total = terms[0].astype(jnp.float32)
    for term in terms[1:]:
        total = total + term.astype(jnp.float32)
    return total.astype(jnp.bfloat16)


def hop(array, axis, bit):
    count = lax.axis_size(axis)
    return array + lax.ppermute(array, axis, [(i, i ^ bit) for i in range(count)])


def cuts(columns, count):
    tiles = -(-columns // 128)
    bounds = [min(columns, 128 * (tiles * i // count)) for i in range(count + 1)]
    return [(a, b) for a, b in zip(bounds[:-1], bounds[1:]) if b > a]


def paired(array):
    rows, kinds, columns = array.shape
    array = jnp.pad(array, ((0, 0), (0, 0), (0, -columns % 128)))
    return jnp.swapaxes(array.reshape(rows, kinds, -1, 128), 1, 2)


def dot(a, b, contract):
    return lax.dot_general(a, b, (contract, ((), ())), preferred_element_type=jnp.float32)


def whole(shape):
    return pl.BlockSpec(shape, lambda *_: (0,) * len(shape))


def kernel_call(kernel, grid, in_specs, out_specs, out_shape, scratch, name, flops=1, moved=1):
    return pl.pallas_call(
        kernel,
        grid=grid,
        in_specs=in_specs,
        out_specs=out_specs,
        out_shape=out_shape,
        scratch_shapes=scratch,
        compiler_params=pltpu.CompilerParams(vmem_limit_bytes=56 * 1024 * 1024),
        cost_estimate=pl.CostEstimate(flops=flops, bytes_accessed=moved, transcendentals=0),
        name=name,
    )


def turn(x, keep, low, high, direction):
    return (
        x * keep
        + pltpu.roll(x, 120, 1) * (low * direction)
        + pltpu.roll(x, 8, 1) * (high * direction)
    )


def row_steps(rows):
    return 128 if rows % 128 == 0 else rows


def fill_bias(bias_ref, column_ref, row_ref):
    rows = bias_ref.shape[0]
    step = row_steps(rows)

    def body(r, _):
        at = pl.ds(pl.multiple_of(r * step, step), step)
        marks = column_ref[at, :]
        visible = (marks[:, 0:1] == row_ref[0:1, :]) & (marks[:, 1:2] >= row_ref[1:2, :])
        bias_ref[at, :] = jnp.where(visible, 0.0, masked_score)
        return 0

    lax.fori_loop(0, rows // step, body, 0)


def matmul(a, b, contract=((1,), (0,))):
    return lax.dot_general(a, b, (contract, ((), ())), preferred_element_type=jnp.float32)


def attend_kernel(
    normed_ref, weight_ref, offset_ref, keep_ref, low_ref, high_ref, column_ref, row_ref,
    mixed_ref, context_ref, totals_ref, bias_ref, score_ref, prob_ref,
):
    kind = pl.program_id(0)
    rows, columns = context_ref.shape
    step = row_steps(rows)
    raw = matmul(normed_ref[...], weight_ref[0]) + offset_ref[0]
    here = pl.multiple_of(kind * columns, 128)

    @pl.when(kind < 2)
    def _():
        for b in range(columns // 128):
            block = turn(raw[:, b * 128 : (b + 1) * 128], keep_ref[...], low_ref[...], high_ref[...], 1.0)
            mixed_ref[:, pl.ds(pl.multiple_of(here + b * 128, 128), 128)] = block.astype(jnp.bfloat16)

    @pl.when(kind == 2)
    def _():
        mixed_ref[:, pl.ds(here, columns)] = raw.astype(jnp.bfloat16)
        fill_bias(bias_ref, column_ref, row_ref)
        lane = lax.broadcasted_iota(jnp.int32, (1, 128), 1)

        def pair_body(pair, _):
            first = pl.multiple_of(pair * 128, 128)
            queries = mixed_ref[:, pl.ds(first, 128)]
            keys = mixed_ref[:, pl.ds(pl.multiple_of(columns + first, 128), 128)]
            values = mixed_ref[:, pl.ds(pl.multiple_of(2 * columns + first, 128), 128)]
            parts = []
            for h in range(2):
                mine = (lane >= HD * h) & (lane < HD * (h + 1))
                score_ref[...] = matmul(
                    jnp.where(mine, queries, jnp.zeros_like(queries)), keys, ((1,), (1,))
                )

                def rows_body(r, _):
                    at = pl.ds(pl.multiple_of(r * step, step), step)
                    scores = score_ref[at, :] * (HD**-0.5) + bias_ref[at, :]
                    summit = jnp.max(scores, axis=1, keepdims=True)
                    weights = jnp.exp(scores - summit)
                    total = jnp.sum(weights, axis=1, keepdims=True)
                    prob_ref[at, :] = (weights * (1.0 / total)).astype(jnp.bfloat16)
                    spot = lane == pair * 2 + h
                    totals_ref[at, :] = jnp.where(
                        spot, summit + jnp.log(total), totals_ref[at, :]
                    )
                    return 0

                lax.fori_loop(0, rows // step, rows_body, 0, unroll=True)
                parts.append(matmul(prob_ref[...], values))
            both = jnp.where(lane < HD, parts[0], parts[1])
            context_ref[:, pl.ds(first, 128)] = both.astype(jnp.bfloat16)
            return 0

        totals_ref[...] = jnp.zeros_like(totals_ref)
        lax.fori_loop(0, columns // 128, pair_body, 0)


def attend(normed_all, entry_full, offsets, tables, marks):
    rows, width = normed_all.shape
    columns = entry_full.shape[2]
    bf16, f32 = jnp.bfloat16, jnp.float32
    return kernel_call(
        attend_kernel,
        (3,),
        [whole((rows, width)), pl.BlockSpec((1, width, columns), lambda k: (k, 0, 0)),
         pl.BlockSpec((1, 1, columns), lambda k: (k, 0, 0))]
        + [whole((rows, 128))] * 3 + [whole((rows, 2)), whole((2, rows))],
        [whole((rows, 3 * columns)), whole((rows, columns)), whole((rows, 128))],
        [jax.ShapeDtypeStruct((rows, 3 * columns), bf16), jax.ShapeDtypeStruct((rows, columns), bf16),
         jax.ShapeDtypeStruct((rows, 128), f32)],
        [pltpu.VMEM((rows, rows), f32), pltpu.VMEM((rows, rows), f32), pltpu.VMEM((rows, rows), bf16)],
        "attention",
    )(normed_all, entry_full, offsets.reshape(3, 1, columns), *tables, *marks)


def attend_back_kernel(
    middle_ref, exit_ref, mixed_ref, totals_ref, keep_ref, low_ref, high_ref, column_ref, row_ref,
    grad_ref, bias_ref, score_ref, prob_grad_ref, prob_ref, score_grad_ref, context_grad_ref,
):
    rows = middle_ref.shape[0]
    columns = exit_ref.shape[2]
    step = row_steps(rows)
    context_grad_ref[...] = matmul(middle_ref[...], exit_ref[0]).astype(jnp.bfloat16)
    fill_bias(bias_ref, column_ref, row_ref)
    lane = lax.broadcasted_iota(jnp.int32, (1, 128), 1)

    def pair_body(pair, _):
        first = pl.multiple_of(pair * 128, 128)
        second = pl.multiple_of(columns + first, 128)
        third = pl.multiple_of(2 * columns + first, 128)
        queries = mixed_ref[:, pl.ds(first, 128)]
        keys = mixed_ref[:, pl.ds(second, 128)]
        values = mixed_ref[:, pl.ds(third, 128)]
        incoming = context_grad_ref[:, pl.ds(first, 128)]
        query_parts, key_parts, value_parts = [], [], []
        for h in range(2):
            mine = (lane >= HD * h) & (lane < HD * (h + 1))
            score_ref[...] = matmul(
                jnp.where(mine, queries, jnp.zeros_like(queries)), keys, ((1,), (1,))
            )
            prob_grad_ref[...] = matmul(
                jnp.where(mine, incoming, jnp.zeros_like(incoming)), values, ((1,), (1,))
            )

            def rows_body(r, _):
                at = pl.ds(pl.multiple_of(r * step, step), step)
                spot = lane == pair * 2 + h
                total = jnp.sum(jnp.where(spot, totals_ref[at, :], 0.0), axis=1, keepdims=True)
                probs = jnp.exp(score_ref[at, :] * (HD**-0.5) + bias_ref[at, :] - total)
                prob_grad = prob_grad_ref[at, :]
                inner = jnp.sum(probs * prob_grad, axis=1, keepdims=True)
                score_grad_ref[at, :] = (probs * (prob_grad - inner)).astype(jnp.bfloat16)
                prob_ref[at, :] = probs.astype(jnp.bfloat16)
                return 0

            lax.fori_loop(0, rows // step, rows_body, 0, unroll=True)
            query_parts.append(matmul(score_grad_ref[...], keys))
            key_parts.append(matmul(score_grad_ref[...], queries, ((0,), (0,))))
            value_parts.append(matmul(prob_ref[...], incoming, ((0,), (0,))))
        keep, low, high = keep_ref[...], low_ref[...], high_ref[...]
        scale = HD**-0.5
        query_grad = jnp.where(lane < HD, query_parts[0], query_parts[1]) * scale
        key_grad = jnp.where(lane < HD, key_parts[0], key_parts[1]) * scale
        value_grad = jnp.where(lane < HD, value_parts[0], value_parts[1])
        grad_ref[:, pl.ds(first, 128)] = turn(query_grad, keep, low, high, -1.0).astype(jnp.bfloat16)
        grad_ref[:, pl.ds(second, 128)] = turn(key_grad, keep, low, high, -1.0).astype(jnp.bfloat16)
        grad_ref[:, pl.ds(third, 128)] = value_grad.astype(jnp.bfloat16)
        return 0

    lax.fori_loop(0, columns // 128, pair_body, 0)


def attend_back(middle_all, exit_full, mixed, totals, tables, marks):
    rows, width = middle_all.shape
    columns = exit_full.shape[2]
    bf16, f32 = jnp.bfloat16, jnp.float32
    square = (rows, rows)
    return kernel_call(
        attend_back_kernel,
        (1,),
        [whole((rows, width)), pl.BlockSpec((1, width, columns), lambda *_: (3, 0, 0)),
         whole((rows, 3 * columns)), whole((rows, 128))]
        + [whole((rows, 128))] * 3 + [whole((rows, 2)), whole((2, rows))],
        whole((rows, 3 * columns)),
        jax.ShapeDtypeStruct((rows, 3 * columns), bf16),
        [pltpu.VMEM(square, f32), pltpu.VMEM(square, f32), pltpu.VMEM(square, f32),
         pltpu.VMEM(square, bf16), pltpu.VMEM(square, bf16), pltpu.VMEM((rows, columns), bf16)],
        "attention_back",
    )(middle_all, exit_full, mixed, totals, *tables, *marks)


def feed_kernel(
    second_ref, cot_ref, full_ref, acts_ref, branch_ref, second_grad_ref, weight_ref, hidden_grad_ref, sems
):
    j = pl.program_id(0)
    rows, width = second_ref.shape
    padded = acts_ref.shape[1] // 3
    pairs = padded // 128
    step = row_steps(rows)
    bf16 = jnp.bfloat16

    def load(at, size, which):
        here = pl.ds(at, size)
        return pltpu.make_async_copy(full_ref.at[:, here], weight_ref.at[:, here], sems.at[which])

    @pl.when(j == 0)
    def _():
        load(2 * padded, padded, 0).start()
        for p in range(pairs):
            load(p * 256, 256, p + 1).start()
        load(2 * padded, padded, 0).wait()
        for low in range(0, padded, 256):
            high = min(low + 256, padded)
            hidden_grad_ref[:, low:high] = matmul(
                cot_ref[...], weight_ref[:, 2 * padded + low : 2 * padded + high]
            )
        for p in range(pairs):
            load(p * 256, 256, p + 1).wait()
            gate_up = matmul(second_ref[...], weight_ref[:, p * 256 : (p + 1) * 256])
            gate, upper = gate_up[:, :128], gate_up[:, 128:]
            grad = hidden_grad_ref[:, p * 128 : (p + 1) * 128]
            sigmoid = jax.nn.sigmoid(gate)
            activated = gate * sigmoid
            acts_ref[:, p * 256 : p * 256 + 128] = (
                grad * upper * sigmoid * (1.0 + gate * (1.0 - sigmoid))
            ).astype(bf16)
            acts_ref[:, p * 256 + 128 : (p + 1) * 256] = (grad * activated).astype(bf16)
            hidden = 2 * padded + p * 128
            acts_ref[:, hidden : hidden + 128] = (activated * upper).astype(bf16)

    @pl.when(j > 0)
    def _():
        size = branch_ref.shape[1]
        here = pl.ds(pl.multiple_of((j - 1) * size, size), size)
        over = ((1,), (1,))
        second_grad_ref[...] = matmul(
            acts_ref[:, : 2 * padded], weight_ref[here, : 2 * padded], over
        ).astype(bf16)
        branch_ref[...] = matmul(
            acts_ref[:, 2 * padded :], weight_ref[here, 2 * padded :], over
        ).astype(bf16)


def feed(second_all, cot_all, full):
    rows, width = second_all.shape
    padded = full.shape[1] // 3
    chunk = 256
    bf16, f32 = jnp.bfloat16, jnp.float32
    out = pl.BlockSpec((rows, chunk), lambda j: (0, jnp.maximum(j - 1, 0)))
    return kernel_call(
        feed_kernel,
        (1 + width // chunk,),
        [whole((rows, width))] * 2 + [pl.BlockSpec(memory_space=pl.ANY)],
        [whole((rows, 3 * padded)), out, out],
        [jax.ShapeDtypeStruct((rows, 3 * padded), bf16)] + [jax.ShapeDtypeStruct((rows, width), bf16)] * 2,
        [pltpu.VMEM((width, 3 * padded), bf16), pltpu.VMEM((rows, padded), f32),
         pltpu.SemaphoreType.DMA((1 + padded // 128,))],
        "feed_forward",
    )(second_all, cot_all, full)


def turned_kernel(blocks_ref, rows_ref, out_ref):
    out_ref[...] = rows_ref[...].T


def turned_blocks(array, blocks, size):
    rows = array.shape[0]
    return pl.pallas_call(
        turned_kernel,
        grid_spec=pltpu.PrefetchScalarGridSpec(
            num_scalar_prefetch=1,
            grid=(len(blocks),),
            in_specs=[pl.BlockSpec((rows, size), lambda b, blocks_ref: (0, blocks_ref[b]))],
            out_specs=pl.BlockSpec((size, rows), lambda b, blocks_ref: (b, 0)),
        ),
        out_shape=jax.ShapeDtypeStruct((len(blocks) * size, rows), array.dtype),
        compiler_params=pltpu.CompilerParams(vmem_limit_bytes=32 * 1024 * 1024),
        cost_estimate=pl.CostEstimate(flops=1, bytes_accessed=1, transcendentals=0),
        name="turned_blocks",
    )(jnp.stack(blocks).astype(jnp.int32), array)


def terms_kernel(split, own_left, other_left, own_last, other_last, own_ref, other_ref, *outs):
    k = pl.program_id(0)

    def write(own, other):
        total = (matmul(own[...], own_ref[...]) + matmul(other[...], other_ref[...])).astype(jnp.bfloat16)
        size = outs[0].shape[0]
        for s, out in enumerate(outs):
            out[...] = total[s * size : (s + 1) * size]

    @pl.when(k < split)
    def _():
        write(own_left, other_left)

    @pl.when(k >= split)
    def _():
        write(own_last, other_last)


def weight_terms(left, left_last, right, tile, split, lines):
    count, rows = left[0].shape
    columns = right[0].shape[1]
    size = count // lines
    left_spec = whole((count, rows))
    right_spec = pl.BlockSpec((rows, tile), lambda k: (0, k))
    return list(
        kernel_call(
            lambda *refs: terms_kernel(split, *refs),
            (columns // tile,),
            [left_spec] * 4 + [right_spec] * 2,
            [pl.BlockSpec((size, tile), lambda k: (0, k))] * lines,
            [jax.ShapeDtypeStruct((size, columns), jnp.bfloat16)] * lines,
            [],
            "weight_terms",
            4 * count * rows * columns,
            2 * (4 * count * rows + 2 * rows * columns + count * columns),
        )(*left, *left_last, *right)
    )


def summed(refs, rows, columns):
    own, up, down = [ref[rows, columns].astype(jnp.float32) for ref in refs]
    return own + up + down


def plain_step_kernel(own, up, down, weight, first, second, *outs):
    everything = slice(None)
    gradient = summed((own, up, down), everything, everything)
    news = adamw(weight[0], first[0], second[0], gradient, matrix_rate, weight_decay)
    for out, value in zip(outs, (gradient,) + tuple(news)):
        out[0] = value


def plain_step(parts_of_sum, params):
    kinds, rows, columns = params[0].shape
    tile = rows // 2
    part = pl.BlockSpec((tile, columns), lambda k, r: (r, k))
    block = pl.BlockSpec((1, tile, columns), lambda k, r: (k, r, 0))
    return kernel_call(
        plain_step_kernel,
        (kinds, 2),
        [part] * 3 + [block] * 3,
        [block] * 4,
        [jax.ShapeDtypeStruct((kinds, rows, columns), jnp.float32)] * 4,
        [],
        "plain_step",
    )(*parts_of_sum, *params)


def feed_step_kernel(runs, *refs):
    count = 3 * len(runs)
    gate, down = refs[count : count + 3], refs[count + 3 : count + 6]
    gate_outs, down_outs = refs[count + 6 : count + 10], refs[count + 10 : count + 14]
    everything = slice(None)
    for at, (low, high) in enumerate(runs):
        sums = refs[3 * at : 3 * at + 3]
        padded = sums[0].shape[1] // 3
        for c in range(0, high - low, 128):
            size = min(128, high - low - c)
            here = slice(low + c, low + c + size)
            for k in range(2):
                gradient = summed(sums, everything, slice(2 * c + 128 * k, 2 * c + 128 * k + size))
                news = adamw(
                    *[ref[:, k, here] for ref in gate], gradient, matrix_rate, weight_decay
                )
                for out, value in zip(gate_outs, (gradient,) + tuple(news)):
                    out[:, k, here] = value
        here = slice(low, high)
        gradient = summed(sums, everything, slice(2 * padded, 2 * padded + high - low))
        news = adamw(*[ref[:, here] for ref in down], gradient, matrix_rate, weight_decay)
        for out, value in zip(down_outs, (gradient,) + tuple(news)):
            out[:, here] = value


def feed_step(runs, sums, gate, down):
    rows, columns = down[0].shape
    tile = 32
    gate_block = pl.BlockSpec((tile, 2, columns), lambda r: (r, 0, 0))
    down_block = pl.BlockSpec((tile, columns), lambda r: (r, 0))
    flat = [part for parts_of_sum in sums for part in parts_of_sum]
    return kernel_call(
        lambda *refs: feed_step_kernel(runs, *refs),
        (rows // tile,),
        [pl.BlockSpec((tile, part.shape[1]), lambda r: (r, 0)) for part in flat]
        + [gate_block] * 3
        + [down_block] * 3,
        [gate_block] * 4 + [down_block] * 4,
        [jax.ShapeDtypeStruct((rows, 2, columns), jnp.float32)] * 4
        + [jax.ShapeDtypeStruct((rows, columns), jnp.float32)] * 4,
        [],
        "feed_step",
    )(*flat, *gate, *down)


def on_device(
    tokens,
    cotangent,
    lengths,
    entry_weight,
    entry_first,
    entry_second,
    exit_weight,
    exit_first,
    exit_second,
    gate_weight,
    gate_first,
    gate_second,
    down_weight,
    down_first,
    down_second,
    bias_rows,
    bias_first,
    bias_second,
    norm_gains,
    gains_first,
    gains_second,
):
    parts = lax.axis_size("tensor")
    part_index = lax.axis_index("tensor")
    dp_index = lax.axis_index("dp")
    dp_count = lax.axis_size("dp")
    lines = dp_count // 2
    last = lines - 1
    place = dp_index // 2
    core = dp_index % 2
    local_rows = tokens.shape[0]
    group = local_rows * parts
    width = tokens.shape[1]
    size = width // dp_count
    head_cols = entry_weight.shape[2]
    hidden_cols = down_weight.shape[1]
    bf16 = jnp.bfloat16
    own_blocks = [((place - s + lines) % lines) * 2 + core for s in range(lines)]
    other_blocks = [((place - s + lines) % lines) * 2 + 1 - core for s in range(lines)]
    none = (None, None)

    def advance(streams):
        return [
            (blocks, scatter_step(blocks, *way, left, lines), left - 1) if left > 0 else stream
            for stream in streams
            for blocks, way, left in [stream]
        ]

    def begin(blocks):
        return advance([(blocks, none, last)])

    def finish(streams):
        while any(left > 0 for _, _, left in streams):
            streams = advance(streams)
        return streams

    def parts_of(stream):
        blocks, way, _ = stream
        return (blocks[0],) + tuple(way)

    def both_cores(array):
        both = turned_blocks(array, own_blocks + other_blocks, size)
        return both[: width // 2], other_core(both[width // 2 :])

    kinds_own = jnp.concatenate(
        [jnp.swapaxes(entry_weight, 0, 1).astype(bf16), exit_weight.astype(bf16)[None]], axis=0
    )
    kinds = lax.all_gather(kinds_own, "dp", axis=1, tiled=True)
    chunks = cuts(hidden_cols, MLP_CHUNKS)

    def unit_of(a, b):
        gates = paired(gate_weight[:, :, a:b].astype(bf16)).reshape(size, -1)
        downs = jnp.pad(down_weight[:, a:b].astype(bf16), ((0, 0), (0, -(b - a) % 128)))
        return jnp.concatenate([gates, downs], axis=1)

    fulls = []
    earlier = kinds_own
    for a, b in chunks:
        earlier = after(unit_of(a, b), earlier)
        fulls.append(lax.all_gather(earlier, "dp", axis=0, tiled=True))

    segment, positions = segments(lengths[0], group)
    row_blocks = jnp.arange(parts, dtype=jnp.int32) ^ part_index
    row_index = (
        row_blocks[:, None] * local_rows + jnp.arange(local_rows, dtype=jnp.int32)[None, :]
    ).reshape(group)
    segment, positions = [
        jnp.concatenate(
            [
                lax.dynamic_slice_in_dim(array, (part_index ^ r) * local_rows, local_rows, 0)
                for r in range(parts)
            ]
        )
        for array in (segment, positions)
    ]
    cosine, sine = rotary_tables(positions.astype(jnp.float32))
    ones = jnp.ones((group, HD - ROT), jnp.float32)
    blank = jnp.zeros((group, ROT // 2), jnp.float32)
    empty = jnp.zeros((group, HD - ROT), jnp.float32)
    tables = [
        jnp.concatenate([a, b, c] * 2, axis=1)
        for a, b, c in ((cosine, cosine, ones), (-sine, blank, empty), (blank, sine, empty))
    ]
    marks = (jnp.stack([segment, row_index], axis=1), jnp.stack([segment, row_index], axis=0))
    column_start = part_index * head_cols
    rotmask = (jnp.arange(head_cols, dtype=jnp.int32) % HD < ROT).astype(jnp.float32)
    query_bias = lax.dynamic_slice_in_dim(bias_rows[0], column_start, head_cols, 0)
    key_bias = lax.dynamic_slice_in_dim(bias_rows[1], column_start, head_cols, 0) * rotmask
    value_bias = lax.dynamic_slice_in_dim(bias_rows[2], column_start, head_cols, 0)
    offsets = jnp.stack([query_bias, key_bias, value_bias])

    rows_in = tokens.astype(jnp.float32)
    normed, unit_one, factor_one = norm_forward(rows_in, norm_gains[0], bias_rows[3])
    normed_all = gather_rows(normed.astype(bf16), parts)
    cot_all = gather_rows(after(cotangent, normed_all), parts)
    normed_sides = both_cores(after(normed_all, cot_all))
    cot_sides = both_cores(after(cot_all, normed_sides[0]))
    kinds, normed_all, normed_sides, cot_all, cot_sides, tables, marks = together(
        kinds, normed_all, normed_sides, cot_all, cot_sides, tables, marks
    )

    mixed, context, log_totals = attend(normed_all, kinds, offsets, tables, marks)
    branch = dot(context, kinds[3], ((1,), (1,))).astype(bf16)
    context_other = other_core(context)
    branch, context_other = together(branch, context_other)
    branch = scatter_rows(branch, parts)
    middle = rows_in + branch
    second, unit_two, factor_two = norm_forward(middle, norm_gains[1], bias_rows[4])
    second_all = gather_rows(second.astype(bf16), parts)
    second_all, fulls[0] = together(second_all, fulls[0])

    second_sides = both_cores(second_all)
    streams, branch_terms, second_terms = [], [], []
    for at, full in enumerate(fulls):
        streams = advance(streams)
        acts, branch_term, second_term = feed(second_all, cot_all, fulls[at])
        branch_terms.append(branch_term)
        second_terms.append(second_term)
        if at + 1 < len(fulls):
            padded = acts.shape[1] // 3
            terms = weight_terms(
                second_sides, cot_sides, (acts, other_core(acts)), padded, 2, lines
            )
            streams = streams + begin(terms)
            streams, fulls[at + 1] = together_streams(streams, fulls[at + 1])
    second_grad = add_terms(second_terms)
    second_grad, acts = together(second_grad, acts)
    acts_other = other_core(acts)
    second_grad = scatter_rows(second_grad, parts)
    branch_two = add_terms(branch_terms)
    padded = acts.shape[1] // 3
    terms = weight_terms(second_sides, cot_sides, (acts, acts_other), padded, 2, lines)
    streams, (second_grad, terms, branch_two) = together_streams(
        streams, (second_grad, terms, branch_two)
    )

    streams = advance(streams) + begin(terms)
    middle_grad = cotangent.astype(jnp.float32) + norm_backward(
        second_grad, unit_two, factor_two, norm_gains[1]
    )
    middle_all = gather_rows(middle_grad.astype(bf16), parts)
    streams, middle_all = together_streams(streams, middle_all)

    streams = advance(streams)
    mixed_grad = attend_back(middle_all, kinds, mixed, log_totals, tables, marks)
    middle_sides = both_cores(middle_all)
    exit_terms = weight_terms(
        middle_sides, middle_sides, (context, context_other), head_cols, 1, lines
    )
    streams, (mixed_grad, exit_terms) = together_streams(streams, (mixed_grad, exit_terms))

    streams = advance(streams) + begin(exit_terms)
    entry_terms = weight_terms(
        normed_sides, normed_sides, (mixed_grad, other_core(mixed_grad)), head_cols, 3, lines
    )
    mixed_grad, entry_terms = together(mixed_grad, entry_terms)
    streams = streams + begin(entry_terms)
    normed_grad = sum(
        dot(mixed_grad[:, k * head_cols : (k + 1) * head_cols], kinds[k], ((1,), (1,)))
        for k in range(3)
    )
    normed_grad = scatter_rows(normed_grad.astype(bf16), parts)
    streams, normed_grad = together_streams(streams, normed_grad)

    streams = finish(streams[:-2]) + advance(streams[-2:])
    input_gradient = middle_grad + norm_backward(normed_grad, unit_one, factor_one, norm_gains[0])
    gain_two_grad = jnp.sum(second_grad * unit_two, axis=0)
    shift_two_grad = jnp.sum(second_grad, axis=0)
    gain_one_grad = jnp.sum(normed_grad * unit_one, axis=0)
    shift_one_grad = jnp.sum(normed_grad, axis=0)
    column_sums = jnp.sum(mixed_grad.astype(jnp.float32), axis=0).reshape(3, head_cols)
    column_sums = column_sums * jnp.stack([jnp.ones_like(rotmask), rotmask, jnp.ones_like(rotmask)])
    placed = lax.dynamic_update_slice_in_dim(
        jnp.zeros((3, width), jnp.float32), column_sums, column_start, 1
    )
    norms_local = jnp.stack([shift_one_grad, shift_two_grad, gain_one_grad, gain_two_grad])
    vectors = jnp.concatenate([placed, norms_local], axis=0)
    bit = 1
    while bit < parts:
        vectors = hop(vectors, "tensor", bit)
        bit *= 2
    vectors = hop(vectors, "dp", 1)

    (
        gate_gradient, gate_updated, gate_first_new, gate_second_new,
        down_gradient, down_updated, down_first_new, down_second_new,
    ) = feed_step(
        chunks,
        [parts_of(stream) for stream in streams[:-2]],
        (gate_weight, gate_first, gate_second),
        (down_weight, down_first, down_second),
    )
    streams, (vectors, gate_updated, down_updated) = together_streams(
        streams, (vectors, gate_updated, down_updated)
    )

    bit = 2
    while bit < dp_count:
        vectors = hop(vectors, "dp", bit)
        bit *= 2
    streams = finish(streams)
    branch_two = scatter_rows(after(branch_two, vectors), parts)
    output_rows = (middle + branch_two).astype(bf16)
    bias_gradient = vectors[:5]
    gains_gradient = vectors[5:]
    exit_gradient, exit_updated, exit_first_new, exit_second_new = [
        array[0]
        for array in plain_step(
            parts_of(streams[-2]), [array[None] for array in (exit_weight, exit_first, exit_second)]
        )
    ]
    entry_gradient, entry_updated, entry_first_new, entry_second_new = [
        jnp.swapaxes(array, 0, 1)
        for array in plain_step(
            parts_of(streams[-1]),
            [jnp.swapaxes(array, 0, 1) for array in (entry_weight, entry_first, entry_second)],
        )
    ]
    bias_updated, bias_first_new, bias_second_new = adamw(
        bias_rows, bias_first, bias_second, bias_gradient, vector_rate, 0.0
    )
    gains_updated, gains_first_new, gains_second_new = adamw(
        norm_gains, gains_first, gains_second, gains_gradient, vector_rate, 0.0
    )
    return (
        output_rows,
        input_gradient,
        entry_gradient,
        entry_updated,
        entry_first_new,
        entry_second_new,
        exit_gradient,
        exit_updated,
        exit_first_new,
        exit_second_new,
        gate_gradient,
        gate_updated,
        gate_first_new,
        gate_second_new,
        down_gradient,
        down_updated,
        down_first_new,
        down_second_new,
        bias_gradient,
        bias_updated,
        bias_first_new,
        bias_second_new,
        gains_gradient,
        gains_updated,
        gains_first_new,
        gains_second_new,
    )


def solution(mesh):
    return jax.shard_map(
        on_device,
        mesh=mesh,
        in_specs=(
            P(("dp", "tensor"), None),
            P(("dp", "tensor"), None),
            P("dp", None),
            P("dp", None, "tensor"),
            P("dp", None, "tensor"),
            P("dp", None, "tensor"),
            P("dp", "tensor"),
            P("dp", "tensor"),
            P("dp", "tensor"),
            P("dp", None, "tensor"),
            P("dp", None, "tensor"),
            P("dp", None, "tensor"),
            P("dp", "tensor"),
            P("dp", "tensor"),
            P("dp", "tensor"),
            P(),
            P(),
            P(),
            P(),
            P(),
            P(),
        ),
        out_specs=(
            P(("dp", "tensor"), None),
            P(("dp", "tensor"), None),
            P("dp", None, "tensor"),
            P("dp", None, "tensor"),
            P("dp", None, "tensor"),
            P("dp", None, "tensor"),
            P("dp", "tensor"),
            P("dp", "tensor"),
            P("dp", "tensor"),
            P("dp", "tensor"),
            P("dp", None, "tensor"),
            P("dp", None, "tensor"),
            P("dp", None, "tensor"),
            P("dp", None, "tensor"),
            P("dp", "tensor"),
            P("dp", "tensor"),
            P("dp", "tensor"),
            P("dp", "tensor"),
            P(),
            P(),
            P(),
            P(),
            P(),
            P(),
            P(),
            P(),
        ),
        check_vma=False,
    )
```

time: 893 us -> 634 us (0.71); the launches traced: 879 us -> 629 us
  starting transfers between devices: 271 us -> 116 us
  Pallas kernels: 0 us -> 148 us
  other arithmetic: 129 us -> 45.2 us
  matrix products: 90.1 us -> 11.8 us
  local copies, waits for them, and re-layouts: 104 us -> 33.8 us
  waiting for transfers between devices: 280 us -> 259 us
  between operations: 4.77 us -> 15.3 us
    ppermute x77 -> x29, starting transfers between devices: 238 us -> 82.1 us  [the longest x12 58.9 us: scatter_step(): up = lax.ppermute(up_send, 'dp', pairs_up(lines, 0, lines - j, 1))]
    pallas_call x0 -> x15, Pallas kernels: none -> 148 us  [the longest x2 43.1 us: feed(): kernel_call(feed_kernel, (1 + width // chunk,), [whole((rows, width))] *...]
    ppermute x77 -> x29, waiting for transfers between devices: 184 us -> 45.3 us  [the longest x12 34.6 us: scatter_step(): up = lax.ppermute(up_send, 'dp', pairs_up(lines, 0, lines - j, 1))]
    dot_general x40 -> x4, matrix products: 77.5 us -> 11.8 us  [dot(): lax.dot_general(a, b, (contract, ((), ())), preferred_element_type=jnp.fl...]
    all_gather x0 -> x3, waiting for transfers between devices: none -> 64.2 us  [the longest x2 64.2 us: on_device(): fulls.append(lax.all_gather(earlier, 'dp', axis=0, tiled=True))]
    ppermute x24, waiting for transfers between devices: 95.7 us -> 144 us  [swap_rows(): lax.ppermute(array, 'tensor', [(t, t ^ offset) for t in range(count)])]
    unnamed x393 -> x131, local copies, waits for them, and re-layouts: 55.1 us -> 11.9 us
    concatenate x23 -> x4, other arithmetic: 33.4 us -> 4.17 us  [the longest x2 3.1 us: unit_of(): return jnp.concatenate([gates, downs], axis=1)]
  transfers between devices with their start and end apart: 121 -> 64, of which waited for: 34 -> 28; matrix products, arithmetic and copies ran while one was open for 33% -> 10% of each run, Pallas kernels for 0% -> 17%
where the time goes in v2:
time: 634 us; the launch traced here: 629 us
  waiting for transfers between devices  259 us (41%)
  Pallas kernels  148 us (23%)
  starting transfers between devices  116 us (18%)
  other arithmetic  45.2 us (7%)
  local copies, waits for them, and re-layouts  33.8 us (5%)
  between operations  15.3 us (2%)
  matrix products  11.8 us (2%)
    ppermute x24, waiting for transfers between devices, swap_rows(): lax.ppermute(array, 'tensor', [(t, t ^ offset) for t in range(count)])  144 us
    all_gather x2, waiting for transfers between devices, on_device(): fulls.append(lax.all_gather(earlier, 'dp', axis=0, tiled=True))  64.2 us
    ppermute x12, starting transfers between devices, scatter_step(): up = lax.ppermute(up_send, 'dp', pairs_up(lines, 0, lines - j, 1))  58.9 us
    pallas_call x2, Pallas kernels, feed(): kernel_call(feed_kernel, (1 + width // chunk,), [whole((rows, width))] *...  43.1 us
    ppermute x12, waiting for transfers between devices, scatter_step(): up = lax.ppermute(up_send, 'dp', pairs_up(lines, 0, lines - j, 1))  34.6 us
    ppermute x24, starting transfers between devices, swap_rows(): lax.ppermute(array, 'tensor', [(t, t ^ offset) for t in range(count)])  32.2 us
    pallas_call x4, Pallas kernels, weight_terms(): kernel_call(lambda *refs: terms_kernel(split, *refs), (columns // tile,),...  31.3 us
    pallas_call x1, Pallas kernels, feed_step(): kernel_call(lambda *refs: feed_step_kernel(runs, *refs), (rows // tile,),...  25.1 us
  transfers between devices with their start and end apart: 64, of which 28 were waited for; matrix products, arithmetic and copies ran while one was open for 10% of the time, Pallas kernels for 17%

profile of v2, /device:TPU:0, one launch (start us, length us, event | category | flops | bytes accessed | tf_op | source)
XLA Modules:
  0.0 629.3 jit_solution(1284061256095248685)
XLA Ops:
  36.1 11.8 %collective-permute-done.2 = bf16[128,2048]{1,0:T(8,128)(2,1)S(1)} collective-permute-done((bf16[128,2048]{1,0:T(8,128)(2,1)S(1)}, bf16[128,2048]{1,0:T(8,128)(2,1)S(1)}, u32[]{:S(2)}, u32[]{:S(2)}) %collective-permute-start.2) | collective-permute-done | bytes 524320 | tf_op jit(solution)/shard_map/ppermute | solution.py:94
  48.0 10.5 %collective-permute-done.1 = bf16[128,2048]{1,0:T(8,128)(2,1)S(1)} collective-permute-done((bf16[128,2048]{1,0:T(8,128)(2,1)S(1)}, bf16[128,2048]{1,0:T(8,128)(2,1)S(1)}, u32[]{:S(2)}, u32[]{:S(2)}) %collective-permute-start.1) | collective-permute-done | bytes 524320 | tf_op jit(solution)/shard_map/ppermute | solution.py:94
  65.3 10.3 %collective-permute-done.3 = bf16[128,2048]{1,0:T(8,128)(2,1)S(1)} collective-permute-done((bf16[128,2048]{1,0:T(8,128)(2,1)S(1)}, bf16[128,2048]{1,0:T(8,128)(2,1)S(1)}, u32[]{:S(2)}, u32[]{:S(2)}) %collective-permute-start.3) | collective-permute-done | bytes 524320 | tf_op jit(solution)/shard_map/ppermute | solution.py:94
  75.7 12.5 %collective-permute-done.4 = bf16[128,2048]{1,0:T(8,128)(2,1)} collective-permute-done((bf16[128,2048]{1,0:T(8,128)(2,1)S(1)}, bf16[128,2048]{1,0:T(8,128)(2,1)}, u32[]{:S(2)}, u32[]{:S(2)}) %collective-permute-start.4) | collective-permute-done | bytes 524320 | tf_op jit(solution)/shard_map/ppermute | solution.py:94
  102.5 15.1 %attention.1 = (bf16[512,1536]{1,0:T(8,128)(2,1)}, bf16[512,512]{1,0:T(8,128)(2,1)}, f32[512,128]{1,0:T(8,128)}) custom-call(bf16[512,2048]{1,0:T(8,128)(2,1)} %copy-done.2, bf16[4,2048,512]{2,1,0:T(8,128)(2,1)} %all-gather.4.cloned.1.call-done.weight_ref.exit_ref, f32[3,1,512]{2,1,0:T(1,128)} %reshape.254.offset_ref, f32[512,128]{1,0:T(8,128)} %concatenate.47.keep_ref, ...), custom_call_target="tpu_custom_call" | custom-call | flops 1 | bytes 1 | tf_op jit(solution)/shard_map/attention/pallas_call | solution.py:253
  124.5 12.2 %collective-permute-done.11 = bf16[128,2048]{1,0:T(8,128)(2,1)S(1)} collective-permute-done((bf16[128,2048]{1,0:T(8,128)(2,1)S(1)}, bf16[128,2048]{1,0:T(8,128)(2,1)S(1)}, u32[]{:S(2)}, u32[]{:S(2)}) %collective-permute-start.11) | collective-permute-done | bytes 524320 | tf_op jit(solution)/shard_map/ppermute | solution.py:94
  136.6 10.8 %collective-permute-done.10 = bf16[128,2048]{1,0:T(8,128)(2,1)S(1)} collective-permute-done((bf16[128,2048]{1,0:T(8,128)(2,1)S(1)}, bf16[128,2048]{1,0:T(8,128)(2,1)S(1)}, u32[]{:S(2)}, u32[]{:S(2)}) %collective-permute-start.10) | collective-permute-done | bytes 524320 | tf_op jit(solution)/shard_map/ppermute | solution.py:94
  152.1 12.2 %collective-permute-done.14 = bf16[128,2048]{1,0:T(8,128)(2,1)S(1)} collective-permute-done((bf16[128,2048]{1,0:T(8,128)(2,1)S(1)}, bf16[128,2048]{1,0:T(8,128)(2,1)S(1)}, u32[]{:S(2)}, u32[]{:S(2)}) %collective-permute-start.14) | collective-permute-done | bytes 524320 | tf_op jit(solution)/shard_map/ppermute | solution.py:94
  164.3 10.4 %collective-permute-done.13 = bf16[128,2048]{1,0:T(8,128)(2,1)S(1)} collective-permute-done((bf16[128,2048]{1,0:T(8,128)(2,1)S(1)}, bf16[128,2048]{1,0:T(8,128)(2,1)S(1)}, u32[]{:S(2)}, u32[]{:S(2)}) %collective-permute-start.13) | collective-permute-done | bytes 524320 | tf_op jit(solution)/shard_map/ppermute | solution.py:94
  176.3 21.0 %feed_forward.2 = (bf16[512,1920]{1,0:T(8,128)(2,1)}, bf16[512,2048]{1,0:T(8,128)(2,1)}, bf16[512,2048]{1,0:T(8,128)(2,1)}) custom-call(bf16[512,2048]{1,0:T(8,128)(2,1)} %pad_maximum_fusion.1.rows_ref.second_ref, bf16[512,2048]{1,0:T(8,128)(2,1)} %copy-done.1, bf16[2048,1920]{1,0:T(8,128)(2,1)} %all-gather.6.cloned.1.call-done.full_ref), custom_call_target="tpu_custom_call" | custom-call | flops 1 | bytes 1 | tf_op jit(solution)/shard_map/feed_forward/pallas_call | solution.py:401
  204.7 9.2 %weight_terms.4 = (bf16[256,1920]{1,0:T(8,128)(2,1)}, bf16[256,1920]{1,0:T(8,128)(2,1)}, bf16[256,1920]{1,0:T(8,128)(2,1)}, bf16[256,1920]{1,0:T(8,128)(2,1)}) custom-call(bf16[1024,512]{1,0:T(8,128)(2,1)} %get-tuple-element.346.refs_0_, bf16[1024,512]{1,0:T(8,128)(2,1)} %copy-done.61, bf16[1024,512]{1,0:T(8,128)(2,1)} %get-tuple-element.183.refs_2_, ...), custom_call_target="tpu_custom_call" | custom-call | flops 4026531840 | bytes 12058624 | tf_op jit(solution)/shard_map/weight_terms/pallas_call | solution.py:459
  218.2 64.2 %all-gather.8.cloned.1.call-done.full_ref = bf16[2048,2304]{1,0:T(8,128)(2,1)} async-done(((bf16[256,2304]{1,0:T(8,128)(2,1)}), bf16[2048,2304]{1,0:T(8,128)(2,1)}) %all-gather.8.cloned.1.call-update) | async-done | bytes 9437200 | tf_op jit(solution)/shard_map/all_gather | solution.py:627
  282.4 22.1 %feed_forward.3 = (bf16[512,2304]{1,0:T(8,128)(2,1)}, bf16[512,2048]{1,0:T(8,128)(2,1)}, bf16[512,2048]{1,0:T(8,128)(2,1)}) custom-call(bf16[512,2048]{1,0:T(8,128)(2,1)} %pad_maximum_fusion.1.rows_ref.second_ref, bf16[512,2048]{1,0:T(8,128)(2,1)} %copy-done.1, bf16[2048,2304]{1,0:T(8,128)(2,1)} %all-gather.8.cloned.1.call-done.full_ref), custom_call_target="tpu_custom_call" | custom-call | flops 1 | bytes 1 | tf_op jit(solution)/shard_map/feed_forward/pallas_call | solution.py:401
  310.3 6.3 collective-permute-start.19
  326.6 7.3 %collective-permute-done.22 = bf16[128,2048]{1,0:T(8,128)(2,1)S(1)} collective-permute-done((bf16[128,2048]{1,0:T(8,128)(2,1)S(1)}, bf16[128,2048]{1,0:T(8,128)(2,1)S(1)}, u32[]{:S(2)}, u32[]{:S(2)}) %collective-permute-start.22) | collective-permute-done | bytes 524320 | tf_op jit(solution)/shard_map/ppermute | solution.py:94
  336.6 9.4 %weight_terms.5 = (bf16[256,2304]{1,0:T(8,128)(2,1)}, bf16[256,2304]{1,0:T(8,128)(2,1)}, bf16[256,2304]{1,0:T(8,128)(2,1)}, bf16[256,2304]{1,0:T(8,128)(2,1)}) custom-call(bf16[1024,512]{1,0:T(8,128)(2,1)} %get-tuple-element.346.refs_0_, bf16[1024,512]{1,0:T(8,128)(2,1)} %copy-done.61, bf16[1024,512]{1,0:T(8,128)(2,1)} %get-tuple-element.183.refs_2_, ...), custom_call_target="tpu_custom_call" | custom-call | flops 4831838208 | bytes 13631488 | tf_op jit(solution)/shard_map/weight_terms/pallas_call | solution.py:459
  351.9 6.0 collective-permute-start.27
  363.7 9.8 %collective-permute-done.30 = bf16[128,2048]{1,0:T(8,128)(2,1)S(1)} collective-permute-done((bf16[128,2048]{1,0:T(8,128)(2,1)S(1)}, bf16[128,2048]{1,0:T(8,128)(2,1)S(1)}, u32[]{:S(2)}, u32[]{:S(2)}) %collective-permute-start.30) | collective-permute-done | bytes 524320 | tf_op jit(solution)/shard_map/ppermute | solution.py:94
  375.2 12.2 %collective-permute-done.29 = bf16[128,2048]{1,0:T(8,128)(2,1)S(1)} collective-permute-done((bf16[128,2048]{1,0:T(8,128)(2,1)S(1)}, bf16[128,2048]{1,0:T(8,128)(2,1)S(1)}, u32[]{:S(2)}, u32[]{:S(2)}) %collective-permute-start.29) | collective-permute-done | bytes 524320 | tf_op jit(solution)/shard_map/ppermute | solution.py:94
  387.6 14.6 %collective-permute-done.25.refs_1_ = bf16[256,1920]{1,0:T(8,128)(2,1)S(1)} collective-permute-done((bf16[256,1920]{1,0:T(8,128)(2,1)S(1)}, bf16[256,1920]{1,0:T(8,128)(2,1)S(1)}, u32[]{:S(2)}, u32[]{:S(2)}) %collective-permute-start.25) | collective-permute-done | bytes 983072 | tf_op jit(solution)/shard_map/ppermute | solution.py:87
  404.2 5.4 collective-permute-start.32
  413.4 14.9 %attention_back.1.refs_4_ = bf16[512,1536]{1,0:T(8,128)(2,1)} custom-call(bf16[512,2048]{1,0:T(8,128)(2,1)} %copy-done.3, bf16[4,2048,512]{2,1,0:T(8,128)(2,1)} %all-gather.4.cloned.1.call-done.weight_ref.exit_ref, bf16[512,1536]{1,0:T(8,128)(2,1)} %get-tuple-element.232.mixed_ref, f32[512,128]{1,0:T(8,128)} %get-tuple-element.233.totals_ref, ...), custom_call_target="tpu_custom_call" | custom-call | flops 1 | bytes 1 | tf_op jit(solution)/shard_map/attention_back/pallas_call | solution.py:329
  437.7 8.0 %weight_terms.7 = (bf16[256,1536]{1,0:T(8,128)(2,1)}, bf16[256,1536]{1,0:T(8,128)(2,1)}, bf16[256,1536]{1,0:T(8,128)(2,1)}, bf16[256,1536]{1,0:T(8,128)(2,1)}) custom-call(bf16[1024,512]{1,0:T(8,128)(2,1)} %get-tuple-element.248.refs_0_.refs_2_, bf16[1024,512]{1,0:T(8,128)(2,1)} %collective-permute-done.6.refs_1_.refs_3_, ...), custom_call_target="tpu_custom_call" | custom-call | flops 3221225472 | bytes 10485760 | tf_op jit(solution)/shard_map/weight_terms/pallas_call | solution.py:459
  457.4 6.1 collective-permute-start.37
  472.7 5.5 collective-permute-start.40
  487.2 8.3 %collective-permute-done.35.refs_4_ = bf16[256,2304]{1,0:T(8,128)(2,1)} collective-permute-done((bf16[256,2304]{1,0:T(8,128)(2,1)}, bf16[256,2304]{1,0:T(8,128)(2,1)}, u32[]{:S(2)}, u32[]{:S(2)}) %collective-permute-start.35) | collective-permute-done | bytes 1179680 | tf_op jit(solution)/shard_map/ppermute | solution.py:87
  499.2 11.7 %collective-permute-done.40 = bf16[256,1536]{1,0:T(8,128)(2,1)} collective-permute-done((bf16[256,1536]{1,0:T(8,128)(2,1)S(1)}, bf16[256,1536]{1,0:T(8,128)(2,1)}, u32[]{:S(2)}, u32[]{:S(2)}) %collective-permute-start.40) | collective-permute-done | bytes 786464 | tf_op jit(solution)/shard_map/ppermute | solution.py:87
  513.7 5.4 collective-permute-start.47
  529.7 9.5 %collective-permute-start.45 = (bf16[256,512]{1,0:T(8,128)(2,1)S(1)}, bf16[256,512]{1,0:T(8,128)(2,1)S(1)}, u32[]{:S(2)}, u32[]{:S(2)}) collective-permute-start(bf16[256,512]{1,0:T(8,128)(2,1)S(1)} %get-tuple-element.361), channel_id=1, source_target_pairs={{0,8},{4,12},{8,16},{12,20},{1,9},{5,13},{9,17},{13,21},{2,10},{6,... | collective-permute-start | bytes 786440 | tf_op jit(solution)/shard_map/ppermute | solution.py:87
  540.7 25.1 %feed_step.1 = (f32[256,2,1408]{2,1,0:T(2,128)}, f32[256,2,1408]{2,1,0:T(2,128)}, f32[256,2,1408]{2,1,0:T(2,128)}, f32[256,2,1408]{2,1,0:T(2,128)}, f32[256,1408...) custom-call(bf16[256,1920]{1,0:T(8,128)(2,1)} %get-tuple-element.273.refs_0_, ...), custom_call_target="tpu_custom_call" | custom-call | flops 1 | bytes 1 | tf_op jit(solution)/shard_map/feed_step/pallas_call | solution.py:533
  602.0 9.5 %collective-permute-done.55 = bf16[128,2048]{1,0:T(8,128)(2,1)S(1)} collective-permute-done((bf16[128,2048]{1,0:T(8,128)(2,1)}, bf16[128,2048]{1,0:T(8,128)(2,1)S(1)}, u32[]{:S(2)}, u32[]{:S(2)}) %collective-permute-start.55) | collective-permute-done | bytes 524320 | tf_op jit(solution)/shard_map/ppermute | solution.py:94
  615.0 7.6 %plain_step.2 = (f32[3,256,512]{2,1,0:T(8,128)}, f32[3,256,512]{2,1,0:T(8,128)}, f32[3,256,512]{2,1,0:T(8,128)}, f32[3,256,512]{2,1,0:T(8,128)}) custom-call(bf16[256,1536]{1,0:T(8,128)(2,1)} %get-tuple-element.286.own, bf16[256,1536]{1,0:T(8,128)(2,1)} %copy-done.33, bf16[256,1536]{1,0:T(8,128)(2,1)} %copy-done.34, f32[3,256,512]{2,1,0:T(8,128)} %bitcast.58, ...), custom_call_target="tpu_custom_call" | custom-call | flops 1 | bytes 1 | tf_op jit(solution)/shard_map/plain_step/pallas_call | solution.py:491
  (351 shorter events, 209.2 us)
Async XLA Ops:
  7.2 94.5 %all-gather.4.cloned.1.call-start = ((), (), s32[]{:S(2)}) async-start(), calls=%async_computation | async-start | bytes 9437184 | tf_op jit(solution)/shard_map/all_gather | solution.py:615
  10.9 165.3 %all-gather.6.cloned.1.call-start = ((), (), s32[]{:S(2)}) async-start(), calls=%async_computation.1 | async-start | bytes 8847360 | tf_op jit(solution)/shard_map/all_gather | solution.py:627
  23.9 258.5 %all-gather.8.cloned.1.call-start = ((), (), s32[]{:S(2)}) async-start(), calls=%async_computation.2 | async-start | bytes 10616832 | tf_op jit(solution)/shard_map/all_gather | solution.py:627
  35.7 23.5 %collective-permute-start = (bf16[128,2048]{1,0:T(8,128)(2,1)S(1)}, bf16[128,2048]{1,0:T(8,128)(2,1)}, u32[]{:S(2)}, u32[]{:S(2)}) collective-permute-start(bf16[128,2048]{1,0:T(8,128)(2,1)S(1)} %fusion.17), channel_id=1, source_target_pairs={{0,1},{1,0},{2,3},{3,2},{4,5},{5,4},{6,7},{7,6},{8,9},{9,8},{10,11... | collective-permute-start | bytes 1572872 | tf_op jit(solution)/shard_map/ppermute | solution.py:94
  63.1 25.1 %collective-permute-start.4 = (bf16[128,2048]{1,0:T(8,128)(2,1)S(1)}, bf16[128,2048]{1,0:T(8,128)(2,1)}, u32[]{:S(2)}, u32[]{:S(2)}) collective-permute-start(bf16[128,2048]{1,0:T(8,128)(2,1)S(1)} %copy-done.18), channel_id=1, source_target_pairs={{0,2},{1,3},{2,0},{3,1},{4,6},{5,7},{6,4},{7,5},{8,10},{9,11},{10,... | collective-permute-start | bytes 1572872 | tf_op jit(solution)/shard_map/ppermute | solution.py:94
  64.0 25.3 %collective-permute-start.5 = (bf16[128,2048]{1,0:T(8,128)(2,1)S(1)}, bf16[128,2048]{1,0:T(8,128)(2,1)S(1)}, u32[]{:S(2)}, u32[]{:S(2)}) collective-permute-start(bf16[128,2048]{1,0:T(8,128)(2,1)S(1)} %copy-done.18), channel_id=1, source_target_pairs={{0,3},{1,2},{2,1},{3,0},{4,7},{5,6},{6,5},{7,4},{8,11},{9,10},{10,... | collective-permute-start | bytes 1572872 | tf_op jit(solution)/shard_map/ppermute | solution.py:94
  122.1 25.3 %collective-permute-start.10 = (bf16[128,2048]{1,0:T(8,128)(2,1)S(1)}, bf16[128,2048]{1,0:T(8,128)(2,1)S(1)}, u32[]{:S(2)}, u32[]{:S(2)}) collective-permute-start(bf16[128,2048]{1,0:T(8,128)(2,1)S(1)} %get-tuple-element.349), channel_id=1, source_target_pairs={{0,2},{1,3},{2,0},{3,1},{4,6},{5,7},{6,4},{7,5},{8,10},{9,11},{10,... | collective-permute-start | bytes 1572872 | tf_op jit(solution)/shard_map/ppermute | solution.py:94
  122.6 24.8 %collective-permute-start.9 = (bf16[128,2048]{1,0:T(8,128)(2,1)S(1)}, bf16[128,2048]{1,0:T(8,128)(2,1)S(1)}, u32[]{:S(2)}, u32[]{:S(2)}) collective-permute-start(bf16[128,2048]{1,0:T(8,128)(2,1)S(1)} %get-tuple-element.347), channel_id=1, source_target_pairs={{0,1},{1,0},{2,3},{3,2},{4,5},{5,4},{6,7},{7,6},{8,9},{9,8},{10,11... | collective-permute-start | bytes 1572872 | tf_op jit(solution)/shard_map/ppermute | solution.py:94
  149.8 24.9 %collective-permute-start.13 = (bf16[128,2048]{1,0:T(8,128)(2,1)S(1)}, bf16[128,2048]{1,0:T(8,128)(2,1)S(1)}, u32[]{:S(2)}, u32[]{:S(2)}) collective-permute-start(bf16[128,2048]{1,0:T(8,128)(2,1)S(1)} %add_convert_fusion.4), channel_id=1, source_target_pairs={{0,2},{1,3},{2,0},{3,1},{4,6},{5,7},{6,4},{7,5},{8,10},{9,11},{10,... | collective-permute-start | bytes 1572872 | tf_op jit(solution)/shard_map/ppermute | solution.py:94
  150.4 24.3 %collective-permute-start.12 = (bf16[128,2048]{1,0:T(8,128)(2,1)S(1)}, bf16[128,2048]{1,0:T(8,128)(2,1)S(1)}, u32[]{:S(2)}, u32[]{:S(2)}) collective-permute-start(bf16[128,2048]{1,0:T(8,128)(2,1)S(1)} %add_convert_fusion.4), channel_id=1, source_target_pairs={{0,1},{1,0},{2,3},{3,2},{4,5},{5,4},{6,7},{7,6},{8,9},{9,8},{10,11... | collective-permute-start | bytes 1572872 | tf_op jit(solution)/shard_map/ppermute | solution.py:94
  214.0 68.4 %collective-permute-start.17 = (bf16[256,1920]{1,0:T(8,128)(2,1)}, bf16[256,1920]{1,0:T(8,128)(2,1)S(1)}, u32[]{:S(2)}, u32[]{:S(2)}) collective-permute-start(bf16[256,1920]{1,0:T(8,128)(2,1)} %get-tuple-element.214), channel_id=1, source_target_pairs={{0,8},{4,12},{1,9},{5,13},{2,10},{6,14},{3,11},{7,15}} | collective-permute-start | bytes 2949128 | tf_op jit(solution)/shard_map/ppermute | solution.py:87
  217.5 64.9 %collective-permute-start.18 = (bf16[256,1920]{1,0:T(8,128)(2,1)}, bf16[256,1920]{1,0:T(8,128)(2,1)S(1)}, u32[]{:S(2)}, u32[]{:S(2)}) collective-permute-start(bf16[256,1920]{1,0:T(8,128)(2,1)} %get-tuple-element.212), channel_id=1, source_target_pairs={{24,16},{28,20},{25,17},{29,21},{26,18},{30,22},{27,19},{31,23}} | collective-permute-start | bytes 2949128 | tf_op jit(solution)/shard_map/ppermute | solution.py:88
  307.1 29.4 %collective-permute-start.24 = (bf16[512,2304]{1,0:T(8,128)(2,1)S(1)}, bf16[512,2304]{1,0:T(8,128)(2,1)}, u32[]{:S(2)}, u32[]{:S(2)}) collective-permute-start(bf16[512,2304]{1,0:T(8,128)(2,1)S(1)} %copy-done.59), channel_id=1, source_target_pairs={{0,4},{4,0},{8,12},{12,8},{16,20},{20,16},{24,28},{28,24},{1,5},{5... | collective-permute-start | bytes 7077896 | tf_op jit(solution)/shard_map/ppermute | solution.py:81
  310.3 35.7 %collective-permute-start.19 = (bf16[256,1920]{1,0:T(8,128)(2,1)S(1)}, bf16[256,1920]{1,0:T(8,128)(2,1)S(1)}, u32[]{:S(2)}, u32[]{:S(2)}) collective-permute-start(bf16[256,1920]{1,0:T(8,128)(2,1)S(1)} %get-tuple-element.357), channel_id=1, source_target_pairs={{0,8},{4,12},{8,16},{12,20},{1,9},{5,13},{9,17},{13,21},{2,10},{6,... | collective-permute-start | bytes 2949128 | tf_op jit(solution)/shard_map/ppermute | solution.py:87
  316.5 29.5 %collective-permute-start.20 = (bf16[256,1920]{1,0:T(8,128)(2,1)S(1)}, bf16[256,1920]{1,0:T(8,128)(2,1)S(1)}, u32[]{:S(2)}, u32[]{:S(2)}) collective-permute-start(bf16[256,1920]{1,0:T(8,128)(2,1)S(1)} %get-tuple-element.356), channel_id=1, source_target_pairs={{16,8},{20,12},{24,16},{28,20},{17,9},{21,13},{25,17},{29,21},{18,... | collective-permute-start | bytes 2949128 | tf_op jit(solution)/shard_map/ppermute | solution.py:88
  351.9 50.2 %collective-permute-start.27 = (bf16[256,2304]{1,0:T(8,128)(2,1)S(1)}, bf16[256,2304]{1,0:T(8,128)(2,1)S(1)}, u32[]{:S(2)}, u32[]{:S(2)}) collective-permute-start(bf16[256,2304]{1,0:T(8,128)(2,1)S(1)} %copy-done.20), channel_id=1, source_target_pairs={{0,8},{4,12},{1,9},{5,13},{2,10},{6,14},{3,11},{7,15}} | collective-permute-start | bytes 3538952 | tf_op jit(solution)/shard_map/ppermute | solution.py:87
  357.9 44.3 %collective-permute-start.28 = (bf16[256,2304]{1,0:T(8,128)(2,1)S(1)}, bf16[256,2304]{1,0:T(8,128)(2,1)S(1)}, u32[]{:S(2)}, u32[]{:S(2)}) collective-permute-start(bf16[256,2304]{1,0:T(8,128)(2,1)S(1)} %copy-done.21), channel_id=1, source_target_pairs={{24,16},{28,20},{25,17},{29,21},{26,18},{30,22},{27,19},{31,23}} | collective-permute-start | bytes 3538952 | tf_op jit(solution)/shard_map/ppermute | solution.py:88
  360.1 42.1 %collective-permute-start.25 = (bf16[256,1920]{1,0:T(8,128)(2,1)S(1)}, bf16[256,1920]{1,0:T(8,128)(2,1)S(1)}, u32[]{:S(2)}, u32[]{:S(2)}) collective-permute-start(bf16[256,1920]{1,0:T(8,128)(2,1)S(1)} %add.380), channel_id=1, source_target_pairs={{0,8},{4,12},{8,16},{12,20},{16,24},{20,28},{1,9},{5,13},{9,17},{1... | collective-permute-start | bytes 2949128 | tf_op jit(solution)/shard_map/ppermute | solution.py:87
  362.4 39.8 %collective-permute-start.26 = (bf16[256,1920]{1,0:T(8,128)(2,1)S(1)}, bf16[256,1920]{1,0:T(8,128)(2,1)S(1)}, u32[]{:S(2)}, u32[]{:S(2)}) collective-permute-start(bf16[256,1920]{1,0:T(8,128)(2,1)S(1)} %add.381), channel_id=1, source_target_pairs={{8,0},{12,4},{16,8},{20,12},{24,16},{28,20},{9,1},{13,5},{17,9},{2... | collective-permute-start | bytes 2949128 | tf_op jit(solution)/shard_map/ppermute | solution.py:88
  404.2 29.7 %collective-permute-start.32 = (bf16[256,2304]{1,0:T(8,128)(2,1)}, bf16[256,2304]{1,0:T(8,128)(2,1)}, u32[]{:S(2)}, u32[]{:S(2)}) collective-permute-start(bf16[256,2304]{1,0:T(8,128)(2,1)} %get-tuple-element.355), channel_id=1, source_target_pairs={{0,8},{4,12},{8,16},{12,20},{1,9},{5,13},{9,17},{13,21},{2,10},{6,... | collective-permute-start | bytes 3538952 | tf_op jit(solution)/shard_map/ppermute | solution.py:87
  409.6 24.3 %collective-permute-start.33 = (bf16[256,2304]{1,0:T(8,128)(2,1)}, bf16[256,2304]{1,0:T(8,128)(2,1)S(1)}, u32[]{:S(2)}, u32[]{:S(2)}) collective-permute-start(bf16[256,2304]{1,0:T(8,128)(2,1)} %get-tuple-element.354), channel_id=1, source_target_pairs={{16,8},{20,12},{24,16},{28,20},{17,9},{21,13},{25,17},{29,21},{18,... | collective-permute-start | bytes 3538952 | tf_op jit(solution)/shard_map/ppermute | solution.py:88
  457.0 25.0 %collective-permute-start.43 = (bf16[128,2048]{1,0:T(8,128)(2,1)S(1)}, bf16[128,2048]{1,0:T(8,128)(2,1)}, u32[]{:S(2)}, u32[]{:S(2)}) collective-permute-start(bf16[128,2048]{1,0:T(8,128)(2,1)S(1)} %get-tuple-element.339), channel_id=1, source_target_pairs={{0,2},{1,3},{2,0},{3,1},{4,6},{5,7},{6,4},{7,5},{8,10},{9,11},{10,... | collective-permute-start | bytes 1572872 | tf_op jit(solution)/shard_map/ppermute | solution.py:94
  466.0 29.4 %collective-permute-start.35 = (bf16[256,2304]{1,0:T(8,128)(2,1)}, bf16[256,2304]{1,0:T(8,128)(2,1)}, u32[]{:S(2)}, u32[]{:S(2)}) collective-permute-start(bf16[256,2304]{1,0:T(8,128)(2,1)} %add.385), channel_id=1, source_target_pairs={{0,8},{4,12},{8,16},{12,20},{16,24},{20,28},{1,9},{5,13},{9,17},{1... | collective-permute-start | bytes 3538952 | tf_op jit(solution)/shard_map/ppermute | solution.py:87
  469.8 29.4 %collective-permute-start.36 = (bf16[256,2304]{1,0:T(8,128)(2,1)}, bf16[256,2304]{1,0:T(8,128)(2,1)}, u32[]{:S(2)}, u32[]{:S(2)}) collective-permute-start(bf16[256,2304]{1,0:T(8,128)(2,1)} %add.386), channel_id=1, source_target_pairs={{8,0},{12,4},{16,8},{20,12},{24,16},{28,20},{9,1},{13,5},{17,9},{2... | collective-permute-start | bytes 3538952 | tf_op jit(solution)/shard_map/ppermute | solution.py:88
  472.7 38.2 %collective-permute-start.40 = (bf16[256,1536]{1,0:T(8,128)(2,1)S(1)}, bf16[256,1536]{1,0:T(8,128)(2,1)}, u32[]{:S(2)}, u32[]{:S(2)}) collective-permute-start(bf16[256,1536]{1,0:T(8,128)(2,1)S(1)} %copy-done.35), channel_id=1, source_target_pairs={{0,8},{4,12},{1,9},{5,13},{2,10},{6,14},{3,11},{7,15}} | collective-permute-start | bytes 2359304 | tf_op jit(solution)/shard_map/ppermute | solution.py:87
  482.0 28.9 %collective-permute-start.41 = (bf16[256,1536]{1,0:T(8,128)(2,1)}, bf16[256,1536]{1,0:T(8,128)(2,1)}, u32[]{:S(2)}, u32[]{:S(2)}) collective-permute-start(bf16[256,1536]{1,0:T(8,128)(2,1)} %get-tuple-element.287), channel_id=1, source_target_pairs={{24,16},{28,20},{25,17},{29,21},{26,18},{30,22},{27,19},{31,23}} | collective-permute-start | bytes 2359304 | tf_op jit(solution)/shard_map/ppermute | solution.py:88
  513.7 52.1 %collective-permute-start.47 = (bf16[256,1536]{1,0:T(8,128)(2,1)}, bf16[256,1536]{1,0:T(8,128)(2,1)}, u32[]{:S(2)}, u32[]{:S(2)}) collective-permute-start(bf16[256,1536]{1,0:T(8,128)(2,1)} %get-tuple-element.359), channel_id=1, source_target_pairs={{0,8},{4,12},{8,16},{12,20},{1,9},{5,13},{9,17},{13,21},{2,10},{6,... | collective-permute-start | bytes 2359304 | tf_op jit(solution)/shard_map/ppermute | solution.py:87
  519.1 46.8 %collective-permute-start.48 = (bf16[256,1536]{1,0:T(8,128)(2,1)}, bf16[256,1536]{1,0:T(8,128)(2,1)}, u32[]{:S(2)}, u32[]{:S(2)}) collective-permute-start(bf16[256,1536]{1,0:T(8,128)(2,1)} %get-tuple-element.358), channel_id=1, source_target_pairs={{16,8},{20,12},{24,16},{28,20},{17,9},{21,13},{25,17},{29,21},{18,... | collective-permute-start | bytes 2359304 | tf_op jit(solution)/shard_map/ppermute | solution.py:88
  529.7 36.2 %collective-permute-start.45 = (bf16[256,512]{1,0:T(8,128)(2,1)S(1)}, bf16[256,512]{1,0:T(8,128)(2,1)S(1)}, u32[]{:S(2)}, u32[]{:S(2)}) collective-permute-start(bf16[256,512]{1,0:T(8,128)(2,1)S(1)} %get-tuple-element.361), channel_id=1, source_target_pairs={{0,8},{4,12},{8,16},{12,20},{1,9},{5,13},{9,17},{13,21},{2,10},{6,... | collective-permute-start | bytes 786440 | tf_op jit(solution)/shard_map/ppermute | solution.py:87
  539.2 26.7 %collective-permute-start.46 = (bf16[256,512]{1,0:T(8,128)(2,1)S(1)}, bf16[256,512]{1,0:T(8,128)(2,1)S(1)}, u32[]{:S(2)}, u32[]{:S(2)}) collective-permute-start(bf16[256,512]{1,0:T(8,128)(2,1)S(1)} %get-tuple-element.360), channel_id=1, source_target_pairs={{16,8},{20,12},{24,16},{28,20},{17,9},{21,13},{25,17},{29,21},{18,... | collective-permute-start | bytes 786440 | tf_op jit(solution)/shard_map/ppermute | solution.py:88
  539.9 25.9 %collective-permute-start.51 = (f32[7,2048]{1,0:T(8,128)S(1)}, f32[7,2048]{1,0:T(8,128)S(1)}, u32[]{:S(2)}, u32[]{:S(2)}) collective-permute-start(f32[7,2048]{1,0:T(8,128)S(1)} %add.397), channel_id=1, source_target_pairs={{0,4},{4,0},{8,12},{12,8},{16,20},{20,16},{24,28},{28,24},{1,5},{5... | collective-permute-start | bytes 172040 | tf_op jit(solution)/shard_map/ppermute | solution.py:125
  587.4 24.1 %collective-permute-start.55 = (bf16[128,2048]{1,0:T(8,128)(2,1)}, bf16[128,2048]{1,0:T(8,128)(2,1)S(1)}, u32[]{:S(2)}, u32[]{:S(2)}) collective-permute-start(bf16[128,2048]{1,0:T(8,128)(2,1)} %get-tuple-element.336), channel_id=1, source_target_pairs={{0,2},{1,3},{2,0},{3,1},{4,6},{5,7},{6,4},{7,5},{8,10},{9,11},{10,... | collective-permute-start | bytes 1572872 | tf_op jit(solution)/shard_map/ppermute | solution.py:94
  (96 other events, 1660.2 us)
Sparse Core Ops, SparseCore 0:
  11.0 84.7 all-gather.3
  98.1 77.2 all-gather.5
  177.6 104.7 all-gather.7

commit v3 on v2

--- a/solution.py
+++ b/solution.py
@@ -81,6 +81,65 @@
     return lax.ppermute(array, "dp", [(d, d ^ 1) for d in range(count)])
 
 
+def gather_step(ups, downs, s, lines):
+    up = lax.ppermute(ups[-1], "dp", pairs_up(lines, s - 1, lines - 1, 1))
+    down = lax.ppermute(downs[-1], "dp", pairs_up(lines, 1, lines - s + 1, -1))
+    return ups + [up], downs + [down]
+
+
+def gather_from(way, low, high, lines):
+    for s in range(low, high):
+        way = gather_step(*way, s, lines)
+    return way
+
+
+def pack_kernel(lines, place_ref, *refs):
+    pieces, out = refs[:-1], refs[-1]
+    place = place_ref[0]
+    s = pl.program_id(0)
+    for at in range(lines):
+
+        @pl.when((s == at) & (place >= at))
+        def _():
+            out[...] = pieces[at][...]
+
+        if at > 0:
+
+            @pl.when((s == at) & (place < at))
+            def _():
+                out[...] = pieces[2 * lines - 1 - at][...]
+
+
+def pack(ups, downs, place, lines):
+    rows, columns = ups[0].shape
+    tile = min(128, rows)
+    tiles = rows // tile
+
+    def spec(at, is_up):
+        def index(s, t, place_ref):
+            wanted = (s == at) & ((place_ref[0] >= at) if is_up else (place_ref[0] < at))
+            return (jnp.where(wanted, t, jnp.where(s > at, tiles - 1, 0)), 0)
+
+        return pl.BlockSpec((tile, columns), index)
+
+    return pl.pallas_call(
+        lambda *refs: pack_kernel(lines, *refs),
+        grid_spec=pltpu.PrefetchScalarGridSpec(
+            num_scalar_prefetch=1,
+            grid=(lines, tiles),
+            in_specs=[spec(at, True) for at in range(lines)]
+            + [spec(lines - at, False) for at in range(1, lines)],
+            out_specs=pl.BlockSpec((tile, columns), lambda s, t, place_ref: (s * tiles + t, 0)),
+        ),
+        out_shape=jax.ShapeDtypeStruct((lines * rows, columns), ups[0].dtype),
+        compiler_params=pltpu.CompilerParams(vmem_limit_bytes=40 * 1024 * 1024),
+        cost_estimate=pl.CostEstimate(
+            flops=0, bytes_accessed=4 * lines * rows * columns, transcendentals=0
+        ),
+        name="pack_blocks",
+    )(place.reshape(1).astype(jnp.int32), *ups, *downs[1:])
+
+
 def scatter_step(blocks, up, down, j, lines):
     up_send = blocks[lines - j] if up is None else blocks[lines - j] + up
     down_send = blocks[j] if down is None else blocks[j] + down
@@ -98,12 +157,21 @@
     return jnp.concatenate([own] + [swap_rows(own, r) for r in range(1, parts)], axis=0)
 
 
+def send_rows(partial, parts):
+    rows = partial.shape[0] // parts
+    blocks = [partial[r * rows : (r + 1) * rows] for r in range(parts)]
+    return [blocks[0]] + [swap_rows(blocks[r], r) for r in range(1, parts)]
+
+
+def add_up(terms):
+    total = terms[0].astype(jnp.float32)
+    for term in terms[1:]:
+        total = total + term.astype(jnp.float32)
+    return total
+
+
 def scatter_rows(partial, parts):
-    rows = partial.shape[0] // parts
-    total = partial[:rows].astype(jnp.float32)
-    for r in range(1, parts):
-        total = total + swap_rows(partial[r * rows : (r + 1) * rows], r).astype(jnp.float32)
-    return total
+    return add_up(send_rows(partial, parts))
 
 
 def together_streams(streams, others):
@@ -114,10 +182,7 @@
 
 
 def add_terms(terms):
-    total = terms[0].astype(jnp.float32)
-    for term in terms[1:]:
-        total = total + term.astype(jnp.float32)
-    return total.astype(jnp.bfloat16)
+    return add_up(terms).astype(jnp.bfloat16)
 
 
 def hop(array, axis, bit):
@@ -261,16 +326,22 @@
          jax.ShapeDtypeStruct((rows, 128), f32)],
         [pltpu.VMEM((rows, rows), f32), pltpu.VMEM((rows, rows), f32), pltpu.VMEM((rows, rows), bf16)],
         "attention",
+        24 * rows * width * columns,
+        8 * rows * width,
     )(normed_all, entry_full, offsets.reshape(3, 1, columns), *tables, *marks)
 
 
 def attend_back_kernel(
-    middle_ref, exit_ref, mixed_ref, totals_ref, keep_ref, low_ref, high_ref, column_ref, row_ref,
-    grad_ref, bias_ref, score_ref, prob_grad_ref, prob_ref, score_grad_ref, context_grad_ref,
+    middle_ref, exit_ref, mixed_ref, context_ref, totals_ref, keep_ref, low_ref, high_ref, column_ref,
+    row_ref, kinds_ref, grad_ref, normed_ref, bias_ref, score_ref, prob_grad_ref, prob_ref,
+    score_grad_ref, context_grad_ref, weight_ref, sem,
 ):
     rows = middle_ref.shape[0]
     columns = exit_ref.shape[2]
     step = row_steps(rows)
+    load = pltpu.make_async_copy(kinds_ref.at[pl.ds(0, 3)], weight_ref, sem)
+    load.start()
+    grad_ref[:, 3 * columns :] = context_ref[...]
     context_grad_ref[...] = matmul(middle_ref[...], exit_ref[0]).astype(jnp.bfloat16)
     fill_bias(bias_ref, column_ref, row_ref)
     lane = lax.broadcasted_iota(jnp.int32, (1, 128), 1)
@@ -319,9 +390,20 @@
         return 0
 
     lax.fori_loop(0, columns // 128, pair_body, 0)
-
-
-def attend_back(middle_all, exit_full, mixed, totals, tables, marks):
+    load.wait()
+    width = normed_ref.shape[1]
+    for low in range(0, width, 512):
+        here = slice(low, min(low + 512, width))
+        total = None
+        for k in range(3):
+            term = matmul(
+                grad_ref[:, k * columns : (k + 1) * columns], weight_ref[k, here, :], ((1,), (1,))
+            )
+            total = term if total is None else total + term
+        normed_ref[:, here] = total.astype(jnp.bfloat16)
+
+
+def attend_back(middle_all, exit_full, mixed, context, totals, tables, marks):
     rows, width = middle_all.shape
     columns = exit_full.shape[2]
     bf16, f32 = jnp.bfloat16, jnp.float32
@@ -330,43 +412,63 @@
         attend_back_kernel,
         (1,),
         [whole((rows, width)), pl.BlockSpec((1, width, columns), lambda *_: (3, 0, 0)),
-         whole((rows, 3 * columns)), whole((rows, 128))]
-        + [whole((rows, 128))] * 3 + [whole((rows, 2)), whole((2, rows))],
-        whole((rows, 3 * columns)),
-        jax.ShapeDtypeStruct((rows, 3 * columns), bf16),
+         whole((rows, 3 * columns)), whole((rows, columns)), whole((rows, 128))]
+        + [whole((rows, 128))] * 3 + [whole((rows, 2)), whole((2, rows))]
+        + [pl.BlockSpec(memory_space=pl.ANY)],
+        [whole((rows, 4 * columns)), whole((rows, width))],
+        [jax.ShapeDtypeStruct((rows, 4 * columns), bf16), jax.ShapeDtypeStruct((rows, width), bf16)],
         [pltpu.VMEM(square, f32), pltpu.VMEM(square, f32), pltpu.VMEM(square, f32),
-         pltpu.VMEM(square, bf16), pltpu.VMEM(square, bf16), pltpu.VMEM((rows, columns), bf16)],
+         pltpu.VMEM(square, bf16), pltpu.VMEM(square, bf16), pltpu.VMEM((rows, columns), bf16),
+         pltpu.VMEM((3, width, columns), bf16), pltpu.SemaphoreType.DMA],
         "attention_back",
-    )(middle_all, exit_full, mixed, totals, *tables, *marks)
-
-
-def feed_kernel(
-    second_ref, cot_ref, full_ref, acts_ref, branch_ref, second_grad_ref, weight_ref, hidden_grad_ref, sems
-):
+        24 * rows * width * columns,
+        8 * rows * width,
+    )(middle_all, exit_full, mixed, context, totals, *tables, *marks, exit_full)
+
+
+def feed_kernel(pieces, order_ref, second_in, cot_in, *refs):
+    fulls, refs = refs[:pieces], refs[pieces:]
+    acts_ref, branch_ref, second_grad_ref, weight_ref, hidden_grad_ref, sems = refs[:6]
     j = pl.program_id(0)
-    rows, width = second_ref.shape
+    rows, width = second_in.shape
     padded = acts_ref.shape[1] // 3
     pairs = padded // 128
-    step = row_steps(rows)
+    size = branch_ref.shape[1]
+    height = width // pieces
     bf16 = jnp.bfloat16
-
-    def load(at, size, which):
-        here = pl.ds(at, size)
-        return pltpu.make_async_copy(full_ref.at[:, here], weight_ref.at[:, here], sems.at[which])
+    second_ref, cot_ref = (second_in, cot_in) if pieces == 1 else refs[6:]
+
+    def loads(at, columns, which):
+        here = pl.ds(at, columns)
+        return [
+            pltpu.make_async_copy(
+                full.at[:, here], weight_ref.at[pl.ds(p * height, height), here], sems.at[p, which]
+            )
+            for p, full in enumerate(fulls)
+        ]
 
     @pl.when(j == 0)
     def _():
-        load(2 * padded, padded, 0).start()
+        for load in loads(2 * padded, padded, 0):
+            load.start()
         for p in range(pairs):
-            load(p * 256, 256, p + 1).start()
-        load(2 * padded, padded, 0).wait()
+            for load in loads(p * 256, 256, p + 1):
+                load.start()
+        if pieces > 1:
+            for b in range(width // size):
+                there = pl.ds(pl.multiple_of(order_ref[b] * size, size), size)
+                second_ref[:, b * size : (b + 1) * size] = second_in[:, there]
+                cot_ref[:, b * size : (b + 1) * size] = cot_in[:, there]
+        for load in loads(2 * padded, padded, 0):
+            load.wait()
         for low in range(0, padded, 256):
             high = min(low + 256, padded)
             hidden_grad_ref[:, low:high] = matmul(
                 cot_ref[...], weight_ref[:, 2 * padded + low : 2 * padded + high]
             )
         for p in range(pairs):
-            load(p * 256, 256, p + 1).wait()
+            for load in loads(p * 256, 256, p + 1):
+                load.wait()
             gate_up = matmul(second_ref[...], weight_ref[:, p * 256 : (p + 1) * 256])
             gate, upper = gate_up[:, :128], gate_up[:, 128:]
             grad = hidden_grad_ref[:, p * 128 : (p + 1) * 128]
@@ -381,7 +483,6 @@
 
     @pl.when(j > 0)
     def _():
-        size = branch_ref.shape[1]
         here = pl.ds(pl.multiple_of((j - 1) * size, size), size)
         over = ((1,), (1,))
         second_grad_ref[...] = matmul(
@@ -392,22 +493,38 @@
         ).astype(bf16)
 
 
-def feed(second_all, cot_all, full):
+def feed(second_all, cot_all, fulls, order, size):
     rows, width = second_all.shape
-    padded = full.shape[1] // 3
-    chunk = 256
+    padded = fulls[0].shape[1] // 3
+    pieces = len(fulls)
     bf16, f32 = jnp.bfloat16, jnp.float32
-    out = pl.BlockSpec((rows, chunk), lambda j: (0, jnp.maximum(j - 1, 0)))
-    return kernel_call(
-        feed_kernel,
-        (1 + width // chunk,),
-        [whole((rows, width))] * 2 + [pl.BlockSpec(memory_space=pl.ANY)],
-        [whole((rows, 3 * padded)), out, out],
-        [jax.ShapeDtypeStruct((rows, 3 * padded), bf16)] + [jax.ShapeDtypeStruct((rows, width), bf16)] * 2,
-        [pltpu.VMEM((width, 3 * padded), bf16), pltpu.VMEM((rows, padded), f32),
-         pltpu.SemaphoreType.DMA((1 + padded // 128,))],
-        "feed_forward",
-    )(second_all, cot_all, full)
+    full = pl.BlockSpec((rows, width), lambda j, order_ref: (0, 0))
+    out = pl.BlockSpec((rows, size), lambda j, order_ref: (0, order_ref[jnp.maximum(j - 1, 0)]))
+    scratch = [
+        pltpu.VMEM((width, 3 * padded), bf16), pltpu.VMEM((rows, padded), f32),
+        pltpu.SemaphoreType.DMA((pieces, 1 + padded // 128)),
+    ]
+    if pieces > 1:
+        scratch += [pltpu.VMEM((rows, width), bf16)] * 2
+    return pl.pallas_call(
+        lambda *refs: feed_kernel(pieces, *refs),
+        grid_spec=pltpu.PrefetchScalarGridSpec(
+            num_scalar_prefetch=1,
+            grid=(1 + width // size,),
+            in_specs=[full] * 2 + [pl.BlockSpec(memory_space=pl.ANY)] * pieces,
+            out_specs=[pl.BlockSpec((rows, 3 * padded), lambda j, order_ref: (0, 0)), out, out],
+            scratch_shapes=scratch,
+        ),
+        out_shape=[jax.ShapeDtypeStruct((rows, 3 * padded), bf16)]
+        + [jax.ShapeDtypeStruct((rows, width), bf16)] * 2,
+        compiler_params=pltpu.CompilerParams(vmem_limit_bytes=56 * 1024 * 1024),
+        cost_estimate=pl.CostEstimate(
+            flops=24 * rows * width * padded,
+            bytes_accessed=12 * width * padded + 16 * rows * width,
+            transcendentals=0,
+        ),
+        name="feed_forward",
+    )(order, second_all, cot_all, *fulls)
 
 
 def turned_kernel(blocks_ref, rows_ref, out_ref):
@@ -483,10 +600,10 @@
         out[0] = value
 
 
-def plain_step(parts_of_sum, params):
+def plain_step(start, parts_of_sum, params):
     kinds, rows, columns = params[0].shape
     tile = rows // 2
-    part = pl.BlockSpec((tile, columns), lambda k, r: (r, k))
+    part = pl.BlockSpec((tile, columns), lambda k, r: (r, start + k))
     block = pl.BlockSpec((1, tile, columns), lambda k, r: (k, r, 0))
     return kernel_call(
         plain_step_kernel,
@@ -541,6 +658,8 @@
         + [jax.ShapeDtypeStruct((rows, columns), jnp.float32)] * 4,
         [],
         "feed_step",
+        0,
+        84 * rows * columns,
     )(*flat, *gate, *down)
 
 
@@ -620,11 +739,8 @@
         downs = jnp.pad(down_weight[:, a:b].astype(bf16), ((0, 0), (0, -(b - a) % 128)))
         return jnp.concatenate([gates, downs], axis=1)
 
-    fulls = []
-    earlier = kinds_own
-    for a, b in chunks:
-        earlier = after(unit_of(a, b), earlier)
-        fulls.append(lax.all_gather(earlier, "dp", axis=0, tiled=True))
+    unit_a, unit_b = [unit_of(a, b) for a, b in chunks]
+    full_a = lax.all_gather(after(unit_a, kinds_own), "dp", axis=0, tiled=True)
 
     segment, positions = segments(lengths[0], group)
     row_blocks = jnp.arange(parts, dtype=jnp.int32) ^ part_index
@@ -668,74 +784,79 @@
 
     mixed, context, log_totals = attend(normed_all, kinds, offsets, tables, marks)
     branch = dot(context, kinds[3], ((1,), (1,))).astype(bf16)
-    context_other = other_core(context)
-    branch, context_other = together(branch, context_other)
     branch = scatter_rows(branch, parts)
     middle = rows_in + branch
     second, unit_two, factor_two = norm_forward(middle, norm_gains[1], bias_rows[4])
     second_all = gather_rows(second.astype(bf16), parts)
-    second_all, fulls[0] = together(second_all, fulls[0])
-
-    second_sides = both_cores(second_all)
-    streams, branch_terms, second_terms = [], [], []
-    for at, full in enumerate(fulls):
-        streams = advance(streams)
-        acts, branch_term, second_term = feed(second_all, cot_all, fulls[at])
-        branch_terms.append(branch_term)
-        second_terms.append(second_term)
-        if at + 1 < len(fulls):
-            padded = acts.shape[1] // 3
-            terms = weight_terms(
-                second_sides, cot_sides, (acts, other_core(acts)), padded, 2, lines
-            )
-            streams = streams + begin(terms)
-            streams, fulls[at + 1] = together_streams(streams, fulls[at + 1])
-    second_grad = add_terms(second_terms)
-    second_grad, acts = together(second_grad, acts)
+    second_all, full_a, unit_b = together(second_all, full_a, unit_b)
+
+    way_b = gather_from(([unit_b], [unit_b]), 1, 2, lines)
+    natural = jnp.arange(dp_count, dtype=jnp.int32)
+    acts, branch_a, second_a = feed(second_all, cot_all, [full_a], natural, size)
+    acts, branch_a, second_a, way_b = together(acts, branch_a, second_a, way_b)
+
+    way_b = gather_from(way_b, 2, 3, lines)
     acts_other = other_core(acts)
-    second_grad = scatter_rows(second_grad, parts)
-    branch_two = add_terms(branch_terms)
+    second_sides = both_cores(after(second_all, acts))
     padded = acts.shape[1] // 3
     terms = weight_terms(second_sides, cot_sides, (acts, acts_other), padded, 2, lines)
-    streams, (second_grad, terms, branch_two) = together_streams(
-        streams, (second_grad, terms, branch_two)
-    )
-
-    streams = advance(streams) + begin(terms)
+    terms, way_b = together(terms, way_b)
+
+    way_b = gather_from(way_b, 3, lines, lines)
+    streams = begin(terms)
+    streams, way_b = together_streams(streams, way_b)
+
+    streams = advance(streams)
+    half = pack(*way_b, place, lines)
+    order = jnp.stack(own_blocks + other_blocks).astype(jnp.int32)
+    acts, branch_b, second_b = feed(second_all, cot_all, [half, other_core(half)], order, size)
+    streams, (second_b, branch_b, acts) = together_streams(streams, (second_b, branch_b, acts))
+    second_grad = add_terms([second_a, second_b])
+    branch_terms = [branch_a, branch_b]
+    streams, second_grad = together_streams(streams, second_grad)
+
+    streams = advance(streams)
+    acts_other = other_core(acts)
+    arrived = send_rows(second_grad, parts)
+    padded = acts.shape[1] // 3
+    terms = weight_terms(second_sides, cot_sides, (acts, acts_other), padded, 2, lines)
+    streams, (arrived, terms) = together_streams(streams, (arrived, terms))
+
+    second_grad = add_up(arrived)
     middle_grad = cotangent.astype(jnp.float32) + norm_backward(
         second_grad, unit_two, factor_two, norm_gains[1]
     )
-    middle_all = gather_rows(middle_grad.astype(bf16), parts)
+    middle_low = middle_grad.astype(bf16)
+    streams, (middle_low, terms) = together_streams(streams, (middle_low, terms))
+    middle_all = gather_rows(middle_low, parts)
+    streams = advance(streams) + begin(terms)
     streams, middle_all = together_streams(streams, middle_all)
 
     streams = advance(streams)
-    mixed_grad = attend_back(middle_all, kinds, mixed, log_totals, tables, marks)
+    mixed_grad, normed_terms = attend_back(
+        middle_all, kinds, mixed, context, log_totals, tables, marks
+    )
+    streams, (mixed_grad, normed_terms, middle_all) = together_streams(
+        streams, (mixed_grad, normed_terms, middle_all)
+    )
+
+    arrived = send_rows(normed_terms, parts)
+    streams = advance(streams)
+    mixed_other = other_core(mixed_grad)
     middle_sides = both_cores(middle_all)
-    exit_terms = weight_terms(
-        middle_sides, middle_sides, (context, context_other), head_cols, 1, lines
-    )
-    streams, (mixed_grad, exit_terms) = together_streams(streams, (mixed_grad, exit_terms))
-
-    streams = advance(streams) + begin(exit_terms)
     entry_terms = weight_terms(
-        normed_sides, normed_sides, (mixed_grad, other_core(mixed_grad)), head_cols, 3, lines
-    )
-    mixed_grad, entry_terms = together(mixed_grad, entry_terms)
+        normed_sides, middle_sides, (mixed_grad, mixed_other), head_cols, 3, lines
+    )
+    streams, (arrived, entry_terms) = together_streams(streams, (arrived, entry_terms))
+
     streams = streams + begin(entry_terms)
-    normed_grad = sum(
-        dot(mixed_grad[:, k * head_cols : (k + 1) * head_cols], kinds[k], ((1,), (1,)))
-        for k in range(3)
-    )
-    normed_grad = scatter_rows(normed_grad.astype(bf16), parts)
-    streams, normed_grad = together_streams(streams, normed_grad)
-
-    streams = finish(streams[:-2]) + advance(streams[-2:])
+    normed_grad = add_up(arrived)
     input_gradient = middle_grad + norm_backward(normed_grad, unit_one, factor_one, norm_gains[0])
     gain_two_grad = jnp.sum(second_grad * unit_two, axis=0)
     shift_two_grad = jnp.sum(second_grad, axis=0)
     gain_one_grad = jnp.sum(normed_grad * unit_one, axis=0)
     shift_one_grad = jnp.sum(normed_grad, axis=0)
-    column_sums = jnp.sum(mixed_grad.astype(jnp.float32), axis=0).reshape(3, head_cols)
+    column_sums = jnp.sum(mixed_grad[:, : 3 * head_cols].astype(jnp.float32), axis=0).reshape(3, head_cols)
     column_sums = column_sums * jnp.stack([jnp.ones_like(rotmask), rotmask, jnp.ones_like(rotmask)])
     placed = lax.dynamic_update_slice_in_dim(
         jnp.zeros((3, width), jnp.float32), column_sums, column_start, 1
@@ -748,39 +869,41 @@
         bit *= 2
     vectors = hop(vectors, "dp", 1)
 
+    streams, vectors = together_streams(streams, vectors)
+
+    streams = finish(streams[:-1]) + advance(streams[-1:])
+    bit = 2
+    while bit < dp_count:
+        vectors = hop(vectors, "dp", bit)
+        bit *= 2
+    streams, (vectors, branch_terms) = together_streams(streams, (vectors, branch_terms))
+
+    streams = finish(streams)
     (
         gate_gradient, gate_updated, gate_first_new, gate_second_new,
         down_gradient, down_updated, down_first_new, down_second_new,
     ) = feed_step(
         chunks,
-        [parts_of(stream) for stream in streams[:-2]],
+        [parts_of(stream) for stream in streams[:-1]],
         (gate_weight, gate_first, gate_second),
         (down_weight, down_first, down_second),
     )
-    streams, (vectors, gate_updated, down_updated) = together_streams(
-        streams, (vectors, gate_updated, down_updated)
-    )
-
-    bit = 2
-    while bit < dp_count:
-        vectors = hop(vectors, "dp", bit)
-        bit *= 2
-    streams = finish(streams)
-    branch_two = scatter_rows(after(branch_two, vectors), parts)
+    branch_two = scatter_rows(add_terms(branch_terms), parts)
     output_rows = (middle + branch_two).astype(bf16)
     bias_gradient = vectors[:5]
     gains_gradient = vectors[5:]
+    streams, _ = together_streams(streams, gate_updated)
+    kind_first = lambda array: jnp.swapaxes(array, 0, 1)
+    entry_gradient, entry_updated, entry_first_new, entry_second_new = [
+        kind_first(array)
+        for array in plain_step(
+            0, parts_of(streams[-1]), [kind_first(array) for array in (entry_weight, entry_first, entry_second)]
+        )
+    ]
     exit_gradient, exit_updated, exit_first_new, exit_second_new = [
         array[0]
         for array in plain_step(
-            parts_of(streams[-2]), [array[None] for array in (exit_weight, exit_first, exit_second)]
-        )
-    ]
-    entry_gradient, entry_updated, entry_first_new, entry_second_new = [
-        jnp.swapaxes(array, 0, 1)
-        for array in plain_step(
-            parts_of(streams[-1]),
-            [jnp.swapaxes(array, 0, 1) for array in (entry_weight, entry_first, entry_second)],
+            3, parts_of(streams[-1]), [array[None] for array in (exit_weight, exit_first, exit_second)]
         )
     ]
     bias_updated, bias_first_new, bias_second_new = adamw(

time: 634 us -> 577 us (0.910)
  waiting for transfers between devices: 259 us -> 230 us
  starting transfers between devices: 116 us -> 91.9 us
  other arithmetic: 45.2 us -> 35.8 us
  matrix products: 11.8 us -> 3.07 us
  local copies, waits for them, and re-layouts: 33.8 us -> 40.6 us
    all_gather x2 -> x1, waiting for transfers between devices: 64.2 us -> 0.79 us  [on_device(): full_a = lax.all_gather(after(unit_a, kinds_own), 'dp', axis=0, tiled=True)]
    ppermute x0 -> x6, waiting for transfers between devices: none -> 27.9 us  [the longest x3 25 us: gather_step(): down = lax.ppermute(downs[-1], 'dp', pairs_up(lines, 1, lines - s + 1, -1))]
    ppermute x12 -> x9, starting transfers between devices: 58.9 us -> 33.6 us  [scatter_step(): up = lax.ppermute(up_send, 'dp', pairs_up(lines, 0, lines - j, 1))]
    ppermute x5, waiting for transfers between devices: 5.55 us -> 26.8 us  [hop(): lax.ppermute(array, axis, [(i, i ^ bit) for i in range(count)])]
    ppermute x24, waiting for transfers between devices: 144 us -> 131 us  [swap_rows(): lax.ppermute(array, 'tensor', [(t, t ^ offset) for t in range(count)])]
    dot_general x4 -> x1, matrix products: 11.8 us -> 3.07 us  [dot(): lax.dot_general(a, b, (contract, ((), ())), preferred_element_type=jnp.fl...]
    unnamed x131 -> x115, local copies, waits for them, and re-layouts: 11.9 us -> 19.6 us
    ppermute x0 -> x6, starting transfers between devices: none -> 6.67 us  [the longest x3 3.86 us: gather_step(): down = lax.ppermute(downs[-1], 'dp', pairs_up(lines, 1, lines - s + 1, -1))]
  transfers between devices with their start and end apart: 64 -> 63, of which waited for: 28 -> 33; matrix products, arithmetic and copies ran while one was open for 10% -> 9% of each run, Pallas kernels for 17% -> 24%
where the time goes in v3:
time: 577 us; the launch traced here: 566 us
  waiting for transfers between devices  230 us (40%)
  Pallas kernels  150 us (26%)
  starting transfers between devices  91.9 us (16%)
  local copies, waits for them, and re-layouts  40.6 us (7%)
  other arithmetic  35.8 us (6%)
  between operations  15.6 us (3%)
    ppermute x24, waiting for transfers between devices, swap_rows(): lax.ppermute(array, 'tensor', [(t, t ^ offset) for t in range(count)])  131 us
    pallas_call x2, Pallas kernels, feed(): pl.pallas_call(lambda *refs: feed_kernel(pieces, *refs), grid_spec=pltpu....  43.9 us
    ppermute x9, starting transfers between devices, scatter_step(): up = lax.ppermute(up_send, 'dp', pairs_up(lines, 0, lines - j, 1))  33.6 us
    ppermute x9, waiting for transfers between devices, scatter_step(): up = lax.ppermute(up_send, 'dp', pairs_up(lines, 0, lines - j, 1))  32 us
    ppermute x24, starting transfers between devices, swap_rows(): lax.ppermute(array, 'tensor', [(t, t ^ offset) for t in range(count)])  29.3 us
    pallas_call x3, Pallas kernels, weight_terms(): kernel_call(lambda *refs: terms_kernel(split, *refs), (columns // tile,),...  27.8 us
    ppermute x5, waiting for transfers between devices, hop(): lax.ppermute(array, axis, [(i, i ^ bit) for i in range(count)])  26.8 us
    pallas_call x1, Pallas kernels, feed_step(): kernel_call(lambda *refs: feed_step_kernel(runs, *refs), (rows // tile,),...  25.1 us
  transfers between devices with their start and end apart: 63, of which 33 were waited for; matrix products, arithmetic and copies ran while one was open for 9% of the time, Pallas kernels for 24%

profile of v3, /device:TPU:0, one launch (start us, length us, event | category | flops | bytes accessed | tf_op | source)
XLA Modules:
  0.0 566.5 jit_solution(15056825611913834367)
XLA Ops:
  23.2 11.9 %collective-permute-done.2 = bf16[128,2048]{1,0:T(8,128)(2,1)S(1)} collective-permute-done((bf16[128,2048]{1,0:T(8,128)(2,1)S(1)}, bf16[128,2048]{1,0:T(8,128)(2,1)S(1)}, u32[]{:S(2)}, u32[]{:S(2)}) %collective-permute-start.2) | collective-permute-done | bytes 524320 | tf_op jit(solution)/shard_map/ppermute | solution.py:153
  35.1 10.4 %collective-permute-done.1 = bf16[128,2048]{1,0:T(8,128)(2,1)S(1)} collective-permute-done((bf16[128,2048]{1,0:T(8,128)(2,1)S(1)}, bf16[128,2048]{1,0:T(8,128)(2,1)S(1)}, u32[]{:S(2)}, u32[]{:S(2)}) %collective-permute-start.1) | collective-permute-done | bytes 524320 | tf_op jit(solution)/shard_map/ppermute | solution.py:153
  52.9 10.2 %collective-permute-done.3 = bf16[128,2048]{1,0:T(8,128)(2,1)} collective-permute-done((bf16[128,2048]{1,0:T(8,128)(2,1)}, bf16[128,2048]{1,0:T(8,128)(2,1)}, u32[]{:S(2)}, u32[]{:S(2)}) %collective-permute-start.3) | collective-permute-done | bytes 524320 | tf_op jit(solution)/shard_map/ppermute | solution.py:153
  64.2 10.9 %collective-permute-done.4 = bf16[128,2048]{1,0:T(8,128)(2,1)} collective-permute-done((bf16[128,2048]{1,0:T(8,128)(2,1)}, bf16[128,2048]{1,0:T(8,128)(2,1)}, u32[]{:S(2)}, u32[]{:S(2)}) %collective-permute-start.4) | collective-permute-done | bytes 524320 | tf_op jit(solution)/shard_map/ppermute | solution.py:153
  89.2 6.6 %all-gather.3.cloned.1.call-done.weight_ref.exit_ref.kinds_ref = bf16[4,2048,512]{2,1,0:T(8,128)(2,1)} async-done(((bf16[4,256,512]{2,1,0:T(8,128)(2,1)}), bf16[4,2048,512]{2,1,0:T(8,128)(2,1)}) %all-gather.3.cloned.1.call-update) | async-done | bytes 8388624 | tf_op jit(solution)/shard_map/all_gather | solution.py:734
  96.7 15.3 %attention.1 = (bf16[512,1536]{1,0:T(8,128)(2,1)}, bf16[512,512]{1,0:T(8,128)(2,1)}, f32[512,128]{1,0:T(8,128)}) custom-call(bf16[512,2048]{1,0:T(8,128)(2,1)} %copy-done, bf16[4,2048,512]{2,1,0:T(8,128)(2,1)} %all-gather.3.cloned.1.call-done.weight_ref.exit_ref.kinds_ref, f32[3,1,512]{2,1,0:T(1,128)} %reshape.257.offset_ref, ...), custom_call_target="tpu_custom_call" | custom-call | flops 12884901888 | bytes 8388608 | tf_op jit(solution)/shard_map/attention/pallas_call | solution.py:318
  118.8 12.2 %collective-permute-done.10 = bf16[128,2048]{1,0:T(8,128)(2,1)S(1)} collective-permute-done((bf16[128,2048]{1,0:T(8,128)(2,1)S(1)}, bf16[128,2048]{1,0:T(8,128)(2,1)S(1)}, u32[]{:S(2)}, u32[]{:S(2)}) %collective-permute-start.10) | collective-permute-done | bytes 524320 | tf_op jit(solution)/shard_map/ppermute | solution.py:153
  131.0 10.5 %collective-permute-done.9 = bf16[128,2048]{1,0:T(8,128)(2,1)S(1)} collective-permute-done((bf16[128,2048]{1,0:T(8,128)(2,1)S(1)}, bf16[128,2048]{1,0:T(8,128)(2,1)S(1)}, u32[]{:S(2)}, u32[]{:S(2)}) %collective-permute-start.9) | collective-permute-done | bytes 524320 | tf_op jit(solution)/shard_map/ppermute | solution.py:153
  151.6 8.5 %collective-permute-done.13 = bf16[128,2048]{1,0:T(8,128)(2,1)} collective-permute-done((bf16[128,2048]{1,0:T(8,128)(2,1)}, bf16[128,2048]{1,0:T(8,128)(2,1)}, u32[]{:S(2)}, u32[]{:S(2)}) %collective-permute-start.13) | collective-permute-done | bytes 524320 | tf_op jit(solution)/shard_map/ppermute | solution.py:153
  160.1 10.3 %collective-permute-done.12 = bf16[128,2048]{1,0:T(8,128)(2,1)} collective-permute-done((bf16[128,2048]{1,0:T(8,128)(2,1)}, bf16[128,2048]{1,0:T(8,128)(2,1)}, u32[]{:S(2)}, u32[]{:S(2)}) %collective-permute-start.12) | collective-permute-done | bytes 524320 | tf_op jit(solution)/shard_map/ppermute | solution.py:153
  177.5 21.2 %feed_forward.2 = (bf16[512,1920]{1,0:T(8,128)(2,1)}, bf16[512,2048]{1,0:T(8,128)(2,1)}, bf16[512,2048]{1,0:T(8,128)(2,1)}) custom-call(s32[8]{0:T(128)} %iota.35.refs_0_, bf16[512,2048]{1,0:T(8,128)(2,1)} %pad_maximum_fusion.1.refs_1_.rows_ref, bf16[512,2048]{1,0:T(8,128)(2,1)} %copy-done.4, bf16[2048,1920]{1,0:T(8,128)(2,1)} %all-gather.5.cloned.1.call-done.refs_3_), custom_call_target="tpu_custom_call" | custom-call | flops 16106127360 | bytes 32505856 | tf_op jit(solution)/shard_map/feed_forward/pallas_call | solution.py:509
  212.6 9.4 %weight_terms.3 = (bf16[256,1920]{1,0:T(8,128)(2,1)}, bf16[256,1920]{1,0:T(8,128)(2,1)}, bf16[256,1920]{1,0:T(8,128)(2,1)}, bf16[256,1920]{1,0:T(8,128)(2,1)}) custom-call(bf16[1024,512]{1,0:T(8,128)(2,1)} %get-tuple-element.434.refs_0_, bf16[1024,512]{1,0:T(8,128)(2,1)} %copy-done.52, bf16[1024,512]{1,0:T(8,128)(2,1)} %get-tuple-element.232.refs_2_, ...), custom_call_target="tpu_custom_call" | custom-call | flops 4026531840 | bytes 12058624 | tf_op jit(solution)/shard_map/weight_terms/pallas_call | solution.py:576
  222.0 19.1 %collective-permute-done.19.refs_6_ = bf16[256,2304]{1,0:T(8,128)(2,1)S(1)} collective-permute-done((bf16[256,2304]{1,0:T(8,128)(2,1)S(1)}, bf16[256,2304]{1,0:T(8,128)(2,1)S(1)}, u32[]{:S(2)}, u32[]{:S(2)}) %collective-permute-start.19) | collective-permute-done | bytes 1179680 | tf_op jit(solution)/shard_map/ppermute | solution.py:86
  245.2 4.7 collective-permute-start.20
  250.6 19.6 %collective-permute-done.20 = bf16[256,1920]{1,0:T(8,128)(2,1)S(1)} collective-permute-done((bf16[256,1920]{1,0:T(8,128)(2,1)}, bf16[256,1920]{1,0:T(8,128)(2,1)S(1)}, u32[]{:S(2)}, u32[]{:S(2)}) %collective-permute-start.20) | collective-permute-done | bytes 983072 | tf_op jit(solution)/shard_map/ppermute | solution.py:146
  283.2 22.7 %feed_forward.3 = (bf16[512,2304]{1,0:T(8,128)(2,1)}, bf16[512,2048]{1,0:T(8,128)(2,1)}, bf16[512,2048]{1,0:T(8,128)(2,1)}) custom-call(s32[8]{0:T(128)} %copy-done.9, bf16[512,2048]{1,0:T(8,128)(2,1)} %pad_maximum_fusion.1.refs_1_.rows_ref, bf16[512,2048]{1,0:T(8,128)(2,1)} %copy-done.4, bf16[1024,2304]{1,0:T(8,128)(2,1)} %copy-done.3, ...), custom_call_target="tpu_custom_call" | custom-call | flops 19327352832 | bytes 35651584 | tf_op jit(solution)/shard_map/feed_forward/pallas_call | solution.py:509
  319.5 9.4 %weight_terms.4 = (bf16[256,2304]{1,0:T(8,128)(2,1)}, bf16[256,2304]{1,0:T(8,128)(2,1)}, bf16[256,2304]{1,0:T(8,128)(2,1)}, bf16[256,2304]{1,0:T(8,128)(2,1)}) custom-call(bf16[1024,512]{1,0:T(8,128)(2,1)} %get-tuple-element.434.refs_0_, bf16[1024,512]{1,0:T(8,128)(2,1)} %copy-done.52, bf16[1024,512]{1,0:T(8,128)(2,1)} %get-tuple-element.232.refs_2_, ...), custom_call_target="tpu_custom_call" | custom-call | flops 4831838208 | bytes 13631488 | tf_op jit(solution)/shard_map/weight_terms/pallas_call | solution.py:576
  329.6 11.6 %collective-permute-done.30 = bf16[128,2048]{1,0:T(8,128)(2,1)S(1)} collective-permute-done((bf16[128,2048]{1,0:T(8,128)(2,1)}, bf16[128,2048]{1,0:T(8,128)(2,1)S(1)}, u32[]{:S(2)}, u32[]{:S(2)}) %collective-permute-start.30) | collective-permute-done | bytes 524320 | tf_op jit(solution)/shard_map/ppermute | solution.py:153
  345.3 4.5 collective-permute-start.33
  354.1 12.3 %collective-permute-done.37 = bf16[128,2048]{1,0:T(8,128)(2,1)S(1)} collective-permute-done((bf16[128,2048]{1,0:T(8,128)(2,1)S(1)}, bf16[128,2048]{1,0:T(8,128)(2,1)S(1)}, u32[]{:S(2)}, u32[]{:S(2)}) %collective-permute-start.37) | collective-permute-done | bytes 524320 | tf_op jit(solution)/shard_map/ppermute | solution.py:153
  366.3 8.5 %collective-permute-done.36 = bf16[128,2048]{1,0:T(8,128)(2,1)S(1)} collective-permute-done((bf16[128,2048]{1,0:T(8,128)(2,1)S(1)}, bf16[128,2048]{1,0:T(8,128)(2,1)S(1)}, u32[]{:S(2)}, u32[]{:S(2)}) %collective-permute-start.36) | collective-permute-done | bytes 524320 | tf_op jit(solution)/shard_map/ppermute | solution.py:153
  380.5 19.0 %attention_back.1 = (bf16[512,2048]{1,0:T(8,128)(2,1)}, bf16[512,2048]{1,0:T(8,128)(2,1)}) custom-call(bf16[512,2048]{1,0:T(8,128)(2,1)} %pad_maximum_fusion.2.middle_ref.rows_ref, bf16[4,2048,512]{2,1,0:T(8,128)(2,1)} %all-gather.3.cloned.1.call-done.weight_ref.exit_ref.kinds_ref, bf16[512,1536]{1,0:T(8,128)(2,1)} %get-tuple-element.313.mixed_ref, ...), custom_call_target="tpu_custom_call" | custom-call | flops 12884901888 | bytes 8388608 | tf_op jit(solution)/shard_map/attention_back/pallas_call | solution.py:411
  399.5 5.9 %collective-permute-done.38 = bf16[256,2304]{1,0:T(8,128)(2,1)S(1)} collective-permute-done((bf16[256,2304]{1,0:T(8,128)(2,1)}, bf16[256,2304]{1,0:T(8,128)(2,1)S(1)}, u32[]{:S(2)}, u32[]{:S(2)}) %collective-permute-start.38) | collective-permute-done | bytes 1179680 | tf_op jit(solution)/shard_map/ppermute | solution.py:146
  410.6 7.2 %collective-permute-start.40 = (bf16[256,2304]{1,0:T(8,128)(2,1)S(1)}, bf16[256,2304]{1,0:T(8,128)(2,1)}, u32[]{:S(2)}, u32[]{:S(2)}) collective-permute-start(bf16[256,2304]{1,0:T(8,128)(2,1)S(1)} %add.366), channel_id=1, source_target_pairs={{0,8},{4,12},{8,16},{12,20},{16,24},{20,28},{1,9},{5,13},{9,17},{1... | collective-permute-start | bytes 3538952 | tf_op jit(solution)/shard_map/ppermute | solution.py:146
  424.3 9.1 %weight_terms.5 = (bf16[256,2048]{1,0:T(8,128)(2,1)}, bf16[256,2048]{1,0:T(8,128)(2,1)}, bf16[256,2048]{1,0:T(8,128)(2,1)}, bf16[256,2048]{1,0:T(8,128)(2,1)}) custom-call(bf16[1024,512]{1,0:T(8,128)(2,1)} %get-tuple-element.326.refs_0_, bf16[1024,512]{1,0:T(8,128)(2,1)} %collective-permute-done.6.refs_1_, bf16[1024,512]{1,0:T(8,128)(2,1)} %get-tuple-element.424.refs_2_, ...), custom_call_target="tpu_custom_call" | custom-call | flops 4294967296 | bytes 12582912 | tf_op jit(solution)/shard_map/weight_terms/pallas_call | solution.py:576
  435.8 10.8 %collective-permute-done.43 = bf16[128,2048]{1,0:T(8,128)(2,1)S(1)} collective-permute-done((bf16[128,2048]{1,0:T(8,128)(2,1)}, bf16[128,2048]{1,0:T(8,128)(2,1)S(1)}, u32[]{:S(2)}, u32[]{:S(2)}) %collective-permute-start.43) | collective-permute-done | bytes 524320 | tf_op jit(solution)/shard_map/ppermute | solution.py:153
  466.0 6.5 %collective-permute-done.47 = bf16[256,2048]{1,0:T(8,128)(2,1)} collective-permute-done((bf16[256,2048]{1,0:T(8,128)(2,1)}, bf16[256,2048]{1,0:T(8,128)(2,1)}, u32[]{:S(2)}, u32[]{:S(2)}) %collective-permute-start.47) | collective-permute-done | bytes 1048608 | tf_op jit(solution)/shard_map/ppermute | solution.py:146
  474.7 4.6 collective-permute-start.52
  481.9 19.2 %collective-permute-done.54 = f32[7,2048]{1,0:T(8,128)S(1)} collective-permute-done((f32[7,2048]{1,0:T(8,128)S(1)}, f32[7,2048]{1,0:T(8,128)S(1)}, u32[]{:S(2)}, u32[]{:S(2)}) %collective-permute-start.54) | collective-permute-done | bytes 57376 | tf_op jit(solution)/shard_map/ppermute | solution.py:190
  501.1 5.6 collective-permute-start.55
  519.2 25.1 %feed_step.1 = (f32[256,2,1408]{2,1,0:T(2,128)}, f32[256,2,1408]{2,1,0:T(2,128)}, f32[256,2,1408]{2,1,0:T(2,128)}, f32[256,2,1408]{2,1,0:T(2,128)}, f32[256,1408...) custom-call(bf16[256,1920]{1,0:T(8,128)(2,1)} %get-tuple-element.373.refs_0_, ...), custom_call_target="tpu_custom_call" | custom-call | bytes 30277632 | tf_op jit(solution)/shard_map/feed_step/pallas_call | solution.py:650
  548.7 7.6 %plain_step.2 = (f32[3,256,512]{2,1,0:T(8,128)}, f32[3,256,512]{2,1,0:T(8,128)}, f32[3,256,512]{2,1,0:T(8,128)}, f32[3,256,512]{2,1,0:T(8,128)}) custom-call(bf16[256,2048]{1,0:T(8,128)(2,1)} %get-tuple-element.377.own, bf16[256,2048]{1,0:T(8,128)(2,1)} %copy-done.17, bf16[256,2048]{1,0:T(8,128)(2,1)} %copy-done.18, f32[3,256,512]{2,1,0:T(8,128)} %bitcast.50, ...), custom_call_target="tpu_custom_call" | custom-call | flops 1 | bytes 1 | tf_op jit(solution)/shard_map/plain_step/pallas_call | solution.py:608
  (325 shorter events, 180.9 us)
Async XLA Ops:
  7.2 88.6 %all-gather.3.cloned.1.call-start = ((), (), s32[]{:S(2)}) async-start(), calls=%async_computation | async-start | bytes 9437184 | tf_op jit(solution)/shard_map/all_gather | solution.py:734
  10.9 163.4 %all-gather.5.cloned.1.call-start = ((), (), s32[]{:S(2)}) async-start(), calls=%async_computation.1 | async-start | bytes 8847360 | tf_op jit(solution)/shard_map/all_gather | solution.py:743
  49.8 25.3 %collective-permute-start.4 = (bf16[128,2048]{1,0:T(8,128)(2,1)}, bf16[128,2048]{1,0:T(8,128)(2,1)}, u32[]{:S(2)}, u32[]{:S(2)}) collective-permute-start(bf16[128,2048]{1,0:T(8,128)(2,1)} %param.22), channel_id=1, source_target_pairs={{0,2},{1,3},{2,0},{3,1},{4,6},{5,7},{6,4},{7,5},{8,10},{9,11},{10,... | collective-permute-start | bytes 1572872 | tf_op jit(solution)/shard_map/ppermute | solution.py:153
  50.6 25.5 %collective-permute-start.5 = (bf16[128,2048]{1,0:T(8,128)(2,1)}, bf16[128,2048]{1,0:T(8,128)(2,1)S(1)}, u32[]{:S(2)}, u32[]{:S(2)}) collective-permute-start(bf16[128,2048]{1,0:T(8,128)(2,1)} %param.22), channel_id=1, source_target_pairs={{0,3},{1,2},{2,1},{3,0},{4,7},{5,6},{6,5},{7,4},{8,11},{9,10},{10,... | collective-permute-start | bytes 1572872 | tf_op jit(solution)/shard_map/ppermute | solution.py:153
  117.7 23.8 %collective-permute-start.9 = (bf16[128,2048]{1,0:T(8,128)(2,1)S(1)}, bf16[128,2048]{1,0:T(8,128)(2,1)S(1)}, u32[]{:S(2)}, u32[]{:S(2)}) collective-permute-start(bf16[128,2048]{1,0:T(8,128)(2,1)S(1)} %get-tuple-element.437), channel_id=1, source_target_pairs={{0,2},{1,3},{2,0},{3,1},{4,6},{5,7},{6,4},{7,5},{8,10},{9,11},{10,... | collective-permute-start | bytes 1572872 | tf_op jit(solution)/shard_map/ppermute | solution.py:153
  145.8 24.7 %collective-permute-start.12 = (bf16[128,2048]{1,0:T(8,128)(2,1)}, bf16[128,2048]{1,0:T(8,128)(2,1)}, u32[]{:S(2)}, u32[]{:S(2)}) collective-permute-start(bf16[128,2048]{1,0:T(8,128)(2,1)} %add_convert_fusion.3), channel_id=1, source_target_pairs={{0,2},{1,3},{2,0},{3,1},{4,6},{5,7},{6,4},{7,5},{8,10},{9,11},{10,... | collective-permute-start | bytes 1572872 | tf_op jit(solution)/shard_map/ppermute | solution.py:153
  174.4 27.2 %collective-permute-start.14 = (bf16[256,2304]{1,0:T(8,128)(2,1)S(1)}, bf16[256,2304]{1,0:T(8,128)(2,1)S(1)}, u32[]{:S(2)}, u32[]{:S(2)}) collective-permute-start(bf16[256,2304]{1,0:T(8,128)(2,1)S(1)} %pad_maximum_fusion.3.refs_1_), channel_id=1, source_target_pairs={{0,8},{4,12},{8,16},{12,20},{16,24},{20,28},{1,9},{5,13},{9,17},{1... | collective-permute-start | bytes 3538952 | tf_op jit(solution)/shard_map/ppermute | solution.py:85
  175.7 30.1 %collective-permute-start.15 = (bf16[256,2304]{1,0:T(8,128)(2,1)S(1)}, bf16[256,2304]{1,0:T(8,128)(2,1)S(1)}, u32[]{:S(2)}, u32[]{:S(2)}) collective-permute-start(bf16[256,2304]{1,0:T(8,128)(2,1)S(1)} %pad_maximum_fusion.3.refs_1_), channel_id=1, source_target_pairs={{8,0},{12,4},{16,8},{20,12},{24,16},{28,20},{9,1},{13,5},{17,9},{2... | collective-permute-start | bytes 3538952 | tf_op jit(solution)/shard_map/ppermute | solution.py:86
  210.1 31.0 %collective-permute-start.19 = (bf16[256,2304]{1,0:T(8,128)(2,1)S(1)}, bf16[256,2304]{1,0:T(8,128)(2,1)S(1)}, u32[]{:S(2)}, u32[]{:S(2)}) collective-permute-start(bf16[256,2304]{1,0:T(8,128)(2,1)S(1)} %collective-permute-done.15.refs_5_), channel_id=1, source_target_pairs={{8,0},{12,4},{16,8},{20,12},{9,1},{13,5},{17,9},{21,13},{10,2},{14... | collective-permute-start | bytes 3538952 | tf_op jit(solution)/shard_map/ppermute | solution.py:86
  241.1 29.0 %collective-permute-start.22 = (bf16[256,2304]{1,0:T(8,128)(2,1)S(1)}, bf16[256,2304]{1,0:T(8,128)(2,1)S(1)}, u32[]{:S(2)}, u32[]{:S(2)}) collective-permute-start(bf16[256,2304]{1,0:T(8,128)(2,1)S(1)} %collective-permute-done.18.refs_3_), channel_id=1, source_target_pairs={{16,24},{20,28},{17,25},{21,29},{18,26},{22,30},{19,27},{23,31}} | collective-permute-start | bytes 3538952 | tf_op jit(solution)/shard_map/ppermute | solution.py:85
  242.9 28.9 %collective-permute-start.23 = (bf16[256,2304]{1,0:T(8,128)(2,1)S(1)}, bf16[256,2304]{1,0:T(8,128)(2,1)S(1)}, u32[]{:S(2)}, u32[]{:S(2)}) collective-permute-start(bf16[256,2304]{1,0:T(8,128)(2,1)S(1)} %collective-permute-done.19.refs_6_), channel_id=1, source_target_pairs={{8,0},{12,4},{9,1},{13,5},{10,2},{14,6},{11,3},{15,7}} | collective-permute-start | bytes 3538952 | tf_op jit(solution)/shard_map/ppermute | solution.py:86
  245.2 25.0 %collective-permute-start.20 = (bf16[256,1920]{1,0:T(8,128)(2,1)}, bf16[256,1920]{1,0:T(8,128)(2,1)S(1)}, u32[]{:S(2)}, u32[]{:S(2)}) collective-permute-start(bf16[256,1920]{1,0:T(8,128)(2,1)} %get-tuple-element.275), channel_id=1, source_target_pairs={{0,8},{4,12},{1,9},{5,13},{2,10},{6,14},{3,11},{7,15}} | collective-permute-start | bytes 2949128 | tf_op jit(solution)/shard_map/ppermute | solution.py:146
  277.3 28.6 %collective-permute-start.24 = (bf16[256,1920]{1,0:T(8,128)(2,1)S(1)}, bf16[256,1920]{1,0:T(8,128)(2,1)S(1)}, u32[]{:S(2)}, u32[]{:S(2)}) collective-permute-start(bf16[256,1920]{1,0:T(8,128)(2,1)S(1)} %get-tuple-element.447), channel_id=1, source_target_pairs={{0,8},{4,12},{8,16},{12,20},{1,9},{5,13},{9,17},{13,21},{2,10},{6,... | collective-permute-start | bytes 2949128 | tf_op jit(solution)/shard_map/ppermute | solution.py:146
  280.0 25.9 %collective-permute-start.25 = (bf16[256,1920]{1,0:T(8,128)(2,1)S(1)}, bf16[256,1920]{1,0:T(8,128)(2,1)S(1)}, u32[]{:S(2)}, u32[]{:S(2)}) collective-permute-start(bf16[256,1920]{1,0:T(8,128)(2,1)S(1)} %get-tuple-element.446), channel_id=1, source_target_pairs={{16,8},{20,12},{24,16},{28,20},{17,9},{21,13},{25,17},{29,21},{18,... | collective-permute-start | bytes 2949128 | tf_op jit(solution)/shard_map/ppermute | solution.py:147
  308.9 32.4 %collective-permute-start.27 = (bf16[256,1920]{1,0:T(8,128)(2,1)S(1)}, bf16[256,1920]{1,0:T(8,128)(2,1)S(1)}, u32[]{:S(2)}, u32[]{:S(2)}) collective-permute-start(bf16[256,1920]{1,0:T(8,128)(2,1)S(1)} %add.358), channel_id=1, source_target_pairs={{0,8},{4,12},{8,16},{12,20},{16,24},{20,28},{1,9},{5,13},{9,17},{1... | collective-permute-start | bytes 2949128 | tf_op jit(solution)/shard_map/ppermute | solution.py:146
  312.0 29.3 %collective-permute-start.28 = (bf16[256,1920]{1,0:T(8,128)(2,1)S(1)}, bf16[256,1920]{1,0:T(8,128)(2,1)S(1)}, u32[]{:S(2)}, u32[]{:S(2)}) collective-permute-start(bf16[256,1920]{1,0:T(8,128)(2,1)S(1)} %add.359), channel_id=1, source_target_pairs={{8,0},{12,4},{16,8},{20,12},{24,16},{28,20},{9,1},{13,5},{17,9},{2... | collective-permute-start | bytes 2949128 | tf_op jit(solution)/shard_map/ppermute | solution.py:147
  316.3 25.0 %collective-permute-start.30 = (bf16[128,2048]{1,0:T(8,128)(2,1)}, bf16[128,2048]{1,0:T(8,128)(2,1)S(1)}, u32[]{:S(2)}, u32[]{:S(2)}) collective-permute-start(bf16[128,2048]{1,0:T(8,128)(2,1)} %get-tuple-element.430), channel_id=1, source_target_pairs={{0,2},{1,3},{2,0},{3,1},{4,6},{5,7},{6,4},{7,5},{8,10},{9,11},{10,... | collective-permute-start | bytes 1572872 | tf_op jit(solution)/shard_map/ppermute | solution.py:153
  345.3 31.2 %collective-permute-start.33 = (bf16[256,2304]{1,0:T(8,128)(2,1)S(1)}, bf16[256,2304]{1,0:T(8,128)(2,1)S(1)}, u32[]{:S(2)}, u32[]{:S(2)}) collective-permute-start(bf16[256,2304]{1,0:T(8,128)(2,1)S(1)} %copy-done.25), channel_id=1, source_target_pairs={{0,8},{4,12},{1,9},{5,13},{2,10},{6,14},{3,11},{7,15}} | collective-permute-start | bytes 3538952 | tf_op jit(solution)/shard_map/ppermute | solution.py:146
  349.8 26.7 %collective-permute-start.34 = (bf16[256,2304]{1,0:T(8,128)(2,1)S(1)}, bf16[256,2304]{1,0:T(8,128)(2,1)S(1)}, u32[]{:S(2)}, u32[]{:S(2)}) collective-permute-start(bf16[256,2304]{1,0:T(8,128)(2,1)S(1)} %copy-done.26), channel_id=1, source_target_pairs={{24,16},{28,20},{25,17},{29,21},{26,18},{30,22},{27,19},{31,23}} | collective-permute-start | bytes 3538952 | tf_op jit(solution)/shard_map/ppermute | solution.py:147
  378.1 27.3 %collective-permute-start.38 = (bf16[256,2304]{1,0:T(8,128)(2,1)}, bf16[256,2304]{1,0:T(8,128)(2,1)S(1)}, u32[]{:S(2)}, u32[]{:S(2)}) collective-permute-start(bf16[256,2304]{1,0:T(8,128)(2,1)} %get-tuple-element.443), channel_id=1, source_target_pairs={{0,8},{4,12},{8,16},{12,20},{1,9},{5,13},{9,17},{13,21},{2,10},{6,... | collective-permute-start | bytes 3538952 | tf_op jit(solution)/shard_map/ppermute | solution.py:146
  379.7 25.6 %collective-permute-start.39 = (bf16[256,2304]{1,0:T(8,128)(2,1)}, bf16[256,2304]{1,0:T(8,128)(2,1)S(1)}, u32[]{:S(2)}, u32[]{:S(2)}) collective-permute-start(bf16[256,2304]{1,0:T(8,128)(2,1)} %get-tuple-element.442), channel_id=1, source_target_pairs={{16,8},{20,12},{24,16},{28,20},{17,9},{21,13},{25,17},{29,21},{18,... | collective-permute-start | bytes 3538952 | tf_op jit(solution)/shard_map/ppermute | solution.py:147
  410.6 35.9 %collective-permute-start.40 = (bf16[256,2304]{1,0:T(8,128)(2,1)S(1)}, bf16[256,2304]{1,0:T(8,128)(2,1)}, u32[]{:S(2)}, u32[]{:S(2)}) collective-permute-start(bf16[256,2304]{1,0:T(8,128)(2,1)S(1)} %add.366), channel_id=1, source_target_pairs={{0,8},{4,12},{8,16},{12,20},{16,24},{20,28},{1,9},{5,13},{9,17},{1... | collective-permute-start | bytes 3538952 | tf_op jit(solution)/shard_map/ppermute | solution.py:146
  418.1 30.1 %collective-permute-start.41 = (bf16[256,2304]{1,0:T(8,128)(2,1)S(1)}, bf16[256,2304]{1,0:T(8,128)(2,1)}, u32[]{:S(2)}, u32[]{:S(2)}) collective-permute-start(bf16[256,2304]{1,0:T(8,128)(2,1)S(1)} %add.367), channel_id=1, source_target_pairs={{8,0},{12,4},{16,8},{20,12},{24,16},{28,20},{9,1},{13,5},{17,9},{2... | collective-permute-start | bytes 3538952 | tf_op jit(solution)/shard_map/ppermute | solution.py:147
  421.3 25.2 %collective-permute-start.43 = (bf16[128,2048]{1,0:T(8,128)(2,1)}, bf16[128,2048]{1,0:T(8,128)(2,1)S(1)}, u32[]{:S(2)}, u32[]{:S(2)}) collective-permute-start(bf16[128,2048]{1,0:T(8,128)(2,1)} %get-tuple-element.426), channel_id=1, source_target_pairs={{0,2},{1,3},{2,0},{3,1},{4,6},{5,7},{6,4},{7,5},{8,10},{9,11},{10,... | collective-permute-start | bytes 1572872 | tf_op jit(solution)/shard_map/ppermute | solution.py:153
  448.2 24.4 %collective-permute-start.47 = (bf16[256,2048]{1,0:T(8,128)(2,1)}, bf16[256,2048]{1,0:T(8,128)(2,1)}, u32[]{:S(2)}, u32[]{:S(2)}) collective-permute-start(bf16[256,2048]{1,0:T(8,128)(2,1)} %get-tuple-element.371), channel_id=1, source_target_pairs={{0,8},{4,12},{1,9},{5,13},{2,10},{6,14},{3,11},{7,15}} | collective-permute-start | bytes 3145736 | tf_op jit(solution)/shard_map/ppermute | solution.py:146
  474.7 34.3 %collective-permute-start.52 = (bf16[256,2048]{1,0:T(8,128)(2,1)S(1)}, bf16[256,2048]{1,0:T(8,128)(2,1)S(1)}, u32[]{:S(2)}, u32[]{:S(2)}) collective-permute-start(bf16[256,2048]{1,0:T(8,128)(2,1)S(1)} %get-tuple-element.445), channel_id=1, source_target_pairs={{0,8},{4,12},{8,16},{12,20},{1,9},{5,13},{9,17},{13,21},{2,10},{6,... | collective-permute-start | bytes 3145736 | tf_op jit(solution)/shard_map/ppermute | solution.py:146
  479.3 29.7 %collective-permute-start.53 = (bf16[256,2048]{1,0:T(8,128)(2,1)S(1)}, bf16[256,2048]{1,0:T(8,128)(2,1)S(1)}, u32[]{:S(2)}, u32[]{:S(2)}) collective-permute-start(bf16[256,2048]{1,0:T(8,128)(2,1)S(1)} %get-tuple-element.444), channel_id=1, source_target_pairs={{16,8},{20,12},{24,16},{28,20},{17,9},{21,13},{25,17},{29,21},{18,... | collective-permute-start | bytes 3145736 | tf_op jit(solution)/shard_map/ppermute | solution.py:147
  511.0 34.0 %collective-permute-start.58 = (bf16[128,2048]{1,0:T(8,128)(2,1)}, bf16[128,2048]{1,0:T(8,128)(2,1)S(1)}, u32[]{:S(2)}, u32[]{:S(2)}) collective-permute-start(bf16[128,2048]{1,0:T(8,128)(2,1)} %get-tuple-element.421), channel_id=1, source_target_pairs={{0,3},{1,2},{2,1},{3,0},{4,7},{5,6},{6,5},{7,4},{8,11},{9,10},{10,... | collective-permute-start | bytes 1572872 | tf_op jit(solution)/shard_map/ppermute | solution.py:153
  512.8 32.2 %collective-permute-start.57 = (bf16[128,2048]{1,0:T(8,128)(2,1)}, bf16[128,2048]{1,0:T(8,128)(2,1)}, u32[]{:S(2)}, u32[]{:S(2)}) collective-permute-start(bf16[128,2048]{1,0:T(8,128)(2,1)} %get-tuple-element.422), channel_id=1, source_target_pairs={{0,2},{1,3},{2,0},{3,1},{4,6},{5,7},{6,4},{7,5},{8,10},{9,11},{10,... | collective-permute-start | bytes 1572872 | tf_op jit(solution)/shard_map/ppermute | solution.py:153
  514.2 30.8 %collective-permute-start.56 = (bf16[128,2048]{1,0:T(8,128)(2,1)}, bf16[128,2048]{1,0:T(8,128)(2,1)}, u32[]{:S(2)}, u32[]{:S(2)}) collective-permute-start(bf16[128,2048]{1,0:T(8,128)(2,1)} %get-tuple-element.420), channel_id=1, source_target_pairs={{0,1},{1,0},{2,3},{3,2},{4,5},{5,4},{6,7},{7,6},{8,9},{9,8},{10,11... | collective-permute-start | bytes 1572872 | tf_op jit(solution)/shard_map/ppermute | solution.py:153
  514.9 32.4 %collective-permute-start.59 = (bf16[256,2048]{1,0:T(8,128)(2,1)S(1)}, bf16[256,2048]{1,0:T(8,128)(2,1)S(1)}, u32[]{:S(2)}, u32[]{:S(2)}) collective-permute-start(bf16[256,2048]{1,0:T(8,128)(2,1)S(1)} %add.384), channel_id=1, source_target_pairs={{0,8},{4,12},{8,16},{12,20},{16,24},{20,28},{1,9},{5,13},{9,17},{1... | collective-permute-start | bytes 3145736 | tf_op jit(solution)/shard_map/ppermute | solution.py:146
  517.2 30.2 %collective-permute-start.60 = (bf16[256,2048]{1,0:T(8,128)(2,1)S(1)}, bf16[256,2048]{1,0:T(8,128)(2,1)S(1)}, u32[]{:S(2)}, u32[]{:S(2)}) collective-permute-start(bf16[256,2048]{1,0:T(8,128)(2,1)S(1)} %add.385), channel_id=1, source_target_pairs={{8,0},{12,4},{16,8},{20,12},{24,16},{28,20},{9,1},{13,5},{17,9},{2... | collective-permute-start | bytes 3145736 | tf_op jit(solution)/shard_map/ppermute | solution.py:147
  (87 other events, 1313.1 us)
Sparse Core Ops, SparseCore 0:
  11.1 84.7 all-gather.2
  98.1 76.2 all-gather.4

commit v4 on v3

--- a/solution.py
+++ b/solution.py
@@ -8,7 +8,6 @@
 HD = 64
 ROT = 16
 STEP = 3
-MLP_CHUNKS = 2
 
 
 norm_eps = 1e-05
@@ -181,19 +180,14 @@
     return [(b, w, left) for b, w, (_, _, left) in zip(blocks, ways, streams)], others
 
 
-def add_terms(terms):
-    return add_up(terms).astype(jnp.bfloat16)
-
-
 def hop(array, axis, bit):
     count = lax.axis_size(axis)
     return array + lax.ppermute(array, axis, [(i, i ^ bit) for i in range(count)])
 
 
-def cuts(columns, count):
-    tiles = -(-columns // 128)
-    bounds = [min(columns, 128 * (tiles * i // count)) for i in range(count + 1)]
-    return [(a, b) for a, b in zip(bounds[:-1], bounds[1:]) if b > a]
+def cuts(columns):
+    first = min(columns, 128 * -(-(-(-columns // 128) * 5) // 11))
+    return [(0, first), (first, columns)]
 
 
 def paired(array):
@@ -428,6 +422,7 @@
 
 def feed_kernel(pieces, order_ref, second_in, cot_in, *refs):
     fulls, refs = refs[:pieces], refs[pieces:]
+    earlier, refs = (refs[:2], refs[2:]) if pieces > 1 else ((), refs)
     acts_ref, branch_ref, second_grad_ref, weight_ref, hidden_grad_ref, sems = refs[:6]
     j = pl.program_id(0)
     rows, width = second_in.shape
@@ -485,15 +480,16 @@
     def _():
         here = pl.ds(pl.multiple_of((j - 1) * size, size), size)
         over = ((1,), (1,))
-        second_grad_ref[...] = matmul(
-            acts_ref[:, : 2 * padded], weight_ref[here, : 2 * padded], over
-        ).astype(bf16)
-        branch_ref[...] = matmul(
-            acts_ref[:, 2 * padded :], weight_ref[here, 2 * padded :], over
-        ).astype(bf16)
-
-
-def feed(second_all, cot_all, fulls, order, size):
+        branch = matmul(acts_ref[:, 2 * padded :], weight_ref[here, 2 * padded :], over)
+        second_grad = matmul(acts_ref[:, : 2 * padded], weight_ref[here, : 2 * padded], over)
+        if pieces > 1:
+            branch = branch + earlier[0][...].astype(jnp.float32)
+            second_grad = second_grad + earlier[1][...].astype(jnp.float32)
+        branch_ref[...] = branch.astype(bf16)
+        second_grad_ref[...] = second_grad.astype(bf16)
+
+
+def feed(second_all, cot_all, fulls, order, size, earlier=()):
     rows, width = second_all.shape
     padded = fulls[0].shape[1] // 3
     pieces = len(fulls)
@@ -511,7 +507,7 @@
         grid_spec=pltpu.PrefetchScalarGridSpec(
             num_scalar_prefetch=1,
             grid=(1 + width // size,),
-            in_specs=[full] * 2 + [pl.BlockSpec(memory_space=pl.ANY)] * pieces,
+            in_specs=[full] * 2 + [pl.BlockSpec(memory_space=pl.ANY)] * pieces + [out] * len(earlier),
             out_specs=[pl.BlockSpec((rows, 3 * padded), lambda j, order_ref: (0, 0)), out, out],
             scratch_shapes=scratch,
         ),
@@ -524,7 +520,7 @@
             transcendentals=0,
         ),
         name="feed_forward",
-    )(order, second_all, cot_all, *fulls)
+    )(order, second_all, cot_all, *fulls, *earlier)
 
 
 def turned_kernel(blocks_ref, rows_ref, out_ref):
@@ -548,14 +544,20 @@
     )(jnp.stack(blocks).astype(jnp.int32), array)
 
 
-def terms_kernel(split, own_left, other_left, own_last, other_last, own_ref, other_ref, *outs):
+def terms_kernel(split, groups, own_left, other_left, own_last, other_last, own_ref, other_ref, *outs):
     k = pl.program_id(0)
+    lines = len(outs) // groups
+    per_group = pl.num_programs(0) // groups
 
     def write(own, other):
         total = (matmul(own[...], own_ref[...]) + matmul(other[...], other_ref[...])).astype(jnp.bfloat16)
         size = outs[0].shape[0]
-        for s, out in enumerate(outs):
-            out[...] = total[s * size : (s + 1) * size]
+        for g in range(groups):
+
+            @pl.when(k // per_group == g)
+            def _():
+                for s, out in enumerate(outs[g * lines : (g + 1) * lines]):
+                    out[...] = total[s * size : (s + 1) * size]
 
     @pl.when(k < split)
     def _():
@@ -566,25 +568,29 @@
         write(own_last, other_last)
 
 
-def weight_terms(left, left_last, right, tile, split, lines):
+def weight_terms(left, left_last, right, tile, split, lines, groups=1):
     count, rows = left[0].shape
     columns = right[0].shape[1]
     size = count // lines
+    per_group = columns // tile // groups
     left_spec = whole((count, rows))
     right_spec = pl.BlockSpec((rows, tile), lambda k: (0, k))
-    return list(
-        kernel_call(
-            lambda *refs: terms_kernel(split, *refs),
-            (columns // tile,),
-            [left_spec] * 4 + [right_spec] * 2,
-            [pl.BlockSpec((size, tile), lambda k: (0, k))] * lines,
-            [jax.ShapeDtypeStruct((size, columns), jnp.bfloat16)] * lines,
-            [],
-            "weight_terms",
-            4 * count * rows * columns,
-            2 * (4 * count * rows + 2 * rows * columns + count * columns),
-        )(*left, *left_last, *right)
-    )
+
+    def out_spec(g):
+        return pl.BlockSpec((size, tile), lambda k: (0, jnp.clip(k - g * per_group, 0, per_group - 1)))
+
+    outs = kernel_call(
+        lambda *refs: terms_kernel(split, groups, *refs),
+        (columns // tile,),
+        [left_spec] * 4 + [right_spec] * 2,
+        [out_spec(g) for g in range(groups) for _ in range(lines)],
+        [jax.ShapeDtypeStruct((size, columns // groups), jnp.bfloat16)] * (lines * groups),
+        [],
+        "weight_terms",
+        4 * count * rows * columns,
+        2 * (4 * count * rows + 2 * rows * columns + count * columns),
+    )(*left, *left_last, *right)
+    return [list(outs[g * lines : (g + 1) * lines]) for g in range(groups)]
 
 
 def summed(refs, rows, columns):
@@ -593,6 +599,7 @@
 
 
 def plain_step_kernel(own, up, down, weight, first, second, *outs):
+    outs = outs[-4:]
     everything = slice(None)
     gradient = summed((own, up, down), everything, everything)
     news = adamw(weight[0], first[0], second[0], gradient, matrix_rate, weight_decay)
@@ -600,67 +607,62 @@
         out[0] = value
 
 
-def plain_step(start, parts_of_sum, params):
-    kinds, rows, columns = params[0].shape
+def plain_step(start, parts_of_sum, params, kinds, earlier=()):
+    count, rows, columns = params[0].shape
     tile = rows // 2
     part = pl.BlockSpec((tile, columns), lambda k, r: (r, start + k))
-    block = pl.BlockSpec((1, tile, columns), lambda k, r: (k, r, 0))
-    return kernel_call(
+    block = pl.BlockSpec((1, tile, columns), lambda k, r: (kinds[0] + k, r, 0))
+    return pl.pallas_call(
         plain_step_kernel,
-        (kinds, 2),
-        [part] * 3 + [block] * 3,
-        [block] * 4,
-        [jax.ShapeDtypeStruct((kinds, rows, columns), jnp.float32)] * 4,
-        [],
-        "plain_step",
-    )(*parts_of_sum, *params)
-
-
-def feed_step_kernel(runs, *refs):
-    count = 3 * len(runs)
-    gate, down = refs[count : count + 3], refs[count + 3 : count + 6]
-    gate_outs, down_outs = refs[count + 6 : count + 10], refs[count + 10 : count + 14]
+        grid=(len(kinds), 2),
+        in_specs=[part] * 3 + [block] * 3 + [pl.BlockSpec(memory_space=pl.ANY)] * len(earlier),
+        out_specs=[block] * 4,
+        out_shape=[jax.ShapeDtypeStruct((count, rows, columns), jnp.float32)] * 4,
+        input_output_aliases={6 + i: i for i in range(len(earlier))},
+        compiler_params=pltpu.CompilerParams(vmem_limit_bytes=56 * 1024 * 1024),
+        cost_estimate=pl.CostEstimate(flops=1, bytes_accessed=1, transcendentals=0),
+        name="plain_step",
+    )(*parts_of_sum, *params, *earlier)
+
+
+def feed_step_kernel(*refs):
+    pairs, singles, gate, down = refs[:3], refs[3:6], refs[6:9], refs[9:12]
+    gate_outs, down_outs = refs[-8:-4], refs[-4:]
     everything = slice(None)
-    for at, (low, high) in enumerate(runs):
-        sums = refs[3 * at : 3 * at + 3]
-        padded = sums[0].shape[1] // 3
-        for c in range(0, high - low, 128):
-            size = min(128, high - low - c)
-            here = slice(low + c, low + c + size)
-            for k in range(2):
-                gradient = summed(sums, everything, slice(2 * c + 128 * k, 2 * c + 128 * k + size))
-                news = adamw(
-                    *[ref[:, k, here] for ref in gate], gradient, matrix_rate, weight_decay
-                )
-                for out, value in zip(gate_outs, (gradient,) + tuple(news)):
-                    out[:, k, here] = value
-        here = slice(low, high)
-        gradient = summed(sums, everything, slice(2 * padded, 2 * padded + high - low))
-        news = adamw(*[ref[:, here] for ref in down], gradient, matrix_rate, weight_decay)
-        for out, value in zip(down_outs, (gradient,) + tuple(news)):
-            out[:, here] = value
-
-
-def feed_step(runs, sums, gate, down):
+    for k in range(2):
+        gradient = summed(pairs, everything, slice(128 * k, 128 * k + 128))
+        news = adamw(*[ref[:, k, :] for ref in gate], gradient, matrix_rate, weight_decay)
+        for out, value in zip(gate_outs, (gradient,) + tuple(news)):
+            out[:, k, :] = value
+    gradient = summed(singles, everything, everything)
+    news = adamw(*[ref[...] for ref in down], gradient, matrix_rate, weight_decay)
+    for out, value in zip(down_outs, (gradient,) + tuple(news)):
+        out[...] = value
+
+
+def feed_step(run, parts_of_sum, gate, down, earlier=()):
     rows, columns = down[0].shape
-    tile = 32
-    gate_block = pl.BlockSpec((tile, 2, columns), lambda r: (r, 0, 0))
-    down_block = pl.BlockSpec((tile, columns), lambda r: (r, 0))
-    flat = [part for parts_of_sum in sums for part in parts_of_sum]
-    return kernel_call(
-        lambda *refs: feed_step_kernel(runs, *refs),
-        (rows // tile,),
-        [pl.BlockSpec((tile, part.shape[1]), lambda r: (r, 0)) for part in flat]
-        + [gate_block] * 3
-        + [down_block] * 3,
-        [gate_block] * 4 + [down_block] * 4,
-        [jax.ShapeDtypeStruct((rows, 2, columns), jnp.float32)] * 4
+    low, high = run
+    blocks = -(-(high - low) // 128)
+    gate_block = pl.BlockSpec((rows, 2, 128), lambda c: (0, 0, low // 128 + c))
+    down_block = pl.BlockSpec((rows, 128), lambda c: (0, low // 128 + c))
+    pair = pl.BlockSpec((rows, 256), lambda c: (0, c))
+    single = pl.BlockSpec((rows, 128), lambda c: (0, 2 * blocks + c))
+    return pl.pallas_call(
+        feed_step_kernel,
+        grid=(blocks,),
+        in_specs=[pair] * 3 + [single] * 3 + [gate_block] * 3 + [down_block] * 3
+        + [pl.BlockSpec(memory_space=pl.ANY)] * len(earlier),
+        out_specs=[gate_block] * 4 + [down_block] * 4,
+        out_shape=[jax.ShapeDtypeStruct((rows, 2, columns), jnp.float32)] * 4
         + [jax.ShapeDtypeStruct((rows, columns), jnp.float32)] * 4,
-        [],
-        "feed_step",
-        0,
-        84 * rows * columns,
-    )(*flat, *gate, *down)
+        input_output_aliases={12 + i: i for i in range(len(earlier))},
+        compiler_params=pltpu.CompilerParams(vmem_limit_bytes=56 * 1024 * 1024),
+        cost_estimate=pl.CostEstimate(
+            flops=0, bytes_accessed=84 * rows * (high - low), transcendentals=0
+        ),
+        name="feed_step",
+    )(*parts_of_sum, *parts_of_sum, *gate, *down, *earlier)
 
 
 def on_device(
@@ -732,7 +734,7 @@
         [jnp.swapaxes(entry_weight, 0, 1).astype(bf16), exit_weight.astype(bf16)[None]], axis=0
     )
     kinds = lax.all_gather(kinds_own, "dp", axis=1, tiled=True)
-    chunks = cuts(hidden_cols, MLP_CHUNKS)
+    chunks = cuts(hidden_cols)
 
     def unit_of(a, b):
         gates = paired(gate_weight[:, :, a:b].astype(bf16)).reshape(size, -1)
@@ -799,7 +801,7 @@
     acts_other = other_core(acts)
     second_sides = both_cores(after(second_all, acts))
     padded = acts.shape[1] // 3
-    terms = weight_terms(second_sides, cot_sides, (acts, acts_other), padded, 2, lines)
+    (terms,) = weight_terms(second_sides, cot_sides, (acts, acts_other), padded, 2, lines)
     terms, way_b = together(terms, way_b)
 
     way_b = gather_from(way_b, 3, lines, lines)
@@ -809,17 +811,18 @@
     streams = advance(streams)
     half = pack(*way_b, place, lines)
     order = jnp.stack(own_blocks + other_blocks).astype(jnp.int32)
-    acts, branch_b, second_b = feed(second_all, cot_all, [half, other_core(half)], order, size)
-    streams, (second_b, branch_b, acts) = together_streams(streams, (second_b, branch_b, acts))
-    second_grad = add_terms([second_a, second_b])
-    branch_terms = [branch_a, branch_b]
-    streams, second_grad = together_streams(streams, second_grad)
+    acts, branch_two, second_grad = feed(
+        second_all, cot_all, [half, other_core(half)], order, size, (branch_a, second_a)
+    )
+    streams, (second_grad, branch_two, acts) = together_streams(
+        streams, (second_grad, branch_two, acts)
+    )
 
     streams = advance(streams)
     acts_other = other_core(acts)
     arrived = send_rows(second_grad, parts)
     padded = acts.shape[1] // 3
-    terms = weight_terms(second_sides, cot_sides, (acts, acts_other), padded, 2, lines)
+    (terms,) = weight_terms(second_sides, cot_sides, (acts, acts_other), padded, 2, lines)
     streams, (arrived, terms) = together_streams(streams, (arrived, terms))
 
     second_grad = add_up(arrived)
@@ -830,14 +833,20 @@
     streams, (middle_low, terms) = together_streams(streams, (middle_low, terms))
     middle_all = gather_rows(middle_low, parts)
     streams = advance(streams) + begin(terms)
-    streams, middle_all = together_streams(streams, middle_all)
+    gate_params = (gate_weight, gate_first, gate_second)
+    down_params = (down_weight, down_first, down_second)
+    feed_news = feed_step(chunks[0], parts_of(finish(streams[:1])[0]), gate_params, down_params)
+    streams, (middle_all, feed_news, branch_two) = together_streams(
+        streams, (middle_all, feed_news, branch_two)
+    )
 
     streams = advance(streams)
+    leaving = send_rows(branch_two, parts)
     mixed_grad, normed_terms = attend_back(
         middle_all, kinds, mixed, context, log_totals, tables, marks
     )
-    streams, (mixed_grad, normed_terms, middle_all) = together_streams(
-        streams, (mixed_grad, normed_terms, middle_all)
+    streams, (mixed_grad, normed_terms, middle_all, leaving) = together_streams(
+        streams, (mixed_grad, normed_terms, middle_all, leaving)
     )
 
     arrived = send_rows(normed_terms, parts)
@@ -845,11 +854,21 @@
     mixed_other = other_core(mixed_grad)
     middle_sides = both_cores(middle_all)
     entry_terms = weight_terms(
-        normed_sides, middle_sides, (mixed_grad, mixed_other), head_cols, 3, lines
+        normed_sides, middle_sides, (mixed_grad, mixed_other), head_cols, 3, lines, 2
     )
     streams, (arrived, entry_terms) = together_streams(streams, (arrived, entry_terms))
 
-    streams = streams + begin(entry_terms)
+    early, late = begin(entry_terms[0]), begin(entry_terms[1])
+    feed_news = feed_step(chunks[1], parts_of(streams[1]), gate_params, down_params, feed_news)
+    early, (arrived, feed_news) = together_streams(early, (arrived, feed_news))
+    (
+        gate_gradient, gate_updated, gate_first_new, gate_second_new,
+        down_gradient, down_updated, down_first_new, down_second_new,
+    ) = feed_news
+
+    early = advance(early)
+    late, arrived = together_streams(late, arrived)
+    late = advance(late)
     normed_grad = add_up(arrived)
     input_gradient = middle_grad + norm_backward(normed_grad, unit_one, factor_one, norm_gains[0])
     gain_two_grad = jnp.sum(second_grad * unit_two, axis=0)
@@ -863,47 +882,41 @@
     )
     norms_local = jnp.stack([shift_one_grad, shift_two_grad, gain_one_grad, gain_two_grad])
     vectors = jnp.concatenate([placed, norms_local], axis=0)
-    bit = 1
-    while bit < parts:
-        vectors = hop(vectors, "tensor", bit)
-        bit *= 2
-    vectors = hop(vectors, "dp", 1)
-
-    streams, vectors = together_streams(streams, vectors)
-
-    streams = finish(streams[:-1]) + advance(streams[-1:])
-    bit = 2
-    while bit < dp_count:
-        vectors = hop(vectors, "dp", bit)
-        bit *= 2
-    streams, (vectors, branch_terms) = together_streams(streams, (vectors, branch_terms))
-
-    streams = finish(streams)
-    (
-        gate_gradient, gate_updated, gate_first_new, gate_second_new,
-        down_gradient, down_updated, down_first_new, down_second_new,
-    ) = feed_step(
-        chunks,
-        [parts_of(stream) for stream in streams[:-1]],
-        (gate_weight, gate_first, gate_second),
-        (down_weight, down_first, down_second),
-    )
-    branch_two = scatter_rows(add_terms(branch_terms), parts)
-    output_rows = (middle + branch_two).astype(bf16)
+    hops = [
+        (axis, 1 << power)
+        for axis, count in (("tensor", parts), ("dp", dp_count))
+        for power in range(count.bit_length() - 1)
+    ]
+    vectors = hop(vectors, *hops[0])
+    early, vectors = together_streams(early, vectors)
+
+    early = advance(early)
+    for which in hops[1:3]:
+        vectors = hop(vectors, *which)
+    late, vectors = together_streams(late, vectors)
+
+    late = advance(late)
+    vectors = hop(vectors, *hops[3])
+    early = finish(early)
+    early, (vectors, leaving) = together_streams(early, (vectors, leaving))
+    output_rows = (middle + add_up(leaving)).astype(bf16)
+
+    for which in hops[4:]:
+        vectors = hop(vectors, *which)
+    kind_first = lambda array: jnp.swapaxes(array, 0, 1)
+    entry_params = [kind_first(array) for array in (entry_weight, entry_first, entry_second)]
+    entry_news = plain_step(0, parts_of(early[0]), entry_params, (0, 1))
+    late = finish(late)
+    late, entry_news = together_streams(late, entry_news)
     bias_gradient = vectors[:5]
     gains_gradient = vectors[5:]
-    streams, _ = together_streams(streams, gate_updated)
-    kind_first = lambda array: jnp.swapaxes(array, 0, 1)
     entry_gradient, entry_updated, entry_first_new, entry_second_new = [
-        kind_first(array)
-        for array in plain_step(
-            0, parts_of(streams[-1]), [kind_first(array) for array in (entry_weight, entry_first, entry_second)]
-        )
+        kind_first(array) for array in plain_step(0, parts_of(late[0]), entry_params, (2,), entry_news)
     ]
     exit_gradient, exit_updated, exit_first_new, exit_second_new = [
         array[0]
         for array in plain_step(
-            3, parts_of(streams[-1]), [array[None] for array in (exit_weight, exit_first, exit_second)]
+            1, parts_of(late[0]), [array[None] for array in (exit_weight, exit_first, exit_second)], (0,)
         )
     ]
     bias_updated, bias_first_new, bias_second_new = adamw(

time: 577 us -> 557 us (0.965)
  waiting for transfers between devices: 230 us -> 187 us
  starting transfers between devices: 91.9 us -> 106 us
  other arithmetic: 35.8 us -> 42 us
    ppermute x5, waiting for transfers between devices: 26.8 us -> 9.3 us  [hop(): lax.ppermute(array, axis, [(i, i ^ bit) for i in range(count)])]
    ppermute x9 -> x12, waiting for transfers between devices: 32 us -> 19.6 us  [scatter_step(): up = lax.ppermute(up_send, 'dp', pairs_up(lines, 0, lines - j, 1))]
    ppermute x9 -> x12, starting transfers between devices: 33.6 us -> 43.3 us  [scatter_step(): up = lax.ppermute(up_send, 'dp', pairs_up(lines, 0, lines - j, 1))]
    ppermute x24, waiting for transfers between devices: 131 us -> 123 us  [swap_rows(): lax.ppermute(array, 'tensor', [(t, t ^ offset) for t in range(count)])]
    ppermute x9 -> x12, starting transfers between devices: 9.75 us -> 14.2 us  [scatter_step(): down = lax.ppermute(down_send, 'dp', pairs_up(lines, j, lines, -1))]
    pallas_call x6 -> x8, Pallas kernels: 63.3 us -> 64.7 us  [the longest x3 29.7 us: weight_terms(): kernel_call(lambda *refs: terms_kernel(split, groups, *refs), (columns //...]
    unnamed x115 -> x135, local copies, waits for them, and re-layouts: 19.6 us -> 19.8 us
  transfers between devices with their start and end apart: 63 -> 69, of which waited for: 33 -> 32; matrix products, arithmetic and copies ran while one was open for 9% -> 11% of each run, Pallas kernels for 24% -> 27%
where the time goes in v4:
time: 557 us; the launch traced here: 547 us
  waiting for transfers between devices  187 us (34%)
  Pallas kernels  153 us (27%)
  starting transfers between devices  106 us (19%)
  other arithmetic  42 us (8%)
  local copies, waits for them, and re-layouts  40.9 us (7%)
  between operations  15.7 us (3%)
    ppermute x24, waiting for transfers between devices, swap_rows(): lax.ppermute(array, 'tensor', [(t, t ^ offset) for t in range(count)])  123 us
    pallas_call x2, Pallas kernels, feed(): pl.pallas_call(lambda *refs: feed_kernel(pieces, *refs), grid_spec=pltpu....  45.4 us
    ppermute x12, starting transfers between devices, scatter_step(): up = lax.ppermute(up_send, 'dp', pairs_up(lines, 0, lines - j, 1))  43.3 us
    pallas_call x3, Pallas kernels, weight_terms(): kernel_call(lambda *refs: terms_kernel(split, groups, *refs), (columns //...  29.7 us
    ppermute x24, starting transfers between devices, swap_rows(): lax.ppermute(array, 'tensor', [(t, t ^ offset) for t in range(count)])  29.3 us
    pallas_call x2, Pallas kernels, feed_step(): pl.pallas_call(feed_step_kernel, grid=(blocks,), in_specs=[pair] * 3 + [s...  23.9 us
    ppermute x3, waiting for transfers between devices, gather_step(): down = lax.ppermute(downs[-1], 'dp', pairs_up(lines, 1, lines - s + 1, -1))  23.5 us
    unnamed x135, local copies, waits for them, and re-layouts  19.8 us
  transfers between devices with their start and end apart: 69, of which 32 were waited for; matrix products, arithmetic and copies ran while one was open for 11% of the time, Pallas kernels for 27%

profile of v4, /device:TPU:0, one launch (start us, length us, event | category | flops | bytes accessed | tf_op | source)
XLA Modules:
  0.0 547.0 jit_solution(13348859349619390306)
XLA Ops:
  17.8 4.0 collective-permute-start.2
  22.7 11.8 %collective-permute-done.2 = bf16[128,2048]{1,0:T(8,128)(2,1)S(1)} collective-permute-done((bf16[128,2048]{1,0:T(8,128)(2,1)S(1)}, bf16[128,2048]{1,0:T(8,128)(2,1)S(1)}, u32[]{:S(2)}, u32[]{:S(2)}) %collective-permute-start.2) | collective-permute-done | bytes 524320 | tf_op jit(solution)/shard_map/ppermute | solution.py:152
  34.6 10.4 %collective-permute-done.1 = bf16[128,2048]{1,0:T(8,128)(2,1)S(1)} collective-permute-done((bf16[128,2048]{1,0:T(8,128)(2,1)S(1)}, bf16[128,2048]{1,0:T(8,128)(2,1)S(1)}, u32[]{:S(2)}, u32[]{:S(2)}) %collective-permute-start.1) | collective-permute-done | bytes 524320 | tf_op jit(solution)/shard_map/ppermute | solution.py:152
  52.4 10.2 %collective-permute-done.3 = bf16[128,2048]{1,0:T(8,128)(2,1)} collective-permute-done((bf16[128,2048]{1,0:T(8,128)(2,1)}, bf16[128,2048]{1,0:T(8,128)(2,1)}, u32[]{:S(2)}, u32[]{:S(2)}) %collective-permute-start.3) | collective-permute-done | bytes 524320 | tf_op jit(solution)/shard_map/ppermute | solution.py:152
  63.7 10.7 %collective-permute-done.4 = bf16[128,2048]{1,0:T(8,128)(2,1)} collective-permute-done((bf16[128,2048]{1,0:T(8,128)(2,1)}, bf16[128,2048]{1,0:T(8,128)(2,1)}, u32[]{:S(2)}, u32[]{:S(2)}) %collective-permute-start.4) | collective-permute-done | bytes 524320 | tf_op jit(solution)/shard_map/ppermute | solution.py:152
  88.6 7.3 %all-gather.3.cloned.1.call-done.weight_ref.exit_ref.kinds_ref = bf16[4,2048,512]{2,1,0:T(8,128)(2,1)} async-done(((bf16[4,256,512]{2,1,0:T(8,128)(2,1)}), bf16[4,2048,512]{2,1,0:T(8,128)(2,1)}) %all-gather.3.cloned.1.call-update) | async-done | bytes 8388624 | tf_op jit(solution)/shard_map/all_gather | solution.py:736
  96.7 15.0 %attention.1 = (bf16[512,1536]{1,0:T(8,128)(2,1)}, bf16[512,512]{1,0:T(8,128)(2,1)}, f32[512,128]{1,0:T(8,128)}) custom-call(bf16[512,2048]{1,0:T(8,128)(2,1)} %copy-done, bf16[4,2048,512]{2,1,0:T(8,128)(2,1)} %all-gather.3.cloned.1.call-done.weight_ref.exit_ref.kinds_ref, f32[3,1,512]{2,1,0:T(1,128)} %reshape.257.offset_ref, ...), custom_call_target="tpu_custom_call" | custom-call | flops 12884901888 | bytes 8388608 | tf_op jit(solution)/shard_map/attention/pallas_call | solution.py:312
  118.5 11.3 %collective-permute-done.8 = bf16[128,2048]{1,0:T(8,128)(2,1)S(1)} collective-permute-done((bf16[128,2048]{1,0:T(8,128)(2,1)S(1)}, bf16[128,2048]{1,0:T(8,128)(2,1)S(1)}, u32[]{:S(2)}, u32[]{:S(2)}) %collective-permute-start.8) | collective-permute-done | bytes 524320 | tf_op jit(solution)/shard_map/ppermute | solution.py:152
  129.7 11.5 %collective-permute-done.10 = bf16[128,2048]{1,0:T(8,128)(2,1)S(1)} collective-permute-done((bf16[128,2048]{1,0:T(8,128)(2,1)S(1)}, bf16[128,2048]{1,0:T(8,128)(2,1)S(1)}, u32[]{:S(2)}, u32[]{:S(2)}) %collective-permute-start.10) | collective-permute-done | bytes 524320 | tf_op jit(solution)/shard_map/ppermute | solution.py:152
  152.7 8.6 %collective-permute-done.13 = bf16[128,2048]{1,0:T(8,128)(2,1)} collective-permute-done((bf16[128,2048]{1,0:T(8,128)(2,1)}, bf16[128,2048]{1,0:T(8,128)(2,1)}, u32[]{:S(2)}, u32[]{:S(2)}) %collective-permute-start.13) | collective-permute-done | bytes 524320 | tf_op jit(solution)/shard_map/ppermute | solution.py:152
  161.3 9.1 %collective-permute-done.12 = bf16[128,2048]{1,0:T(8,128)(2,1)} collective-permute-done((bf16[128,2048]{1,0:T(8,128)(2,1)}, bf16[128,2048]{1,0:T(8,128)(2,1)}, u32[]{:S(2)}, u32[]{:S(2)}) %collective-permute-start.12) | collective-permute-done | bytes 524320 | tf_op jit(solution)/shard_map/ppermute | solution.py:152
  175.6 4.6 collective-permute-start.14
  180.8 21.2 %feed_forward.2 = (bf16[512,1920]{1,0:T(8,128)(2,1)}, bf16[512,2048]{1,0:T(8,128)(2,1)}, bf16[512,2048]{1,0:T(8,128)(2,1)}) custom-call(s32[8]{0:T(128)} %iota.35.refs_0_, bf16[512,2048]{1,0:T(8,128)(2,1)} %pad_maximum_fusion.1.refs_1_.rows_ref, bf16[512,2048]{1,0:T(8,128)(2,1)} %copy-done.4, bf16[2048,1920]{1,0:T(8,128)(2,1)} %all-gather.5.cloned.1.call-done.refs_3_), custom_call_target="tpu_custom_call" | custom-call | flops 16106127360 | bytes 32505856 | tf_op jit(solution)/shard_map/feed_forward/pallas_call | solution.py:505
  212.3 9.7 %weight_terms.3 = (bf16[256,1920]{1,0:T(8,128)(2,1)}, bf16[256,1920]{1,0:T(8,128)(2,1)}, bf16[256,1920]{1,0:T(8,128)(2,1)}, bf16[256,1920]{1,0:T(8,128)(2,1)}) custom-call(bf16[1024,512]{1,0:T(8,128)(2,1)} %get-tuple-element.521.refs_0_, bf16[1024,512]{1,0:T(8,128)(2,1)} %copy-done.62, bf16[1024,512]{1,0:T(8,128)(2,1)} %get-tuple-element.275.refs_2_, ...), custom_call_target="tpu_custom_call" | custom-call | flops 4026531840 | bytes 12058624 | tf_op jit(solution)/shard_map/weight_terms/pallas_call | solution.py:582
  222.1 19.5 %collective-permute-done.19.refs_6_ = bf16[256,2304]{1,0:T(8,128)(2,1)S(1)} collective-permute-done((bf16[256,2304]{1,0:T(8,128)(2,1)S(1)}, bf16[256,2304]{1,0:T(8,128)(2,1)S(1)}, u32[]{:S(2)}, u32[]{:S(2)}) %collective-permute-start.19) | collective-permute-done | bytes 1179680 | tf_op jit(solution)/shard_map/ppermute | solution.py:85
  245.7 4.7 collective-permute-start.20
  251.1 19.6 %collective-permute-done.20 = bf16[256,1920]{1,0:T(8,128)(2,1)S(1)} collective-permute-done((bf16[256,1920]{1,0:T(8,128)(2,1)}, bf16[256,1920]{1,0:T(8,128)(2,1)S(1)}, u32[]{:S(2)}, u32[]{:S(2)}) %collective-permute-start.20) | collective-permute-done | bytes 983072 | tf_op jit(solution)/shard_map/ppermute | solution.py:145
  283.7 24.2 %feed_forward.3 = (bf16[512,2304]{1,0:T(8,128)(2,1)}, bf16[512,2048]{1,0:T(8,128)(2,1)}, bf16[512,2048]{1,0:T(8,128)(2,1)}) custom-call(s32[8]{0:T(128)} %copy-done.9, bf16[512,2048]{1,0:T(8,128)(2,1)} %pad_maximum_fusion.1.refs_1_.rows_ref, bf16[512,2048]{1,0:T(8,128)(2,1)} %copy-done.4, bf16[1024,2304]{1,0:T(8,128)(2,1)} %copy-done.3, ...), custom_call_target="tpu_custom_call" | custom-call | flops 19327352832 | bytes 35651584 | tf_op jit(solution)/shard_map/feed_forward/pallas_call | solution.py:505
  310.0 4.6 collective-permute-start.27
  320.7 10.1 %weight_terms.4 = (bf16[256,2304]{1,0:T(8,128)(2,1)}, bf16[256,2304]{1,0:T(8,128)(2,1)}, bf16[256,2304]{1,0:T(8,128)(2,1)}, bf16[256,2304]{1,0:T(8,128)(2,1)}) custom-call(bf16[1024,512]{1,0:T(8,128)(2,1)} %get-tuple-element.521.refs_0_, bf16[1024,512]{1,0:T(8,128)(2,1)} %copy-done.62, bf16[1024,512]{1,0:T(8,128)(2,1)} %get-tuple-element.275.refs_2_, ...), custom_call_target="tpu_custom_call" | custom-call | flops 4831838208 | bytes 13631488 | tf_op jit(solution)/shard_map/weight_terms/pallas_call | solution.py:582
  331.8 10.0 %collective-permute-done.30 = bf16[128,2048]{1,0:T(8,128)(2,1)S(1)} collective-permute-done((bf16[128,2048]{1,0:T(8,128)(2,1)}, bf16[128,2048]{1,0:T(8,128)(2,1)S(1)}, u32[]{:S(2)}, u32[]{:S(2)}) %collective-permute-start.30) | collective-permute-done | bytes 524320 | tf_op jit(solution)/shard_map/ppermute | solution.py:152
  352.9 11.0 %feed_step.2 = (f32[256,2,1408]{2,1,0:T(2,128)}, f32[256,2,1408]{2,1,0:T(2,128)}, f32[256,2,1408]{2,1,0:T(2,128)}, f32[256,2,1408]{2,1,0:T(2,128)}, f32[256,1408...) custom-call(bf16[256,1920]{1,0:T(8,128)(2,1)} %get-tuple-element.337.refs_0_.refs_3_, ...), custom_call_target="tpu_custom_call" | custom-call | bytes 13762560 | tf_op jit(solution)/shard_map/feed_step/pallas_call | solution.py:651
  365.2 9.9 %collective-permute-done.36 = bf16[128,2048]{1,0:T(8,128)(2,1)} collective-permute-done((bf16[128,2048]{1,0:T(8,128)(2,1)S(1)}, bf16[128,2048]{1,0:T(8,128)(2,1)}, u32[]{:S(2)}, u32[]{:S(2)}) %collective-permute-start.36) | collective-permute-done | bytes 524320 | tf_op jit(solution)/shard_map/ppermute | solution.py:152
  387.4 19.1 %attention_back.1 = (bf16[512,2048]{1,0:T(8,128)(2,1)}, bf16[512,2048]{1,0:T(8,128)(2,1)}) custom-call(bf16[512,2048]{1,0:T(8,128)(2,1)} %pad_maximum_fusion.2.middle_ref.rows_ref, bf16[4,2048,512]{2,1,0:T(8,128)(2,1)} %all-gather.3.cloned.1.call-done.weight_ref.exit_ref.kinds_ref, bf16[512,1536]{1,0:T(8,128)(2,1)} %get-tuple-element.357.mixed_ref, ...), custom_call_target="tpu_custom_call" | custom-call | flops 12884901888 | bytes 8388608 | tf_op jit(solution)/shard_map/attention_back/pallas_call | solution.py:405
  416.9 4.9 collective-permute-start.43
  427.4 9.8 %weight_terms.5 = (bf16[256,1024]{1,0:T(8,128)(2,1)}, bf16[256,1024]{1,0:T(8,128)(2,1)}, bf16[256,1024]{1,0:T(8,128)(2,1)}, bf16[256,1024]{1,0:T(8,128)(2,1)}, b...) custom-call(bf16[1024,512]{1,0:T(8,128)(2,1)} %get-tuple-element.368, ...), custom_call_target="tpu_custom_call" | custom-call | flops 4294967296 | bytes 12582912 | tf_op jit(solution)/shard_map/weight_terms/pallas_call | solution.py:582
  439.2 10.5 %collective-permute-done.46 = bf16[128,2048]{1,0:T(8,128)(2,1)} collective-permute-done((bf16[128,2048]{1,0:T(8,128)(2,1)}, bf16[128,2048]{1,0:T(8,128)(2,1)}, u32[]{:S(2)}, u32[]{:S(2)}) %collective-permute-start.46) | collective-permute-done | bytes 524320 | tf_op jit(solution)/shard_map/ppermute | solution.py:152
  449.7 4.4 collective-permute-start.50
  460.7 12.8 %feed_step.3 = (f32[256,2,1408]{2,1,0:T(2,128)}, f32[256,2,1408]{2,1,0:T(2,128)}, f32[256,2,1408]{2,1,0:T(2,128)}, f32[256,2,1408]{2,1,0:T(2,128)}, f32[256,1408...) custom-call(bf16[256,2304]{1,0:T(8,128)(2,1)} %get-tuple-element.388, ...), custom_call_target="tpu_custom_call", output_to_operand_aliasing={{0}: (12, {}), {1}: (13, {}), {2}: (14, {}), {3}: (15, {}),... | custom-call | bytes 16515072 | tf_op jit(solution)/shard_map/feed_step/pallas_call | solution.py:651
  501.2 4.7 collective-permute-start.57
  513.2 4.6 collective-permute-start.64
  524.5 5.3 plain_step.3
  (360 shorter events, 196.2 us)
Async XLA Ops:
  7.2 88.6 %all-gather.3.cloned.1.call-start = ((), (), s32[]{:S(2)}) async-start(), calls=%async_computation | async-start | bytes 9437184 | tf_op jit(solution)/shard_map/all_gather | solution.py:736
  10.9 163.4 %all-gather.5.cloned.1.call-start = ((), (), s32[]{:S(2)}) async-start(), calls=%async_computation.1 | async-start | bytes 8847360 | tf_op jit(solution)/shard_map/all_gather | solution.py:745
  22.3 23.5 %collective-permute-start = (bf16[128,2048]{1,0:T(8,128)(2,1)S(1)}, bf16[128,2048]{1,0:T(8,128)(2,1)}, u32[]{:S(2)}, u32[]{:S(2)}) collective-permute-start(bf16[128,2048]{1,0:T(8,128)(2,1)S(1)} %fusion.9), channel_id=1, source_target_pairs={{0,1},{1,0},{2,3},{3,2},{4,5},{5,4},{6,7},{7,6},{8,9},{9,8},{10,11... | collective-permute-start | bytes 1572872 | tf_op jit(solution)/shard_map/ppermute | solution.py:152
  49.2 25.2 %collective-permute-start.4 = (bf16[128,2048]{1,0:T(8,128)(2,1)}, bf16[128,2048]{1,0:T(8,128)(2,1)}, u32[]{:S(2)}, u32[]{:S(2)}) collective-permute-start(bf16[128,2048]{1,0:T(8,128)(2,1)} %param.22), channel_id=1, source_target_pairs={{0,2},{1,3},{2,0},{3,1},{4,6},{5,7},{6,4},{7,5},{8,10},{9,11},{10,... | collective-permute-start | bytes 1572872 | tf_op jit(solution)/shard_map/ppermute | solution.py:152
  50.1 25.4 %collective-permute-start.5 = (bf16[128,2048]{1,0:T(8,128)(2,1)}, bf16[128,2048]{1,0:T(8,128)(2,1)S(1)}, u32[]{:S(2)}, u32[]{:S(2)}) collective-permute-start(bf16[128,2048]{1,0:T(8,128)(2,1)} %param.22), channel_id=1, source_target_pairs={{0,3},{1,2},{2,1},{3,0},{4,7},{5,6},{6,5},{7,4},{8,11},{9,10},{10,... | collective-permute-start | bytes 1572872 | tf_op jit(solution)/shard_map/ppermute | solution.py:152
  116.4 24.8 %collective-permute-start.10 = (bf16[128,2048]{1,0:T(8,128)(2,1)S(1)}, bf16[128,2048]{1,0:T(8,128)(2,1)S(1)}, u32[]{:S(2)}, u32[]{:S(2)}) collective-permute-start(bf16[128,2048]{1,0:T(8,128)(2,1)S(1)} %get-tuple-element.523), channel_id=1, source_target_pairs={{0,3},{1,2},{2,1},{3,0},{4,7},{5,6},{6,5},{7,4},{8,11},{9,10},{10,... | collective-permute-start | bytes 1572872 | tf_op jit(solution)/shard_map/ppermute | solution.py:152
  117.9 24.7 %collective-permute-start.9 = (bf16[128,2048]{1,0:T(8,128)(2,1)S(1)}, bf16[128,2048]{1,0:T(8,128)(2,1)S(1)}, u32[]{:S(2)}, u32[]{:S(2)}) collective-permute-start(bf16[128,2048]{1,0:T(8,128)(2,1)S(1)} %get-tuple-element.524), channel_id=1, source_target_pairs={{0,2},{1,3},{2,0},{3,1},{4,6},{5,7},{6,4},{7,5},{8,10},{9,11},{10,... | collective-permute-start | bytes 1572872 | tf_op jit(solution)/shard_map/ppermute | solution.py:152
  146.6 23.7 %collective-permute-start.12 = (bf16[128,2048]{1,0:T(8,128)(2,1)}, bf16[128,2048]{1,0:T(8,128)(2,1)}, u32[]{:S(2)}, u32[]{:S(2)}) collective-permute-start(bf16[128,2048]{1,0:T(8,128)(2,1)} %add_convert_fusion.1), channel_id=1, source_target_pairs={{0,2},{1,3},{2,0},{3,1},{4,6},{5,7},{6,4},{7,5},{8,10},{9,11},{10,... | collective-permute-start | bytes 1572872 | tf_op jit(solution)/shard_map/ppermute | solution.py:152
  174.4 30.0 %collective-permute-start.15 = (bf16[256,2304]{1,0:T(8,128)(2,1)S(1)}, bf16[256,2304]{1,0:T(8,128)(2,1)S(1)}, u32[]{:S(2)}, u32[]{:S(2)}) collective-permute-start(bf16[256,2304]{1,0:T(8,128)(2,1)S(1)} %pad_maximum_fusion.3.refs_1_), channel_id=1, source_target_pairs={{8,0},{12,4},{16,8},{20,12},{24,16},{28,20},{9,1},{13,5},{17,9},{2... | collective-permute-start | bytes 3538952 | tf_op jit(solution)/shard_map/ppermute | solution.py:85
  175.6 29.9 %collective-permute-start.14 = (bf16[256,2304]{1,0:T(8,128)(2,1)S(1)}, bf16[256,2304]{1,0:T(8,128)(2,1)S(1)}, u32[]{:S(2)}, u32[]{:S(2)}) collective-permute-start(bf16[256,2304]{1,0:T(8,128)(2,1)S(1)} %pad_maximum_fusion.3.refs_1_), channel_id=1, source_target_pairs={{0,8},{4,12},{8,16},{12,20},{16,24},{20,28},{1,9},{5,13},{9,17},{1... | collective-permute-start | bytes 3538952 | tf_op jit(solution)/shard_map/ppermute | solution.py:84
  209.8 31.8 %collective-permute-start.19 = (bf16[256,2304]{1,0:T(8,128)(2,1)S(1)}, bf16[256,2304]{1,0:T(8,128)(2,1)S(1)}, u32[]{:S(2)}, u32[]{:S(2)}) collective-permute-start(bf16[256,2304]{1,0:T(8,128)(2,1)S(1)} %collective-permute-done.15.refs_5_), channel_id=1, source_target_pairs={{8,0},{12,4},{16,8},{20,12},{9,1},{13,5},{17,9},{21,13},{10,2},{14... | collective-permute-start | bytes 3538952 | tf_op jit(solution)/shard_map/ppermute | solution.py:85
  241.6 29.0 %collective-permute-start.22 = (bf16[256,2304]{1,0:T(8,128)(2,1)S(1)}, bf16[256,2304]{1,0:T(8,128)(2,1)S(1)}, u32[]{:S(2)}, u32[]{:S(2)}) collective-permute-start(bf16[256,2304]{1,0:T(8,128)(2,1)S(1)} %collective-permute-done.18.refs_3_), channel_id=1, source_target_pairs={{16,24},{20,28},{17,25},{21,29},{18,26},{22,30},{19,27},{23,31}} | collective-permute-start | bytes 3538952 | tf_op jit(solution)/shard_map/ppermute | solution.py:84
  243.3 28.9 %collective-permute-start.23 = (bf16[256,2304]{1,0:T(8,128)(2,1)S(1)}, bf16[256,2304]{1,0:T(8,128)(2,1)S(1)}, u32[]{:S(2)}, u32[]{:S(2)}) collective-permute-start(bf16[256,2304]{1,0:T(8,128)(2,1)S(1)} %collective-permute-done.19.refs_6_), channel_id=1, source_target_pairs={{8,0},{12,4},{9,1},{13,5},{10,2},{14,6},{11,3},{15,7}} | collective-permute-start | bytes 3538952 | tf_op jit(solution)/shard_map/ppermute | solution.py:85
  245.7 25.0 %collective-permute-start.20 = (bf16[256,1920]{1,0:T(8,128)(2,1)}, bf16[256,1920]{1,0:T(8,128)(2,1)S(1)}, u32[]{:S(2)}, u32[]{:S(2)}) collective-permute-start(bf16[256,1920]{1,0:T(8,128)(2,1)} %get-tuple-element.313), channel_id=1, source_target_pairs={{0,8},{4,12},{1,9},{5,13},{2,10},{6,14},{3,11},{7,15}} | collective-permute-start | bytes 2949128 | tf_op jit(solution)/shard_map/ppermute | solution.py:145
  277.8 30.1 %collective-permute-start.25 = (bf16[256,1920]{1,0:T(8,128)(2,1)S(1)}, bf16[256,1920]{1,0:T(8,128)(2,1)S(1)}, u32[]{:S(2)}, u32[]{:S(2)}) collective-permute-start(bf16[256,1920]{1,0:T(8,128)(2,1)S(1)} %get-tuple-element.531), channel_id=1, source_target_pairs={{16,8},{20,12},{24,16},{28,20},{17,9},{21,13},{25,17},{29,21},{18,... | collective-permute-start | bytes 2949128 | tf_op jit(solution)/shard_map/ppermute | solution.py:146
  278.5 29.4 %collective-permute-start.24 = (bf16[256,1920]{1,0:T(8,128)(2,1)S(1)}, bf16[256,1920]{1,0:T(8,128)(2,1)S(1)}, u32[]{:S(2)}, u32[]{:S(2)}) collective-permute-start(bf16[256,1920]{1,0:T(8,128)(2,1)S(1)} %get-tuple-element.532), channel_id=1, source_target_pairs={{0,8},{4,12},{8,16},{12,20},{1,9},{5,13},{9,17},{13,21},{2,10},{6,... | collective-permute-start | bytes 2949128 | tf_op jit(solution)/shard_map/ppermute | solution.py:145
  308.4 33.5 %collective-permute-start.28 = (bf16[256,1920]{1,0:T(8,128)(2,1)S(1)}, bf16[256,1920]{1,0:T(8,128)(2,1)S(1)}, u32[]{:S(2)}, u32[]{:S(2)}) collective-permute-start(bf16[256,1920]{1,0:T(8,128)(2,1)S(1)} %add.364), channel_id=1, source_target_pairs={{8,0},{12,4},{16,8},{20,12},{24,16},{28,20},{9,1},{13,5},{17,9},{2... | collective-permute-start | bytes 2949128 | tf_op jit(solution)/shard_map/ppermute | solution.py:146
  310.0 31.9 %collective-permute-start.27 = (bf16[256,1920]{1,0:T(8,128)(2,1)S(1)}, bf16[256,1920]{1,0:T(8,128)(2,1)S(1)}, u32[]{:S(2)}, u32[]{:S(2)}) collective-permute-start(bf16[256,1920]{1,0:T(8,128)(2,1)S(1)} %add.363), channel_id=1, source_target_pairs={{0,8},{4,12},{8,16},{12,20},{16,24},{20,28},{1,9},{5,13},{9,17},{1... | collective-permute-start | bytes 2949128 | tf_op jit(solution)/shard_map/ppermute | solution.py:145
  318.3 23.5 %collective-permute-start.30 = (bf16[128,2048]{1,0:T(8,128)(2,1)}, bf16[128,2048]{1,0:T(8,128)(2,1)S(1)}, u32[]{:S(2)}, u32[]{:S(2)}) collective-permute-start(bf16[128,2048]{1,0:T(8,128)(2,1)} %get-tuple-element.517), channel_id=1, source_target_pairs={{0,2},{1,3},{2,0},{3,1},{4,6},{5,7},{6,4},{7,5},{8,10},{9,11},{10,... | collective-permute-start | bytes 1572872 | tf_op jit(solution)/shard_map/ppermute | solution.py:152
  345.9 32.2 %collective-permute-start.33 = (bf16[256,2304]{1,0:T(8,128)(2,1)S(1)}, bf16[256,2304]{1,0:T(8,128)(2,1)S(1)}, u32[]{:S(2)}, u32[]{:S(2)}) collective-permute-start(bf16[256,2304]{1,0:T(8,128)(2,1)S(1)} %copy-done.31), channel_id=1, source_target_pairs={{0,8},{4,12},{1,9},{5,13},{2,10},{6,14},{3,11},{7,15}} | collective-permute-start | bytes 3538952 | tf_op jit(solution)/shard_map/ppermute | solution.py:145
  348.6 29.4 %collective-permute-start.34 = (bf16[256,2304]{1,0:T(8,128)(2,1)S(1)}, bf16[256,2304]{1,0:T(8,128)(2,1)S(1)}, u32[]{:S(2)}, u32[]{:S(2)}) collective-permute-start(bf16[256,2304]{1,0:T(8,128)(2,1)S(1)} %copy-done.30), channel_id=1, source_target_pairs={{24,16},{28,20},{25,17},{29,21},{26,18},{30,22},{27,19},{31,23}} | collective-permute-start | bytes 3538952 | tf_op jit(solution)/shard_map/ppermute | solution.py:146
  351.1 24.1 %collective-permute-start.36 = (bf16[128,2048]{1,0:T(8,128)(2,1)S(1)}, bf16[128,2048]{1,0:T(8,128)(2,1)}, u32[]{:S(2)}, u32[]{:S(2)}) collective-permute-start(bf16[128,2048]{1,0:T(8,128)(2,1)S(1)} %get-tuple-element.340), channel_id=1, source_target_pairs={{0,2},{1,3},{2,0},{3,1},{4,6},{5,7},{6,4},{7,5},{8,10},{9,11},{10,... | collective-permute-start | bytes 1572872 | tf_op jit(solution)/shard_map/ppermute | solution.py:152
  379.7 30.2 %collective-permute-start.39 = (bf16[256,2304]{1,0:T(8,128)(2,1)}, bf16[256,2304]{1,0:T(8,128)(2,1)S(1)}, u32[]{:S(2)}, u32[]{:S(2)}) collective-permute-start(bf16[256,2304]{1,0:T(8,128)(2,1)} %get-tuple-element.529), channel_id=1, source_target_pairs={{16,8},{20,12},{24,16},{28,20},{17,9},{21,13},{25,17},{29,21},{18,... | collective-permute-start | bytes 3538952 | tf_op jit(solution)/shard_map/ppermute | solution.py:146
  380.4 29.5 %collective-permute-start.38 = (bf16[256,2304]{1,0:T(8,128)(2,1)}, bf16[256,2304]{1,0:T(8,128)(2,1)S(1)}, u32[]{:S(2)}, u32[]{:S(2)}) collective-permute-start(bf16[256,2304]{1,0:T(8,128)(2,1)} %get-tuple-element.530), channel_id=1, source_target_pairs={{0,8},{4,12},{8,16},{12,20},{1,9},{5,13},{9,17},{13,21},{2,10},{6,... | collective-permute-start | bytes 3538952 | tf_op jit(solution)/shard_map/ppermute | solution.py:145
  385.3 24.5 %collective-permute-start.41 = (bf16[128,2048]{1,0:T(8,128)(2,1)}, bf16[128,2048]{1,0:T(8,128)(2,1)}, u32[]{:S(2)}, u32[]{:S(2)}) collective-permute-start(bf16[128,2048]{1,0:T(8,128)(2,1)} %get-tuple-element.513), channel_id=1, source_target_pairs={{0,2},{1,3},{2,0},{3,1},{4,6},{5,7},{6,4},{7,5},{8,10},{9,11},{10,... | collective-permute-start | bytes 1572872 | tf_op jit(solution)/shard_map/ppermute | solution.py:152
  415.2 34.5 %collective-permute-start.44 = (bf16[256,2304]{1,0:T(8,128)(2,1)S(1)}, bf16[256,2304]{1,0:T(8,128)(2,1)S(1)}, u32[]{:S(2)}, u32[]{:S(2)}) collective-permute-start(bf16[256,2304]{1,0:T(8,128)(2,1)S(1)} %add.372), channel_id=1, source_target_pairs={{8,0},{12,4},{16,8},{20,12},{24,16},{28,20},{9,1},{13,5},{17,9},{2... | collective-permute-start | bytes 3538952 | tf_op jit(solution)/shard_map/ppermute | solution.py:146
  416.9 32.8 %collective-permute-start.43 = (bf16[256,2304]{1,0:T(8,128)(2,1)S(1)}, bf16[256,2304]{1,0:T(8,128)(2,1)S(1)}, u32[]{:S(2)}, u32[]{:S(2)}) collective-permute-start(bf16[256,2304]{1,0:T(8,128)(2,1)S(1)} %add.371), channel_id=1, source_target_pairs={{0,8},{4,12},{8,16},{12,20},{16,24},{20,28},{1,9},{5,13},{9,17},{1... | collective-permute-start | bytes 3538952 | tf_op jit(solution)/shard_map/ppermute | solution.py:145
  424.6 25.0 %collective-permute-start.46 = (bf16[128,2048]{1,0:T(8,128)(2,1)}, bf16[128,2048]{1,0:T(8,128)(2,1)}, u32[]{:S(2)}, u32[]{:S(2)}) collective-permute-start(bf16[128,2048]{1,0:T(8,128)(2,1)} %get-tuple-element.509), channel_id=1, source_target_pairs={{0,2},{1,3},{2,0},{3,1},{4,6},{5,7},{6,4},{7,5},{8,10},{9,11},{10,... | collective-permute-start | bytes 1572872 | tf_op jit(solution)/shard_map/ppermute | solution.py:152
  426.1 23.6 %collective-permute-start.45 = (bf16[128,2048]{1,0:T(8,128)(2,1)}, bf16[128,2048]{1,0:T(8,128)(2,1)}, u32[]{:S(2)}, u32[]{:S(2)}) collective-permute-start(bf16[128,2048]{1,0:T(8,128)(2,1)} %get-tuple-element.510), channel_id=1, source_target_pairs={{0,1},{1,0},{2,3},{3,2},{4,5},{5,4},{6,7},{7,6},{8,9},{9,8},{10,11... | collective-permute-start | bytes 1572872 | tf_op jit(solution)/shard_map/ppermute | solution.py:152
  449.7 23.8 %collective-permute-start.50 = (bf16[256,1024]{1,0:T(8,128)(2,1)}, bf16[256,1024]{1,0:T(8,128)(2,1)}, u32[]{:S(2)}, u32[]{:S(2)}) collective-permute-start(bf16[256,1024]{1,0:T(8,128)(2,1)} %get-tuple-element.427), channel_id=1, source_target_pairs={{0,8},{4,12},{1,9},{5,13},{2,10},{6,14},{3,11},{7,15}} | collective-permute-start | bytes 1572872 | tf_op jit(solution)/shard_map/ppermute | solution.py:145
  456.1 23.4 %collective-permute-start.54 = (bf16[256,1024]{1,0:T(8,128)(2,1)}, bf16[256,1024]{1,0:T(8,128)(2,1)}, u32[]{:S(2)}, u32[]{:S(2)}) collective-permute-start(bf16[256,1024]{1,0:T(8,128)(2,1)} %get-tuple-element.448), channel_id=1, source_target_pairs={{0,8},{4,12},{1,9},{5,13},{2,10},{6,14},{3,11},{7,15}} | collective-permute-start | bytes 1572872 | tf_op jit(solution)/shard_map/ppermute | solution.py:145
  481.8 24.2 %collective-permute-start.60 = (bf16[256,1024]{1,0:T(8,128)(2,1)}, bf16[256,1024]{1,0:T(8,128)(2,1)}, u32[]{:S(2)}, u32[]{:S(2)}) collective-permute-start(bf16[256,1024]{1,0:T(8,128)(2,1)} %get-tuple-element.533), channel_id=1, source_target_pairs={{16,8},{20,12},{24,16},{28,20},{17,9},{21,13},{25,17},{29,21},{18,... | collective-permute-start | bytes 1572872 | tf_op jit(solution)/shard_map/ppermute | solution.py:146
  (103 other events, 1393.5 us)
Sparse Core Ops, SparseCore 0:
  11.0 84.7 all-gather.2
  98.1 76.2 all-gather.4

commit v5 on v4

--- a/solution.py
+++ b/solution.py
@@ -856,7 +856,6 @@
     entry_terms = weight_terms(
         normed_sides, middle_sides, (mixed_grad, mixed_other), head_cols, 3, lines, 2
     )
-    streams, (arrived, entry_terms) = together_streams(streams, (arrived, entry_terms))
 
     early, late = begin(entry_terms[0]), begin(entry_terms[1])
     feed_news = feed_step(chunks[1], parts_of(streams[1]), gate_params, down_params, feed_news)

time: 557 us -> 550 us (0.987)
  waiting for transfers between devices: 187 us -> 181 us
    ppermute x24, waiting for transfers between devices: 123 us -> 114 us  [swap_rows(): lax.ppermute(array, 'tensor', [(t, t ^ offset) for t in range(count)])]
    unnamed x135 -> x137, local copies, waits for them, and re-layouts: 19.8 us -> 19.5 us
  transfers between devices with their start and end apart: 69 -> 69, of which waited for: 32 -> 27; matrix products, arithmetic and copies ran while one was open for 11% -> 11% of each run, Pallas kernels for 27% -> 27%
where the time goes in v5:
time: 550 us; the launch traced here: 541 us
  waiting for transfers between devices  181 us (33%)
  Pallas kernels  153 us (28%)
  starting transfers between devices  106 us (19%)
  other arithmetic  41 us (7%)
  local copies, waits for them, and re-layouts  40.8 us (7%)
  between operations  15.7 us (3%)
    ppermute x24, waiting for transfers between devices, swap_rows(): lax.ppermute(array, 'tensor', [(t, t ^ offset) for t in range(count)])  114 us
    ppermute x12, starting transfers between devices, scatter_step(): up = lax.ppermute(up_send, 'dp', pairs_up(lines, 0, lines - j, 1))  45.5 us
    pallas_call x2, Pallas kernels, feed(): pl.pallas_call(lambda *refs: feed_kernel(pieces, *refs), grid_spec=pltpu....  45.3 us
    pallas_call x3, Pallas kernels, weight_terms(): kernel_call(lambda *refs: terms_kernel(split, groups, *refs), (columns //...  29.7 us
    ppermute x24, starting transfers between devices, swap_rows(): lax.ppermute(array, 'tensor', [(t, t ^ offset) for t in range(count)])  29.3 us
    ppermute x3, waiting for transfers between devices, gather_step(): down = lax.ppermute(downs[-1], 'dp', pairs_up(lines, 1, lines - s + 1, -1))  24.6 us
    pallas_call x2, Pallas kernels, feed_step(): pl.pallas_call(feed_step_kernel, grid=(blocks,), in_specs=[pair] * 3 + [s...  23.9 us
    ppermute x12, waiting for transfers between devices, scatter_step(): up = lax.ppermute(up_send, 'dp', pairs_up(lines, 0, lines - j, 1))  19.6 us
  transfers between devices with their start and end apart: 69, of which 27 were waited for; matrix products, arithmetic and copies ran while one was open for 11% of the time, Pallas kernels for 27%

profile of v5, /device:TPU:0, one launch (start us, length us, event | category | flops | bytes accessed | tf_op | source)
XLA Modules:
  0.0 540.6 jit_solution(540417667345236680)
XLA Ops:
  22.2 10.9 %collective-permute-done = bf16[128,2048]{1,0:T(8,128)(2,1)S(1)} collective-permute-done((bf16[128,2048]{1,0:T(8,128)(2,1)S(1)}, bf16[128,2048]{1,0:T(8,128)(2,1)S(1)}, u32[]{:S(2)}, u32[]{:S(2)}) %collective-permute-start) | collective-permute-done | bytes 524320 | tf_op jit(solution)/shard_map/ppermute | solution.py:152
  33.1 11.9 %collective-permute-done.1 = bf16[128,2048]{1,0:T(8,128)(2,1)S(1)} collective-permute-done((bf16[128,2048]{1,0:T(8,128)(2,1)S(1)}, bf16[128,2048]{1,0:T(8,128)(2,1)S(1)}, u32[]{:S(2)}, u32[]{:S(2)}) %collective-permute-start.1) | collective-permute-done | bytes 524320 | tf_op jit(solution)/shard_map/ppermute | solution.py:152
  52.4 10.3 %collective-permute-done.3 = bf16[128,2048]{1,0:T(8,128)(2,1)} collective-permute-done((bf16[128,2048]{1,0:T(8,128)(2,1)}, bf16[128,2048]{1,0:T(8,128)(2,1)}, u32[]{:S(2)}, u32[]{:S(2)}) %collective-permute-start.3) | collective-permute-done | bytes 524320 | tf_op jit(solution)/shard_map/ppermute | solution.py:152
  63.8 8.5 %collective-permute-done.4 = bf16[128,2048]{1,0:T(8,128)(2,1)} collective-permute-done((bf16[128,2048]{1,0:T(8,128)(2,1)}, bf16[128,2048]{1,0:T(8,128)(2,1)}, u32[]{:S(2)}, u32[]{:S(2)}) %collective-permute-start.4) | collective-permute-done | bytes 524320 | tf_op jit(solution)/shard_map/ppermute | solution.py:152
  86.5 8.5 %all-gather.3.cloned.1.call-done.weight_ref.exit_ref.kinds_ref = bf16[4,2048,512]{2,1,0:T(8,128)(2,1)} async-done(((bf16[4,256,512]{2,1,0:T(8,128)(2,1)}), bf16[4,2048,512]{2,1,0:T(8,128)(2,1)}) %all-gather.3.cloned.1.call-update) | async-done | bytes 8388624 | tf_op jit(solution)/shard_map/all_gather | solution.py:736
  95.9 15.0 %attention.1 = (bf16[512,1536]{1,0:T(8,128)(2,1)}, bf16[512,512]{1,0:T(8,128)(2,1)}, f32[512,128]{1,0:T(8,128)}) custom-call(bf16[512,2048]{1,0:T(8,128)(2,1)} %copy-done, bf16[4,2048,512]{2,1,0:T(8,128)(2,1)} %all-gather.3.cloned.1.call-done.weight_ref.exit_ref.kinds_ref, f32[3,1,512]{2,1,0:T(1,128)} %reshape.257.offset_ref, ...), custom_call_target="tpu_custom_call" | custom-call | flops 12884901888 | bytes 8388608 | tf_op jit(solution)/shard_map/attention/pallas_call | solution.py:312
  117.6 12.2 %collective-permute-done.10 = bf16[128,2048]{1,0:T(8,128)(2,1)S(1)} collective-permute-done((bf16[128,2048]{1,0:T(8,128)(2,1)S(1)}, bf16[128,2048]{1,0:T(8,128)(2,1)S(1)}, u32[]{:S(2)}, u32[]{:S(2)}) %collective-permute-start.10) | collective-permute-done | bytes 524320 | tf_op jit(solution)/shard_map/ppermute | solution.py:152
  129.9 10.6 %collective-permute-done.8 = bf16[128,2048]{1,0:T(8,128)(2,1)S(1)} collective-permute-done((bf16[128,2048]{1,0:T(8,128)(2,1)S(1)}, bf16[128,2048]{1,0:T(8,128)(2,1)S(1)}, u32[]{:S(2)}, u32[]{:S(2)}) %collective-permute-start.8) | collective-permute-done | bytes 524320 | tf_op jit(solution)/shard_map/ppermute | solution.py:152
  150.5 7.6 %collective-permute-done.11 = bf16[128,2048]{1,0:T(8,128)(2,1)} collective-permute-done((bf16[128,2048]{1,0:T(8,128)(2,1)}, bf16[128,2048]{1,0:T(8,128)(2,1)}, u32[]{:S(2)}, u32[]{:S(2)}) %collective-permute-start.11) | collective-permute-done | bytes 524320 | tf_op jit(solution)/shard_map/ppermute | solution.py:152
  158.1 11.5 %collective-permute-done.12 = bf16[128,2048]{1,0:T(8,128)(2,1)} collective-permute-done((bf16[128,2048]{1,0:T(8,128)(2,1)}, bf16[128,2048]{1,0:T(8,128)(2,1)}, u32[]{:S(2)}, u32[]{:S(2)}) %collective-permute-start.12) | collective-permute-done | bytes 524320 | tf_op jit(solution)/shard_map/ppermute | solution.py:152
  176.7 21.2 %feed_forward.2 = (bf16[512,1920]{1,0:T(8,128)(2,1)}, bf16[512,2048]{1,0:T(8,128)(2,1)}, bf16[512,2048]{1,0:T(8,128)(2,1)}) custom-call(s32[8]{0:T(128)} %iota.35.refs_0_, bf16[512,2048]{1,0:T(8,128)(2,1)} %pad_maximum_fusion.1.refs_1_.rows_ref, bf16[512,2048]{1,0:T(8,128)(2,1)} %copy-done.4, bf16[2048,1920]{1,0:T(8,128)(2,1)} %all-gather.5.cloned.1.call-done.refs_3_), custom_call_target="tpu_custom_call" | custom-call | flops 16106127360 | bytes 32505856 | tf_op jit(solution)/shard_map/feed_forward/pallas_call | solution.py:505
  200.7 4.3 collective-permute-done.15.refs_5_
  211.8 9.8 %weight_terms.3 = (bf16[256,1920]{1,0:T(8,128)(2,1)}, bf16[256,1920]{1,0:T(8,128)(2,1)}, bf16[256,1920]{1,0:T(8,128)(2,1)}, bf16[256,1920]{1,0:T(8,128)(2,1)}) custom-call(bf16[1024,512]{1,0:T(8,128)(2,1)} %get-tuple-element.491.refs_0_, bf16[1024,512]{1,0:T(8,128)(2,1)} %copy-done.63, bf16[1024,512]{1,0:T(8,128)(2,1)} %get-tuple-element.262.refs_2_, ...), custom_call_target="tpu_custom_call" | custom-call | flops 4026531840 | bytes 12058624 | tf_op jit(solution)/shard_map/weight_terms/pallas_call | solution.py:582
  221.6 18.7 %collective-permute-done.19.refs_6_ = bf16[256,2304]{1,0:T(8,128)(2,1)S(1)} collective-permute-done((bf16[256,2304]{1,0:T(8,128)(2,1)S(1)}, bf16[256,2304]{1,0:T(8,128)(2,1)S(1)}, u32[]{:S(2)}, u32[]{:S(2)}) %collective-permute-start.19) | collective-permute-done | bytes 1179680 | tf_op jit(solution)/shard_map/ppermute | solution.py:85
  244.3 4.7 collective-permute-start.20
  249.8 19.6 %collective-permute-done.20 = bf16[256,1920]{1,0:T(8,128)(2,1)S(1)} collective-permute-done((bf16[256,1920]{1,0:T(8,128)(2,1)}, bf16[256,1920]{1,0:T(8,128)(2,1)S(1)}, u32[]{:S(2)}, u32[]{:S(2)}) %collective-permute-start.20) | collective-permute-done | bytes 983072 | tf_op jit(solution)/shard_map/ppermute | solution.py:145
  282.4 24.2 %feed_forward.3 = (bf16[512,2304]{1,0:T(8,128)(2,1)}, bf16[512,2048]{1,0:T(8,128)(2,1)}, bf16[512,2048]{1,0:T(8,128)(2,1)}) custom-call(s32[8]{0:T(128)} %copy-done.9, bf16[512,2048]{1,0:T(8,128)(2,1)} %pad_maximum_fusion.1.refs_1_.rows_ref, bf16[512,2048]{1,0:T(8,128)(2,1)} %copy-done.4, bf16[1024,2304]{1,0:T(8,128)(2,1)} %copy-done.3, ...), custom_call_target="tpu_custom_call" | custom-call | flops 19327352832 | bytes 35651584 | tf_op jit(solution)/shard_map/feed_forward/pallas_call | solution.py:505
  308.7 4.6 collective-permute-start.27
  319.4 10.1 %weight_terms.4 = (bf16[256,2304]{1,0:T(8,128)(2,1)}, bf16[256,2304]{1,0:T(8,128)(2,1)}, bf16[256,2304]{1,0:T(8,128)(2,1)}, bf16[256,2304]{1,0:T(8,128)(2,1)}) custom-call(bf16[1024,512]{1,0:T(8,128)(2,1)} %get-tuple-element.491.refs_0_, bf16[1024,512]{1,0:T(8,128)(2,1)} %copy-done.63, bf16[1024,512]{1,0:T(8,128)(2,1)} %get-tuple-element.262.refs_2_, ...), custom_call_target="tpu_custom_call" | custom-call | flops 4831838208 | bytes 13631488 | tf_op jit(solution)/shard_map/weight_terms/pallas_call | solution.py:582
  329.6 11.3 %collective-permute-done.30 = bf16[128,2048]{1,0:T(8,128)(2,1)S(1)} collective-permute-done((bf16[128,2048]{1,0:T(8,128)(2,1)}, bf16[128,2048]{1,0:T(8,128)(2,1)S(1)}, u32[]{:S(2)}, u32[]{:S(2)}) %collective-permute-start.30) | collective-permute-done | bytes 524320 | tf_op jit(solution)/shard_map/ppermute | solution.py:152
  351.9 11.0 %feed_step.2 = (f32[256,2,1408]{2,1,0:T(2,128)}, f32[256,2,1408]{2,1,0:T(2,128)}, f32[256,2,1408]{2,1,0:T(2,128)}, f32[256,2,1408]{2,1,0:T(2,128)}, f32[256,1408...) custom-call(bf16[256,1920]{1,0:T(8,128)(2,1)} %get-tuple-element.324.refs_0_.refs_3_, ...), custom_call_target="tpu_custom_call" | custom-call | bytes 13762560 | tf_op jit(solution)/shard_map/feed_step/pallas_call | solution.py:651
  363.2 9.9 %collective-permute-done.36 = bf16[128,2048]{1,0:T(8,128)(2,1)} collective-permute-done((bf16[128,2048]{1,0:T(8,128)(2,1)S(1)}, bf16[128,2048]{1,0:T(8,128)(2,1)}, u32[]{:S(2)}, u32[]{:S(2)}) %collective-permute-start.36) | collective-permute-done | bytes 524320 | tf_op jit(solution)/shard_map/ppermute | solution.py:152
  384.7 19.1 %attention_back.1 = (bf16[512,2048]{1,0:T(8,128)(2,1)}, bf16[512,2048]{1,0:T(8,128)(2,1)}) custom-call(bf16[512,2048]{1,0:T(8,128)(2,1)} %pad_maximum_fusion.2.middle_ref.rows_ref, bf16[4,2048,512]{2,1,0:T(8,128)(2,1)} %all-gather.3.cloned.1.call-done.weight_ref.exit_ref.kinds_ref, bf16[512,1536]{1,0:T(8,128)(2,1)} %get-tuple-element.344.mixed_ref, ...), custom_call_target="tpu_custom_call" | custom-call | flops 12884901888 | bytes 8388608 | tf_op jit(solution)/shard_map/attention_back/pallas_call | solution.py:405
  411.1 5.1 collective-permute-start.50
  421.2 9.8 %weight_terms.5 = (bf16[256,1024]{1,0:T(8,128)(2,1)}, bf16[256,1024]{1,0:T(8,128)(2,1)}, bf16[256,1024]{1,0:T(8,128)(2,1)}, bf16[256,1024]{1,0:T(8,128)(2,1)}, b...) custom-call(bf16[1024,512]{1,0:T(8,128)(2,1)} %get-tuple-element.250, ...), custom_call_target="tpu_custom_call" | custom-call | flops 4294967296 | bytes 12582912 | tf_op jit(solution)/shard_map/weight_terms/pallas_call | solution.py:582
  432.6 4.7 collective-permute-start.45
  437.3 6.9 %collective-permute-done.48 = bf16[128,2048]{1,0:T(8,128)(2,1)} collective-permute-done((bf16[128,2048]{1,0:T(8,128)(2,1)}, bf16[128,2048]{1,0:T(8,128)(2,1)}, u32[]{:S(2)}, u32[]{:S(2)}) %collective-permute-start.48) | collective-permute-done | bytes 524320 | tf_op jit(solution)/shard_map/ppermute | solution.py:152
  445.6 4.4 collective-permute-start.54
  453.1 12.8 %feed_step.3 = (f32[256,2,1408]{2,1,0:T(2,128)}, f32[256,2,1408]{2,1,0:T(2,128)}, f32[256,2,1408]{2,1,0:T(2,128)}, f32[256,2,1408]{2,1,0:T(2,128)}, f32[256,1408...) custom-call(bf16[256,2304]{1,0:T(8,128)(2,1)} %get-tuple-element.356, ...), custom_call_target="tpu_custom_call", output_to_operand_aliasing={{0}: (12, {}), {1}: (13, {}), {2}: (14, {}), {3}: (15, {}),... | custom-call | bytes 16515072 | tf_op jit(solution)/shard_map/feed_step/pallas_call | solution.py:651
  494.6 4.8 collective-permute-start.57
  506.8 4.6 collective-permute-start.64
  519.2 5.3 plain_step.3
  (362 shorter events, 191.1 us)
Async XLA Ops:
  7.2 87.8 %all-gather.3.cloned.1.call-start = ((), (), s32[]{:S(2)}) async-start(), calls=%async_computation | async-start | bytes 9437184 | tf_op jit(solution)/shard_map/all_gather | solution.py:736
  10.0 163.6 %all-gather.5.cloned.1.call-start = ((), (), s32[]{:S(2)}) async-start(), calls=%async_computation.1 | async-start | bytes 8847360 | tf_op jit(solution)/shard_map/all_gather | solution.py:745
  20.3 24.6 %collective-permute-start.1 = (bf16[128,2048]{1,0:T(8,128)(2,1)S(1)}, bf16[128,2048]{1,0:T(8,128)(2,1)S(1)}, u32[]{:S(2)}, u32[]{:S(2)}) collective-permute-start(bf16[128,2048]{1,0:T(8,128)(2,1)S(1)} %fusion.9), channel_id=1, source_target_pairs={{0,2},{1,3},{2,0},{3,1},{4,6},{5,7},{6,4},{7,5},{8,10},{9,11},{10,... | collective-permute-start | bytes 1572872 | tf_op jit(solution)/shard_map/ppermute | solution.py:152
  21.8 23.9 %collective-permute-start.2 = (bf16[128,2048]{1,0:T(8,128)(2,1)S(1)}, bf16[128,2048]{1,0:T(8,128)(2,1)}, u32[]{:S(2)}, u32[]{:S(2)}) collective-permute-start(bf16[128,2048]{1,0:T(8,128)(2,1)S(1)} %fusion.9), channel_id=1, source_target_pairs={{0,3},{1,2},{2,1},{3,0},{4,7},{5,6},{6,5},{7,4},{8,11},{9,10},{10,... | collective-permute-start | bytes 1572872 | tf_op jit(solution)/shard_map/ppermute | solution.py:152
  48.2 24.2 %collective-permute-start.4 = (bf16[128,2048]{1,0:T(8,128)(2,1)}, bf16[128,2048]{1,0:T(8,128)(2,1)}, u32[]{:S(2)}, u32[]{:S(2)}) collective-permute-start(bf16[128,2048]{1,0:T(8,128)(2,1)} %param.22), channel_id=1, source_target_pairs={{0,2},{1,3},{2,0},{3,1},{4,6},{5,7},{6,4},{7,5},{8,10},{9,11},{10,... | collective-permute-start | bytes 1572872 | tf_op jit(solution)/shard_map/ppermute | solution.py:152
  49.8 23.6 %collective-permute-start.5 = (bf16[128,2048]{1,0:T(8,128)(2,1)}, bf16[128,2048]{1,0:T(8,128)(2,1)S(1)}, u32[]{:S(2)}, u32[]{:S(2)}) collective-permute-start(bf16[128,2048]{1,0:T(8,128)(2,1)} %param.22), channel_id=1, source_target_pairs={{0,3},{1,2},{2,1},{3,0},{4,7},{5,6},{6,5},{7,4},{8,11},{9,10},{10,... | collective-permute-start | bytes 1572872 | tf_op jit(solution)/shard_map/ppermute | solution.py:152
  116.6 23.8 %collective-permute-start.8 = (bf16[128,2048]{1,0:T(8,128)(2,1)S(1)}, bf16[128,2048]{1,0:T(8,128)(2,1)S(1)}, u32[]{:S(2)}, u32[]{:S(2)}) collective-permute-start(bf16[128,2048]{1,0:T(8,128)(2,1)S(1)} %get-tuple-element.492), channel_id=1, source_target_pairs={{0,1},{1,0},{2,3},{3,2},{4,5},{5,4},{6,7},{7,6},{8,9},{9,8},{10,11... | collective-permute-start | bytes 1572872 | tf_op jit(solution)/shard_map/ppermute | solution.py:152
  117.1 23.3 %collective-permute-start.9 = (bf16[128,2048]{1,0:T(8,128)(2,1)S(1)}, bf16[128,2048]{1,0:T(8,128)(2,1)S(1)}, u32[]{:S(2)}, u32[]{:S(2)}) collective-permute-start(bf16[128,2048]{1,0:T(8,128)(2,1)S(1)} %get-tuple-element.494), channel_id=1, source_target_pairs={{0,2},{1,3},{2,0},{3,1},{4,6},{5,7},{6,4},{7,5},{8,10},{9,11},{10,... | collective-permute-start | bytes 1572872 | tf_op jit(solution)/shard_map/ppermute | solution.py:152
  144.5 25.1 %collective-permute-start.12 = (bf16[128,2048]{1,0:T(8,128)(2,1)}, bf16[128,2048]{1,0:T(8,128)(2,1)}, u32[]{:S(2)}, u32[]{:S(2)}) collective-permute-start(bf16[128,2048]{1,0:T(8,128)(2,1)} %add_convert_fusion.1), channel_id=1, source_target_pairs={{0,2},{1,3},{2,0},{3,1},{4,6},{5,7},{6,4},{7,5},{8,10},{9,11},{10,... | collective-permute-start | bytes 1572872 | tf_op jit(solution)/shard_map/ppermute | solution.py:152
  145.9 23.7 %collective-permute-start.13 = (bf16[128,2048]{1,0:T(8,128)(2,1)}, bf16[128,2048]{1,0:T(8,128)(2,1)}, u32[]{:S(2)}, u32[]{:S(2)}) collective-permute-start(bf16[128,2048]{1,0:T(8,128)(2,1)} %add_convert_fusion.1), channel_id=1, source_target_pairs={{0,3},{1,2},{2,1},{3,0},{4,7},{5,6},{6,5},{7,4},{8,11},{9,10},{10,... | collective-permute-start | bytes 1572872 | tf_op jit(solution)/shard_map/ppermute | solution.py:152
  173.5 27.2 %collective-permute-start.14 = (bf16[256,2304]{1,0:T(8,128)(2,1)S(1)}, bf16[256,2304]{1,0:T(8,128)(2,1)S(1)}, u32[]{:S(2)}, u32[]{:S(2)}) collective-permute-start(bf16[256,2304]{1,0:T(8,128)(2,1)S(1)} %pad_maximum_fusion.3.refs_1_), channel_id=1, source_target_pairs={{0,8},{4,12},{8,16},{12,20},{16,24},{20,28},{1,9},{5,13},{9,17},{1... | collective-permute-start | bytes 3538952 | tf_op jit(solution)/shard_map/ppermute | solution.py:84
  174.9 30.1 %collective-permute-start.15 = (bf16[256,2304]{1,0:T(8,128)(2,1)S(1)}, bf16[256,2304]{1,0:T(8,128)(2,1)S(1)}, u32[]{:S(2)}, u32[]{:S(2)}) collective-permute-start(bf16[256,2304]{1,0:T(8,128)(2,1)S(1)} %pad_maximum_fusion.3.refs_1_), channel_id=1, source_target_pairs={{8,0},{12,4},{16,8},{20,12},{24,16},{28,20},{9,1},{13,5},{17,9},{2... | collective-permute-start | bytes 3538952 | tf_op jit(solution)/shard_map/ppermute | solution.py:85
  209.3 31.0 %collective-permute-start.19 = (bf16[256,2304]{1,0:T(8,128)(2,1)S(1)}, bf16[256,2304]{1,0:T(8,128)(2,1)S(1)}, u32[]{:S(2)}, u32[]{:S(2)}) collective-permute-start(bf16[256,2304]{1,0:T(8,128)(2,1)S(1)} %collective-permute-done.15.refs_5_), channel_id=1, source_target_pairs={{8,0},{12,4},{16,8},{20,12},{9,1},{13,5},{17,9},{21,13},{10,2},{14... | collective-permute-start | bytes 3538952 | tf_op jit(solution)/shard_map/ppermute | solution.py:85
  240.3 29.0 %collective-permute-start.22 = (bf16[256,2304]{1,0:T(8,128)(2,1)S(1)}, bf16[256,2304]{1,0:T(8,128)(2,1)S(1)}, u32[]{:S(2)}, u32[]{:S(2)}) collective-permute-start(bf16[256,2304]{1,0:T(8,128)(2,1)S(1)} %collective-permute-done.18.refs_3_), channel_id=1, source_target_pairs={{16,24},{20,28},{17,25},{21,29},{18,26},{22,30},{19,27},{23,31}} | collective-permute-start | bytes 3538952 | tf_op jit(solution)/shard_map/ppermute | solution.py:84
  242.0 28.9 %collective-permute-start.23 = (bf16[256,2304]{1,0:T(8,128)(2,1)S(1)}, bf16[256,2304]{1,0:T(8,128)(2,1)S(1)}, u32[]{:S(2)}, u32[]{:S(2)}) collective-permute-start(bf16[256,2304]{1,0:T(8,128)(2,1)S(1)} %collective-permute-done.19.refs_6_), channel_id=1, source_target_pairs={{8,0},{12,4},{9,1},{13,5},{10,2},{14,6},{11,3},{15,7}} | collective-permute-start | bytes 3538952 | tf_op jit(solution)/shard_map/ppermute | solution.py:85
  244.3 25.0 %collective-permute-start.20 = (bf16[256,1920]{1,0:T(8,128)(2,1)}, bf16[256,1920]{1,0:T(8,128)(2,1)S(1)}, u32[]{:S(2)}, u32[]{:S(2)}) collective-permute-start(bf16[256,1920]{1,0:T(8,128)(2,1)} %get-tuple-element.300), channel_id=1, source_target_pairs={{0,8},{4,12},{1,9},{5,13},{2,10},{6,14},{3,11},{7,15}} | collective-permute-start | bytes 2949128 | tf_op jit(solution)/shard_map/ppermute | solution.py:145
  276.5 30.1 %collective-permute-start.24 = (bf16[256,1920]{1,0:T(8,128)(2,1)S(1)}, bf16[256,1920]{1,0:T(8,128)(2,1)S(1)}, u32[]{:S(2)}, u32[]{:S(2)}) collective-permute-start(bf16[256,1920]{1,0:T(8,128)(2,1)S(1)} %get-tuple-element.502), channel_id=1, source_target_pairs={{0,8},{4,12},{8,16},{12,20},{1,9},{5,13},{9,17},{13,21},{2,10},{6,... | collective-permute-start | bytes 2949128 | tf_op jit(solution)/shard_map/ppermute | solution.py:145
  279.2 27.4 %collective-permute-start.25 = (bf16[256,1920]{1,0:T(8,128)(2,1)S(1)}, bf16[256,1920]{1,0:T(8,128)(2,1)S(1)}, u32[]{:S(2)}, u32[]{:S(2)}) collective-permute-start(bf16[256,1920]{1,0:T(8,128)(2,1)S(1)} %get-tuple-element.501), channel_id=1, source_target_pairs={{16,8},{20,12},{24,16},{28,20},{17,9},{21,13},{25,17},{29,21},{18,... | collective-permute-start | bytes 2949128 | tf_op jit(solution)/shard_map/ppermute | solution.py:146
  307.1 33.9 %collective-permute-start.28 = (bf16[256,1920]{1,0:T(8,128)(2,1)S(1)}, bf16[256,1920]{1,0:T(8,128)(2,1)S(1)}, u32[]{:S(2)}, u32[]{:S(2)}) collective-permute-start(bf16[256,1920]{1,0:T(8,128)(2,1)S(1)} %add.364), channel_id=1, source_target_pairs={{8,0},{12,4},{16,8},{20,12},{24,16},{28,20},{9,1},{13,5},{17,9},{2... | collective-permute-start | bytes 2949128 | tf_op jit(solution)/shard_map/ppermute | solution.py:146
  308.7 32.2 %collective-permute-start.27 = (bf16[256,1920]{1,0:T(8,128)(2,1)S(1)}, bf16[256,1920]{1,0:T(8,128)(2,1)S(1)}, u32[]{:S(2)}, u32[]{:S(2)}) collective-permute-start(bf16[256,1920]{1,0:T(8,128)(2,1)S(1)} %add.363), channel_id=1, source_target_pairs={{0,8},{4,12},{8,16},{12,20},{16,24},{20,28},{1,9},{5,13},{9,17},{1... | collective-permute-start | bytes 2949128 | tf_op jit(solution)/shard_map/ppermute | solution.py:145
  316.1 24.8 %collective-permute-start.30 = (bf16[128,2048]{1,0:T(8,128)(2,1)}, bf16[128,2048]{1,0:T(8,128)(2,1)S(1)}, u32[]{:S(2)}, u32[]{:S(2)}) collective-permute-start(bf16[128,2048]{1,0:T(8,128)(2,1)} %get-tuple-element.487), channel_id=1, source_target_pairs={{0,2},{1,3},{2,0},{3,1},{4,6},{5,7},{6,4},{7,5},{8,10},{9,11},{10,... | collective-permute-start | bytes 1572872 | tf_op jit(solution)/shard_map/ppermute | solution.py:152
  344.9 31.0 %collective-permute-start.33 = (bf16[256,2304]{1,0:T(8,128)(2,1)S(1)}, bf16[256,2304]{1,0:T(8,128)(2,1)S(1)}, u32[]{:S(2)}, u32[]{:S(2)}) collective-permute-start(bf16[256,2304]{1,0:T(8,128)(2,1)S(1)} %copy-done.32), channel_id=1, source_target_pairs={{0,8},{4,12},{1,9},{5,13},{2,10},{6,14},{3,11},{7,15}} | collective-permute-start | bytes 3538952 | tf_op jit(solution)/shard_map/ppermute | solution.py:145
  347.6 28.3 %collective-permute-start.34 = (bf16[256,2304]{1,0:T(8,128)(2,1)S(1)}, bf16[256,2304]{1,0:T(8,128)(2,1)S(1)}, u32[]{:S(2)}, u32[]{:S(2)}) collective-permute-start(bf16[256,2304]{1,0:T(8,128)(2,1)S(1)} %copy-done.31), channel_id=1, source_target_pairs={{24,16},{28,20},{25,17},{29,21},{26,18},{30,22},{27,19},{31,23}} | collective-permute-start | bytes 3538952 | tf_op jit(solution)/shard_map/ppermute | solution.py:146
  349.6 23.5 %collective-permute-start.36 = (bf16[128,2048]{1,0:T(8,128)(2,1)S(1)}, bf16[128,2048]{1,0:T(8,128)(2,1)}, u32[]{:S(2)}, u32[]{:S(2)}) collective-permute-start(bf16[128,2048]{1,0:T(8,128)(2,1)S(1)} %get-tuple-element.327), channel_id=1, source_target_pairs={{0,2},{1,3},{2,0},{3,1},{4,6},{5,7},{6,4},{7,5},{8,10},{9,11},{10,... | collective-permute-start | bytes 1572872 | tf_op jit(solution)/shard_map/ppermute | solution.py:152
  377.5 26.6 %collective-permute-start.38 = (bf16[256,2304]{1,0:T(8,128)(2,1)}, bf16[256,2304]{1,0:T(8,128)(2,1)S(1)}, u32[]{:S(2)}, u32[]{:S(2)}) collective-permute-start(bf16[256,2304]{1,0:T(8,128)(2,1)} %get-tuple-element.500), channel_id=1, source_target_pairs={{0,8},{4,12},{8,16},{12,20},{1,9},{5,13},{9,17},{13,21},{2,10},{6,... | collective-permute-start | bytes 3538952 | tf_op jit(solution)/shard_map/ppermute | solution.py:145
  379.1 25.0 %collective-permute-start.39 = (bf16[256,2304]{1,0:T(8,128)(2,1)}, bf16[256,2304]{1,0:T(8,128)(2,1)S(1)}, u32[]{:S(2)}, u32[]{:S(2)}) collective-permute-start(bf16[256,2304]{1,0:T(8,128)(2,1)} %get-tuple-element.499), channel_id=1, source_target_pairs={{16,8},{20,12},{24,16},{28,20},{17,9},{21,13},{25,17},{29,21},{18,... | collective-permute-start | bytes 3538952 | tf_op jit(solution)/shard_map/ppermute | solution.py:146
  409.4 36.2 %collective-permute-start.51 = (bf16[256,2304]{1,0:T(8,128)(2,1)S(1)}, bf16[256,2304]{1,0:T(8,128)(2,1)S(1)}, u32[]{:S(2)}, u32[]{:S(2)}) collective-permute-start(bf16[256,2304]{1,0:T(8,128)(2,1)S(1)} %add.372), channel_id=1, source_target_pairs={{8,0},{12,4},{16,8},{20,12},{24,16},{28,20},{9,1},{13,5},{17,9},{2... | collective-permute-start | bytes 3538952 | tf_op jit(solution)/shard_map/ppermute | solution.py:146
  411.1 38.9 %collective-permute-start.50 = (bf16[256,2304]{1,0:T(8,128)(2,1)S(1)}, bf16[256,2304]{1,0:T(8,128)(2,1)S(1)}, u32[]{:S(2)}, u32[]{:S(2)}) collective-permute-start(bf16[256,2304]{1,0:T(8,128)(2,1)S(1)} %add.371), channel_id=1, source_target_pairs={{0,8},{4,12},{8,16},{12,20},{16,24},{20,28},{1,9},{5,13},{9,17},{1... | collective-permute-start | bytes 3538952 | tf_op jit(solution)/shard_map/ppermute | solution.py:145
  418.9 25.3 %collective-permute-start.48 = (bf16[128,2048]{1,0:T(8,128)(2,1)}, bf16[128,2048]{1,0:T(8,128)(2,1)}, u32[]{:S(2)}, u32[]{:S(2)}) collective-permute-start(bf16[128,2048]{1,0:T(8,128)(2,1)} %get-tuple-element.477), channel_id=1, source_target_pairs={{0,2},{1,3},{2,0},{3,1},{4,6},{5,7},{6,4},{7,5},{8,10},{9,11},{10,... | collective-permute-start | bytes 1572872 | tf_op jit(solution)/shard_map/ppermute | solution.py:152
  419.9 46.0 %collective-permute-start.49 = (bf16[128,2048]{1,0:T(8,128)(2,1)}, bf16[128,2048]{1,0:T(8,128)(2,1)}, u32[]{:S(2)}, u32[]{:S(2)}) collective-permute-start(bf16[128,2048]{1,0:T(8,128)(2,1)} %get-tuple-element.476), channel_id=1, source_target_pairs={{0,3},{1,2},{2,1},{3,0},{4,7},{5,6},{6,5},{7,4},{8,11},{9,10},{10,... | collective-permute-start | bytes 1572872 | tf_op jit(solution)/shard_map/ppermute | solution.py:152
  432.6 33.3 %collective-permute-start.45 = (bf16[256,1024]{1,0:T(8,128)(2,1)}, bf16[256,1024]{1,0:T(8,128)(2,1)}, u32[]{:S(2)}, u32[]{:S(2)}) collective-permute-start(bf16[256,1024]{1,0:T(8,128)(2,1)} %get-tuple-element.397), channel_id=1, source_target_pairs={{0,8},{4,12},{1,9},{5,13},{2,10},{6,14},{3,11},{7,15}} | collective-permute-start | bytes 1572872 | tf_op jit(solution)/shard_map/ppermute | solution.py:145
  475.8 23.6 %collective-permute-start.59 = (bf16[256,1024]{1,0:T(8,128)(2,1)}, bf16[256,1024]{1,0:T(8,128)(2,1)}, u32[]{:S(2)}, u32[]{:S(2)}) collective-permute-start(bf16[256,1024]{1,0:T(8,128)(2,1)} %get-tuple-element.504), channel_id=1, source_target_pairs={{0,8},{4,12},{8,16},{12,20},{1,9},{5,13},{9,17},{13,21},{2,10},{6,... | collective-permute-start | bytes 1572872 | tf_op jit(solution)/shard_map/ppermute | solution.py:145
  (104 other events, 1390.5 us)
Sparse Core Ops, SparseCore 0:
  10.2 84.7 all-gather.2
  97.2 76.2 all-gather.4

commit v6 on v5

--- a/solution.py
+++ b/solution.py
@@ -446,7 +446,7 @@
     def _():
         for load in loads(2 * padded, padded, 0):
             load.start()
-        for p in range(pairs):
+        for p in range(min(2, pairs)):
             for load in loads(p * 256, 256, p + 1):
                 load.start()
         if pieces > 1:
@@ -456,6 +456,9 @@
                 cot_ref[:, b * size : (b + 1) * size] = cot_in[:, there]
         for load in loads(2 * padded, padded, 0):
             load.wait()
+        for p in range(2, pairs):
+            for load in loads(p * 256, 256, p + 1):
+                load.start()
         for low in range(0, padded, 256):
             high = min(low + 256, padded)
             hidden_grad_ref[:, low:high] = matmul(

time: 550 us -> 550 us (level)
  no operation moved by 1% of the time
where the time goes in v6:
time: 550 us; the launch traced here: 541 us
  waiting for transfers between devices  181 us (33%)
  Pallas kernels  153 us (28%)
  starting transfers between devices  106 us (19%)
  other arithmetic  41 us (7%)
  local copies, waits for them, and re-layouts  40.8 us (7%)
  between operations  15.7 us (3%)
    ppermute x24, waiting for transfers between devices, swap_rows(): lax.ppermute(array, 'tensor', [(t, t ^ offset) for t in range(count)])  114 us
    ppermute x12, starting transfers between devices, scatter_step(): up = lax.ppermute(up_send, 'dp', pairs_up(lines, 0, lines - j, 1))  45.5 us
    pallas_call x2, Pallas kernels, feed(): pl.pallas_call(lambda *refs: feed_kernel(pieces, *refs), grid_spec=pltpu....  45.4 us
    pallas_call x3, Pallas kernels, weight_terms(): kernel_call(lambda *refs: terms_kernel(split, groups, *refs), (columns //...  29.7 us
    ppermute x24, starting transfers between devices, swap_rows(): lax.ppermute(array, 'tensor', [(t, t ^ offset) for t in range(count)])  29.3 us
    ppermute x3, waiting for transfers between devices, gather_step(): down = lax.ppermute(downs[-1], 'dp', pairs_up(lines, 1, lines - s + 1, -1))  24.6 us
    pallas_call x2, Pallas kernels, feed_step(): pl.pallas_call(feed_step_kernel, grid=(blocks,), in_specs=[pair] * 3 + [s...  23.9 us
    ppermute x12, waiting for transfers between devices, scatter_step(): up = lax.ppermute(up_send, 'dp', pairs_up(lines, 0, lines - j, 1))  19.6 us
  transfers between devices with their start and end apart: 69, of which 27 were waited for; matrix products, arithmetic and copies ran while one was open for 11% of the time, Pallas kernels for 27%

profile of v6, /device:TPU:0, one launch (start us, length us, event | category | flops | bytes accessed | tf_op | source)
XLA Modules:
  0.0 540.6 jit_solution(3333775158595424486)
XLA Ops:
  22.2 10.9 %collective-permute-done = bf16[128,2048]{1,0:T(8,128)(2,1)S(1)} collective-permute-done((bf16[128,2048]{1,0:T(8,128)(2,1)S(1)}, bf16[128,2048]{1,0:T(8,128)(2,1)S(1)}, u32[]{:S(2)}, u32[]{:S(2)}) %collective-permute-start) | collective-permute-done | bytes 524320 | tf_op jit(solution)/shard_map/ppermute | solution.py:152
  33.1 11.9 %collective-permute-done.1 = bf16[128,2048]{1,0:T(8,128)(2,1)S(1)} collective-permute-done((bf16[128,2048]{1,0:T(8,128)(2,1)S(1)}, bf16[128,2048]{1,0:T(8,128)(2,1)S(1)}, u32[]{:S(2)}, u32[]{:S(2)}) %collective-permute-start.1) | collective-permute-done | bytes 524320 | tf_op jit(solution)/shard_map/ppermute | solution.py:152
  52.4 10.3 %collective-permute-done.3 = bf16[128,2048]{1,0:T(8,128)(2,1)} collective-permute-done((bf16[128,2048]{1,0:T(8,128)(2,1)}, bf16[128,2048]{1,0:T(8,128)(2,1)}, u32[]{:S(2)}, u32[]{:S(2)}) %collective-permute-start.3) | collective-permute-done | bytes 524320 | tf_op jit(solution)/shard_map/ppermute | solution.py:152
  63.8 8.5 %collective-permute-done.4 = bf16[128,2048]{1,0:T(8,128)(2,1)} collective-permute-done((bf16[128,2048]{1,0:T(8,128)(2,1)}, bf16[128,2048]{1,0:T(8,128)(2,1)}, u32[]{:S(2)}, u32[]{:S(2)}) %collective-permute-start.4) | collective-permute-done | bytes 524320 | tf_op jit(solution)/shard_map/ppermute | solution.py:152
  86.5 8.5 %all-gather.3.cloned.1.call-done.weight_ref.exit_ref.kinds_ref = bf16[4,2048,512]{2,1,0:T(8,128)(2,1)} async-done(((bf16[4,256,512]{2,1,0:T(8,128)(2,1)}), bf16[4,2048,512]{2,1,0:T(8,128)(2,1)}) %all-gather.3.cloned.1.call-update) | async-done | bytes 8388624 | tf_op jit(solution)/shard_map/all_gather | solution.py:739
  95.9 15.0 %attention.1 = (bf16[512,1536]{1,0:T(8,128)(2,1)}, bf16[512,512]{1,0:T(8,128)(2,1)}, f32[512,128]{1,0:T(8,128)}) custom-call(bf16[512,2048]{1,0:T(8,128)(2,1)} %copy-done, bf16[4,2048,512]{2,1,0:T(8,128)(2,1)} %all-gather.3.cloned.1.call-done.weight_ref.exit_ref.kinds_ref, f32[3,1,512]{2,1,0:T(1,128)} %reshape.257.offset_ref, ...), custom_call_target="tpu_custom_call" | custom-call | flops 12884901888 | bytes 8388608 | tf_op jit(solution)/shard_map/attention/pallas_call | solution.py:312
  117.6 12.2 %collective-permute-done.10 = bf16[128,2048]{1,0:T(8,128)(2,1)S(1)} collective-permute-done((bf16[128,2048]{1,0:T(8,128)(2,1)S(1)}, bf16[128,2048]{1,0:T(8,128)(2,1)S(1)}, u32[]{:S(2)}, u32[]{:S(2)}) %collective-permute-start.10) | collective-permute-done | bytes 524320 | tf_op jit(solution)/shard_map/ppermute | solution.py:152
  129.9 10.6 %collective-permute-done.8 = bf16[128,2048]{1,0:T(8,128)(2,1)S(1)} collective-permute-done((bf16[128,2048]{1,0:T(8,128)(2,1)S(1)}, bf16[128,2048]{1,0:T(8,128)(2,1)S(1)}, u32[]{:S(2)}, u32[]{:S(2)}) %collective-permute-start.8) | collective-permute-done | bytes 524320 | tf_op jit(solution)/shard_map/ppermute | solution.py:152
  150.5 7.6 %collective-permute-done.11 = bf16[128,2048]{1,0:T(8,128)(2,1)} collective-permute-done((bf16[128,2048]{1,0:T(8,128)(2,1)}, bf16[128,2048]{1,0:T(8,128)(2,1)}, u32[]{:S(2)}, u32[]{:S(2)}) %collective-permute-start.11) | collective-permute-done | bytes 524320 | tf_op jit(solution)/shard_map/ppermute | solution.py:152
  158.1 11.5 %collective-permute-done.12 = bf16[128,2048]{1,0:T(8,128)(2,1)} collective-permute-done((bf16[128,2048]{1,0:T(8,128)(2,1)}, bf16[128,2048]{1,0:T(8,128)(2,1)}, u32[]{:S(2)}, u32[]{:S(2)}) %collective-permute-start.12) | collective-permute-done | bytes 524320 | tf_op jit(solution)/shard_map/ppermute | solution.py:152
  176.7 21.2 %feed_forward.2 = (bf16[512,1920]{1,0:T(8,128)(2,1)}, bf16[512,2048]{1,0:T(8,128)(2,1)}, bf16[512,2048]{1,0:T(8,128)(2,1)}) custom-call(s32[8]{0:T(128)} %iota.35.refs_0_, bf16[512,2048]{1,0:T(8,128)(2,1)} %pad_maximum_fusion.1.refs_1_.rows_ref, bf16[512,2048]{1,0:T(8,128)(2,1)} %copy-done.4, bf16[2048,1920]{1,0:T(8,128)(2,1)} %all-gather.5.cloned.1.call-done.refs_3_), custom_call_target="tpu_custom_call" | custom-call | flops 16106127360 | bytes 32505856 | tf_op jit(solution)/shard_map/feed_forward/pallas_call | solution.py:508
  200.7 4.3 collective-permute-done.15.refs_5_
  211.8 9.8 %weight_terms.3 = (bf16[256,1920]{1,0:T(8,128)(2,1)}, bf16[256,1920]{1,0:T(8,128)(2,1)}, bf16[256,1920]{1,0:T(8,128)(2,1)}, bf16[256,1920]{1,0:T(8,128)(2,1)}) custom-call(bf16[1024,512]{1,0:T(8,128)(2,1)} %get-tuple-element.491.refs_0_, bf16[1024,512]{1,0:T(8,128)(2,1)} %copy-done.63, bf16[1024,512]{1,0:T(8,128)(2,1)} %get-tuple-element.262.refs_2_, ...), custom_call_target="tpu_custom_call" | custom-call | flops 4026531840 | bytes 12058624 | tf_op jit(solution)/shard_map/weight_terms/pallas_call | solution.py:585
  221.6 18.7 %collective-permute-done.19.refs_6_ = bf16[256,2304]{1,0:T(8,128)(2,1)S(1)} collective-permute-done((bf16[256,2304]{1,0:T(8,128)(2,1)S(1)}, bf16[256,2304]{1,0:T(8,128)(2,1)S(1)}, u32[]{:S(2)}, u32[]{:S(2)}) %collective-permute-start.19) | collective-permute-done | bytes 1179680 | tf_op jit(solution)/shard_map/ppermute | solution.py:85
  244.3 4.7 collective-permute-start.20
  249.8 19.6 %collective-permute-done.20 = bf16[256,1920]{1,0:T(8,128)(2,1)S(1)} collective-permute-done((bf16[256,1920]{1,0:T(8,128)(2,1)}, bf16[256,1920]{1,0:T(8,128)(2,1)S(1)}, u32[]{:S(2)}, u32[]{:S(2)}) %collective-permute-start.20) | collective-permute-done | bytes 983072 | tf_op jit(solution)/shard_map/ppermute | solution.py:145
  282.4 24.2 %feed_forward.3 = (bf16[512,2304]{1,0:T(8,128)(2,1)}, bf16[512,2048]{1,0:T(8,128)(2,1)}, bf16[512,2048]{1,0:T(8,128)(2,1)}) custom-call(s32[8]{0:T(128)} %copy-done.9, bf16[512,2048]{1,0:T(8,128)(2,1)} %pad_maximum_fusion.1.refs_1_.rows_ref, bf16[512,2048]{1,0:T(8,128)(2,1)} %copy-done.4, bf16[1024,2304]{1,0:T(8,128)(2,1)} %copy-done.3, ...), custom_call_target="tpu_custom_call" | custom-call | flops 19327352832 | bytes 35651584 | tf_op jit(solution)/shard_map/feed_forward/pallas_call | solution.py:508
  308.7 4.6 collective-permute-start.27
  319.4 10.1 %weight_terms.4 = (bf16[256,2304]{1,0:T(8,128)(2,1)}, bf16[256,2304]{1,0:T(8,128)(2,1)}, bf16[256,2304]{1,0:T(8,128)(2,1)}, bf16[256,2304]{1,0:T(8,128)(2,1)}) custom-call(bf16[1024,512]{1,0:T(8,128)(2,1)} %get-tuple-element.491.refs_0_, bf16[1024,512]{1,0:T(8,128)(2,1)} %copy-done.63, bf16[1024,512]{1,0:T(8,128)(2,1)} %get-tuple-element.262.refs_2_, ...), custom_call_target="tpu_custom_call" | custom-call | flops 4831838208 | bytes 13631488 | tf_op jit(solution)/shard_map/weight_terms/pallas_call | solution.py:585
  329.6 11.4 %collective-permute-done.30 = bf16[128,2048]{1,0:T(8,128)(2,1)S(1)} collective-permute-done((bf16[128,2048]{1,0:T(8,128)(2,1)}, bf16[128,2048]{1,0:T(8,128)(2,1)S(1)}, u32[]{:S(2)}, u32[]{:S(2)}) %collective-permute-start.30) | collective-permute-done | bytes 524320 | tf_op jit(solution)/shard_map/ppermute | solution.py:152
  351.9 11.0 %feed_step.2 = (f32[256,2,1408]{2,1,0:T(2,128)}, f32[256,2,1408]{2,1,0:T(2,128)}, f32[256,2,1408]{2,1,0:T(2,128)}, f32[256,2,1408]{2,1,0:T(2,128)}, f32[256,1408...) custom-call(bf16[256,1920]{1,0:T(8,128)(2,1)} %get-tuple-element.324.refs_0_.refs_3_, ...), custom_call_target="tpu_custom_call" | custom-call | bytes 13762560 | tf_op jit(solution)/shard_map/feed_step/pallas_call | solution.py:654
  363.3 9.9 %collective-permute-done.36 = bf16[128,2048]{1,0:T(8,128)(2,1)} collective-permute-done((bf16[128,2048]{1,0:T(8,128)(2,1)S(1)}, bf16[128,2048]{1,0:T(8,128)(2,1)}, u32[]{:S(2)}, u32[]{:S(2)}) %collective-permute-start.36) | collective-permute-done | bytes 524320 | tf_op jit(solution)/shard_map/ppermute | solution.py:152
  384.7 19.1 %attention_back.1 = (bf16[512,2048]{1,0:T(8,128)(2,1)}, bf16[512,2048]{1,0:T(8,128)(2,1)}) custom-call(bf16[512,2048]{1,0:T(8,128)(2,1)} %pad_maximum_fusion.2.middle_ref.rows_ref, bf16[4,2048,512]{2,1,0:T(8,128)(2,1)} %all-gather.3.cloned.1.call-done.weight_ref.exit_ref.kinds_ref, bf16[512,1536]{1,0:T(8,128)(2,1)} %get-tuple-element.344.mixed_ref, ...), custom_call_target="tpu_custom_call" | custom-call | flops 12884901888 | bytes 8388608 | tf_op jit(solution)/shard_map/attention_back/pallas_call | solution.py:405
  411.1 5.1 collective-permute-start.50
  421.3 9.8 %weight_terms.5 = (bf16[256,1024]{1,0:T(8,128)(2,1)}, bf16[256,1024]{1,0:T(8,128)(2,1)}, bf16[256,1024]{1,0:T(8,128)(2,1)}, bf16[256,1024]{1,0:T(8,128)(2,1)}, b...) custom-call(bf16[1024,512]{1,0:T(8,128)(2,1)} %get-tuple-element.250, ...), custom_call_target="tpu_custom_call" | custom-call | flops 4294967296 | bytes 12582912 | tf_op jit(solution)/shard_map/weight_terms/pallas_call | solution.py:585
  432.7 4.7 collective-permute-start.45
  437.3 6.9 %collective-permute-done.48 = bf16[128,2048]{1,0:T(8,128)(2,1)} collective-permute-done((bf16[128,2048]{1,0:T(8,128)(2,1)}, bf16[128,2048]{1,0:T(8,128)(2,1)}, u32[]{:S(2)}, u32[]{:S(2)}) %collective-permute-start.48) | collective-permute-done | bytes 524320 | tf_op jit(solution)/shard_map/ppermute | solution.py:152
  445.7 4.4 collective-permute-start.54
  453.1 12.8 %feed_step.3 = (f32[256,2,1408]{2,1,0:T(2,128)}, f32[256,2,1408]{2,1,0:T(2,128)}, f32[256,2,1408]{2,1,0:T(2,128)}, f32[256,2,1408]{2,1,0:T(2,128)}, f32[256,1408...) custom-call(bf16[256,2304]{1,0:T(8,128)(2,1)} %get-tuple-element.356, ...), custom_call_target="tpu_custom_call", output_to_operand_aliasing={{0}: (12, {}), {1}: (13, {}), {2}: (14, {}), {3}: (15, {}),... | custom-call | bytes 16515072 | tf_op jit(solution)/shard_map/feed_step/pallas_call | solution.py:654
  494.7 4.8 collective-permute-start.57
  506.8 4.6 collective-permute-start.64
  519.3 5.3 plain_step.3
  (362 shorter events, 191.1 us)
Async XLA Ops:
  7.2 87.8 %all-gather.3.cloned.1.call-start = ((), (), s32[]{:S(2)}) async-start(), calls=%async_computation | async-start | bytes 9437184 | tf_op jit(solution)/shard_map/all_gather | solution.py:739
  10.0 163.6 %all-gather.5.cloned.1.call-start = ((), (), s32[]{:S(2)}) async-start(), calls=%async_computation.1 | async-start | bytes 8847360 | tf_op jit(solution)/shard_map/all_gather | solution.py:748
  20.3 24.6 %collective-permute-start.1 = (bf16[128,2048]{1,0:T(8,128)(2,1)S(1)}, bf16[128,2048]{1,0:T(8,128)(2,1)S(1)}, u32[]{:S(2)}, u32[]{:S(2)}) collective-permute-start(bf16[128,2048]{1,0:T(8,128)(2,1)S(1)} %fusion.9), channel_id=1, source_target_pairs={{0,2},{1,3},{2,0},{3,1},{4,6},{5,7},{6,4},{7,5},{8,10},{9,11},{10,... | collective-permute-start | bytes 1572872 | tf_op jit(solution)/shard_map/ppermute | solution.py:152
  21.8 23.9 %collective-permute-start.2 = (bf16[128,2048]{1,0:T(8,128)(2,1)S(1)}, bf16[128,2048]{1,0:T(8,128)(2,1)}, u32[]{:S(2)}, u32[]{:S(2)}) collective-permute-start(bf16[128,2048]{1,0:T(8,128)(2,1)S(1)} %fusion.9), channel_id=1, source_target_pairs={{0,3},{1,2},{2,1},{3,0},{4,7},{5,6},{6,5},{7,4},{8,11},{9,10},{10,... | collective-permute-start | bytes 1572872 | tf_op jit(solution)/shard_map/ppermute | solution.py:152
  48.2 24.2 %collective-permute-start.4 = (bf16[128,2048]{1,0:T(8,128)(2,1)}, bf16[128,2048]{1,0:T(8,128)(2,1)}, u32[]{:S(2)}, u32[]{:S(2)}) collective-permute-start(bf16[128,2048]{1,0:T(8,128)(2,1)} %param.22), channel_id=1, source_target_pairs={{0,2},{1,3},{2,0},{3,1},{4,6},{5,7},{6,4},{7,5},{8,10},{9,11},{10,... | collective-permute-start | bytes 1572872 | tf_op jit(solution)/shard_map/ppermute | solution.py:152
  49.8 23.6 %collective-permute-start.5 = (bf16[128,2048]{1,0:T(8,128)(2,1)}, bf16[128,2048]{1,0:T(8,128)(2,1)S(1)}, u32[]{:S(2)}, u32[]{:S(2)}) collective-permute-start(bf16[128,2048]{1,0:T(8,128)(2,1)} %param.22), channel_id=1, source_target_pairs={{0,3},{1,2},{2,1},{3,0},{4,7},{5,6},{6,5},{7,4},{8,11},{9,10},{10,... | collective-permute-start | bytes 1572872 | tf_op jit(solution)/shard_map/ppermute | solution.py:152
  116.6 23.8 %collective-permute-start.8 = (bf16[128,2048]{1,0:T(8,128)(2,1)S(1)}, bf16[128,2048]{1,0:T(8,128)(2,1)S(1)}, u32[]{:S(2)}, u32[]{:S(2)}) collective-permute-start(bf16[128,2048]{1,0:T(8,128)(2,1)S(1)} %get-tuple-element.492), channel_id=1, source_target_pairs={{0,1},{1,0},{2,3},{3,2},{4,5},{5,4},{6,7},{7,6},{8,9},{9,8},{10,11... | collective-permute-start | bytes 1572872 | tf_op jit(solution)/shard_map/ppermute | solution.py:152
  117.1 23.3 %collective-permute-start.9 = (bf16[128,2048]{1,0:T(8,128)(2,1)S(1)}, bf16[128,2048]{1,0:T(8,128)(2,1)S(1)}, u32[]{:S(2)}, u32[]{:S(2)}) collective-permute-start(bf16[128,2048]{1,0:T(8,128)(2,1)S(1)} %get-tuple-element.494), channel_id=1, source_target_pairs={{0,2},{1,3},{2,0},{3,1},{4,6},{5,7},{6,4},{7,5},{8,10},{9,11},{10,... | collective-permute-start | bytes 1572872 | tf_op jit(solution)/shard_map/ppermute | solution.py:152
  144.5 25.1 %collective-permute-start.12 = (bf16[128,2048]{1,0:T(8,128)(2,1)}, bf16[128,2048]{1,0:T(8,128)(2,1)}, u32[]{:S(2)}, u32[]{:S(2)}) collective-permute-start(bf16[128,2048]{1,0:T(8,128)(2,1)} %add_convert_fusion.1), channel_id=1, source_target_pairs={{0,2},{1,3},{2,0},{3,1},{4,6},{5,7},{6,4},{7,5},{8,10},{9,11},{10,... | collective-permute-start | bytes 1572872 | tf_op jit(solution)/shard_map/ppermute | solution.py:152
  145.9 23.7 %collective-permute-start.13 = (bf16[128,2048]{1,0:T(8,128)(2,1)}, bf16[128,2048]{1,0:T(8,128)(2,1)}, u32[]{:S(2)}, u32[]{:S(2)}) collective-permute-start(bf16[128,2048]{1,0:T(8,128)(2,1)} %add_convert_fusion.1), channel_id=1, source_target_pairs={{0,3},{1,2},{2,1},{3,0},{4,7},{5,6},{6,5},{7,4},{8,11},{9,10},{10,... | collective-permute-start | bytes 1572872 | tf_op jit(solution)/shard_map/ppermute | solution.py:152
  173.5 27.2 %collective-permute-start.14 = (bf16[256,2304]{1,0:T(8,128)(2,1)S(1)}, bf16[256,2304]{1,0:T(8,128)(2,1)S(1)}, u32[]{:S(2)}, u32[]{:S(2)}) collective-permute-start(bf16[256,2304]{1,0:T(8,128)(2,1)S(1)} %pad_maximum_fusion.3.refs_1_), channel_id=1, source_target_pairs={{0,8},{4,12},{8,16},{12,20},{16,24},{20,28},{1,9},{5,13},{9,17},{1... | collective-permute-start | bytes 3538952 | tf_op jit(solution)/shard_map/ppermute | solution.py:84
  174.9 30.1 %collective-permute-start.15 = (bf16[256,2304]{1,0:T(8,128)(2,1)S(1)}, bf16[256,2304]{1,0:T(8,128)(2,1)S(1)}, u32[]{:S(2)}, u32[]{:S(2)}) collective-permute-start(bf16[256,2304]{1,0:T(8,128)(2,1)S(1)} %pad_maximum_fusion.3.refs_1_), channel_id=1, source_target_pairs={{8,0},{12,4},{16,8},{20,12},{24,16},{28,20},{9,1},{13,5},{17,9},{2... | collective-permute-start | bytes 3538952 | tf_op jit(solution)/shard_map/ppermute | solution.py:85
  209.3 31.0 %collective-permute-start.19 = (bf16[256,2304]{1,0:T(8,128)(2,1)S(1)}, bf16[256,2304]{1,0:T(8,128)(2,1)S(1)}, u32[]{:S(2)}, u32[]{:S(2)}) collective-permute-start(bf16[256,2304]{1,0:T(8,128)(2,1)S(1)} %collective-permute-done.15.refs_5_), channel_id=1, source_target_pairs={{8,0},{12,4},{16,8},{20,12},{9,1},{13,5},{17,9},{21,13},{10,2},{14... | collective-permute-start | bytes 3538952 | tf_op jit(solution)/shard_map/ppermute | solution.py:85
  240.3 29.0 %collective-permute-start.22 = (bf16[256,2304]{1,0:T(8,128)(2,1)S(1)}, bf16[256,2304]{1,0:T(8,128)(2,1)S(1)}, u32[]{:S(2)}, u32[]{:S(2)}) collective-permute-start(bf16[256,2304]{1,0:T(8,128)(2,1)S(1)} %collective-permute-done.18.refs_3_), channel_id=1, source_target_pairs={{16,24},{20,28},{17,25},{21,29},{18,26},{22,30},{19,27},{23,31}} | collective-permute-start | bytes 3538952 | tf_op jit(solution)/shard_map/ppermute | solution.py:84
  242.0 28.9 %collective-permute-start.23 = (bf16[256,2304]{1,0:T(8,128)(2,1)S(1)}, bf16[256,2304]{1,0:T(8,128)(2,1)S(1)}, u32[]{:S(2)}, u32[]{:S(2)}) collective-permute-start(bf16[256,2304]{1,0:T(8,128)(2,1)S(1)} %collective-permute-done.19.refs_6_), channel_id=1, source_target_pairs={{8,0},{12,4},{9,1},{13,5},{10,2},{14,6},{11,3},{15,7}} | collective-permute-start | bytes 3538952 | tf_op jit(solution)/shard_map/ppermute | solution.py:85
  244.3 25.0 %collective-permute-start.20 = (bf16[256,1920]{1,0:T(8,128)(2,1)}, bf16[256,1920]{1,0:T(8,128)(2,1)S(1)}, u32[]{:S(2)}, u32[]{:S(2)}) collective-permute-start(bf16[256,1920]{1,0:T(8,128)(2,1)} %get-tuple-element.300), channel_id=1, source_target_pairs={{0,8},{4,12},{1,9},{5,13},{2,10},{6,14},{3,11},{7,15}} | collective-permute-start | bytes 2949128 | tf_op jit(solution)/shard_map/ppermute | solution.py:145
  276.5 30.1 %collective-permute-start.24 = (bf16[256,1920]{1,0:T(8,128)(2,1)S(1)}, bf16[256,1920]{1,0:T(8,128)(2,1)S(1)}, u32[]{:S(2)}, u32[]{:S(2)}) collective-permute-start(bf16[256,1920]{1,0:T(8,128)(2,1)S(1)} %get-tuple-element.502), channel_id=1, source_target_pairs={{0,8},{4,12},{8,16},{12,20},{1,9},{5,13},{9,17},{13,21},{2,10},{6,... | collective-permute-start | bytes 2949128 | tf_op jit(solution)/shard_map/ppermute | solution.py:145
  279.2 27.4 %collective-permute-start.25 = (bf16[256,1920]{1,0:T(8,128)(2,1)S(1)}, bf16[256,1920]{1,0:T(8,128)(2,1)S(1)}, u32[]{:S(2)}, u32[]{:S(2)}) collective-permute-start(bf16[256,1920]{1,0:T(8,128)(2,1)S(1)} %get-tuple-element.501), channel_id=1, source_target_pairs={{16,8},{20,12},{24,16},{28,20},{17,9},{21,13},{25,17},{29,21},{18,... | collective-permute-start | bytes 2949128 | tf_op jit(solution)/shard_map/ppermute | solution.py:146
  307.1 33.9 %collective-permute-start.28 = (bf16[256,1920]{1,0:T(8,128)(2,1)S(1)}, bf16[256,1920]{1,0:T(8,128)(2,1)S(1)}, u32[]{:S(2)}, u32[]{:S(2)}) collective-permute-start(bf16[256,1920]{1,0:T(8,128)(2,1)S(1)} %add.364), channel_id=1, source_target_pairs={{8,0},{12,4},{16,8},{20,12},{24,16},{28,20},{9,1},{13,5},{17,9},{2... | collective-permute-start | bytes 2949128 | tf_op jit(solution)/shard_map/ppermute | solution.py:146
  308.7 32.2 %collective-permute-start.27 = (bf16[256,1920]{1,0:T(8,128)(2,1)S(1)}, bf16[256,1920]{1,0:T(8,128)(2,1)S(1)}, u32[]{:S(2)}, u32[]{:S(2)}) collective-permute-start(bf16[256,1920]{1,0:T(8,128)(2,1)S(1)} %add.363), channel_id=1, source_target_pairs={{0,8},{4,12},{8,16},{12,20},{16,24},{20,28},{1,9},{5,13},{9,17},{1... | collective-permute-start | bytes 2949128 | tf_op jit(solution)/shard_map/ppermute | solution.py:145
  316.1 24.8 %collective-permute-start.30 = (bf16[128,2048]{1,0:T(8,128)(2,1)}, bf16[128,2048]{1,0:T(8,128)(2,1)S(1)}, u32[]{:S(2)}, u32[]{:S(2)}) collective-permute-start(bf16[128,2048]{1,0:T(8,128)(2,1)} %get-tuple-element.487), channel_id=1, source_target_pairs={{0,2},{1,3},{2,0},{3,1},{4,6},{5,7},{6,4},{7,5},{8,10},{9,11},{10,... | collective-permute-start | bytes 1572872 | tf_op jit(solution)/shard_map/ppermute | solution.py:152
  344.9 31.0 %collective-permute-start.33 = (bf16[256,2304]{1,0:T(8,128)(2,1)S(1)}, bf16[256,2304]{1,0:T(8,128)(2,1)S(1)}, u32[]{:S(2)}, u32[]{:S(2)}) collective-permute-start(bf16[256,2304]{1,0:T(8,128)(2,1)S(1)} %copy-done.32), channel_id=1, source_target_pairs={{0,8},{4,12},{1,9},{5,13},{2,10},{6,14},{3,11},{7,15}} | collective-permute-start | bytes 3538952 | tf_op jit(solution)/shard_map/ppermute | solution.py:145
  347.6 28.3 %collective-permute-start.34 = (bf16[256,2304]{1,0:T(8,128)(2,1)S(1)}, bf16[256,2304]{1,0:T(8,128)(2,1)S(1)}, u32[]{:S(2)}, u32[]{:S(2)}) collective-permute-start(bf16[256,2304]{1,0:T(8,128)(2,1)S(1)} %copy-done.31), channel_id=1, source_target_pairs={{24,16},{28,20},{25,17},{29,21},{26,18},{30,22},{27,19},{31,23}} | collective-permute-start | bytes 3538952 | tf_op jit(solution)/shard_map/ppermute | solution.py:146
  349.6 23.5 %collective-permute-start.36 = (bf16[128,2048]{1,0:T(8,128)(2,1)S(1)}, bf16[128,2048]{1,0:T(8,128)(2,1)}, u32[]{:S(2)}, u32[]{:S(2)}) collective-permute-start(bf16[128,2048]{1,0:T(8,128)(2,1)S(1)} %get-tuple-element.327), channel_id=1, source_target_pairs={{0,2},{1,3},{2,0},{3,1},{4,6},{5,7},{6,4},{7,5},{8,10},{9,11},{10,... | collective-permute-start | bytes 1572872 | tf_op jit(solution)/shard_map/ppermute | solution.py:152
  377.5 26.6 %collective-permute-start.38 = (bf16[256,2304]{1,0:T(8,128)(2,1)}, bf16[256,2304]{1,0:T(8,128)(2,1)S(1)}, u32[]{:S(2)}, u32[]{:S(2)}) collective-permute-start(bf16[256,2304]{1,0:T(8,128)(2,1)} %get-tuple-element.500), channel_id=1, source_target_pairs={{0,8},{4,12},{8,16},{12,20},{1,9},{5,13},{9,17},{13,21},{2,10},{6,... | collective-permute-start | bytes 3538952 | tf_op jit(solution)/shard_map/ppermute | solution.py:145
  379.1 25.0 %collective-permute-start.39 = (bf16[256,2304]{1,0:T(8,128)(2,1)}, bf16[256,2304]{1,0:T(8,128)(2,1)S(1)}, u32[]{:S(2)}, u32[]{:S(2)}) collective-permute-start(bf16[256,2304]{1,0:T(8,128)(2,1)} %get-tuple-element.499), channel_id=1, source_target_pairs={{16,8},{20,12},{24,16},{28,20},{17,9},{21,13},{25,17},{29,21},{18,... | collective-permute-start | bytes 3538952 | tf_op jit(solution)/shard_map/ppermute | solution.py:146
  409.4 36.3 %collective-permute-start.51 = (bf16[256,2304]{1,0:T(8,128)(2,1)S(1)}, bf16[256,2304]{1,0:T(8,128)(2,1)S(1)}, u32[]{:S(2)}, u32[]{:S(2)}) collective-permute-start(bf16[256,2304]{1,0:T(8,128)(2,1)S(1)} %add.372), channel_id=1, source_target_pairs={{8,0},{12,4},{16,8},{20,12},{24,16},{28,20},{9,1},{13,5},{17,9},{2... | collective-permute-start | bytes 3538952 | tf_op jit(solution)/shard_map/ppermute | solution.py:146
  411.1 38.9 %collective-permute-start.50 = (bf16[256,2304]{1,0:T(8,128)(2,1)S(1)}, bf16[256,2304]{1,0:T(8,128)(2,1)S(1)}, u32[]{:S(2)}, u32[]{:S(2)}) collective-permute-start(bf16[256,2304]{1,0:T(8,128)(2,1)S(1)} %add.371), channel_id=1, source_target_pairs={{0,8},{4,12},{8,16},{12,20},{16,24},{20,28},{1,9},{5,13},{9,17},{1... | collective-permute-start | bytes 3538952 | tf_op jit(solution)/shard_map/ppermute | solution.py:145
  418.9 25.3 %collective-permute-start.48 = (bf16[128,2048]{1,0:T(8,128)(2,1)}, bf16[128,2048]{1,0:T(8,128)(2,1)}, u32[]{:S(2)}, u32[]{:S(2)}) collective-permute-start(bf16[128,2048]{1,0:T(8,128)(2,1)} %get-tuple-element.477), channel_id=1, source_target_pairs={{0,2},{1,3},{2,0},{3,1},{4,6},{5,7},{6,4},{7,5},{8,10},{9,11},{10,... | collective-permute-start | bytes 1572872 | tf_op jit(solution)/shard_map/ppermute | solution.py:152
  420.0 46.0 %collective-permute-start.49 = (bf16[128,2048]{1,0:T(8,128)(2,1)}, bf16[128,2048]{1,0:T(8,128)(2,1)}, u32[]{:S(2)}, u32[]{:S(2)}) collective-permute-start(bf16[128,2048]{1,0:T(8,128)(2,1)} %get-tuple-element.476), channel_id=1, source_target_pairs={{0,3},{1,2},{2,1},{3,0},{4,7},{5,6},{6,5},{7,4},{8,11},{9,10},{10,... | collective-permute-start | bytes 1572872 | tf_op jit(solution)/shard_map/ppermute | solution.py:152
  432.7 33.3 %collective-permute-start.45 = (bf16[256,1024]{1,0:T(8,128)(2,1)}, bf16[256,1024]{1,0:T(8,128)(2,1)}, u32[]{:S(2)}, u32[]{:S(2)}) collective-permute-start(bf16[256,1024]{1,0:T(8,128)(2,1)} %get-tuple-element.397), channel_id=1, source_target_pairs={{0,8},{4,12},{1,9},{5,13},{2,10},{6,14},{3,11},{7,15}} | collective-permute-start | bytes 1572872 | tf_op jit(solution)/shard_map/ppermute | solution.py:145
  475.9 23.6 %collective-permute-start.59 = (bf16[256,1024]{1,0:T(8,128)(2,1)}, bf16[256,1024]{1,0:T(8,128)(2,1)}, u32[]{:S(2)}, u32[]{:S(2)}) collective-permute-start(bf16[256,1024]{1,0:T(8,128)(2,1)} %get-tuple-element.504), channel_id=1, source_target_pairs={{0,8},{4,12},{8,16},{12,20},{1,9},{5,13},{9,17},{13,21},{2,10},{6,... | collective-permute-start | bytes 1572872 | tf_op jit(solution)/shard_map/ppermute | solution.py:145
  (104 other events, 1390.6 us)
Sparse Core Ops, SparseCore 0:
  10.2 84.7 all-gather.2
  97.2 76.2 all-gather.4
